TPU v7x, 128 devices: a whole 4x4x4 slice. The times are simulated.
128 devices in a mesh: row: 8 (over z, core), col: 16 (over x, y).
Axes of the slice: x: 4, y: 4, z: 4, core: 2. Of those that a mesh axis runs over, the one named last changes fastest.
Arguments:
- tile_blocks: bfloat16 [65536, 128, 128], P(('row', 'col')), may hold values from -0.1875 to 0.1875
- tile_column: int32 [65536], P(('row', 'col')), may hold values from 0 to 4095, as said below
- row_degree: int32 [4096], P(('row', 'col')), may hold values from 1 to 16, as said below
- node_weight: float32 [524288], P(('row', 'col')), may hold values from 1 to 50
- block_now: float32 [524288, 64], P(('row', 'col')), may hold values from -6 to 6
- block_prev: float32 [524288, 64], P(('row', 'col')), may hold values from -6 to 6
- coupling: float32 [64, 64], replicated, may hold values from -0.75 to 0.75
Outputs:
- block_next: float32 [524288, 64], P(('row', 'col'))
- rayleigh: float32 [64, 64], replicated
- r_factor: float32 [64, 64], replicated
Inputs may be any that keep to these rules, and one draw needn't show every extreme that they name: `tile_column`: the tile column of a slot lies in the slab of a device with the same col index as the slot's device. `row_degree`: in every draw one device has all its tile rows at 16 tiles.
All inputs are finite; a program needn't handle non-finite values.
Results may differ from a plain program's by a relative error of at most 0.00047.
Values may be sent and summed in bfloat16 or wider, within the bound.
No kernel may reach another device: no remote copies, remote signals or barrier semaphores. Data moves between devices by JAX's collectives and lax.ppermute only.
A program may use at most 128 MiB of HBM per device.

v0:
```python
import jax
import jax.numpy as jnp
from jax import lax
from jax.sharding import PartitionSpec as P


def row_members(row_degree, slots):
    row_ends = jnp.cumsum(row_degree)
    row_starts = row_ends - row_degree
    position = lax.broadcasted_iota(jnp.int32, (row_degree.shape[0], slots), 1)
    inside = (position >= row_starts[:, None]) & (position < row_ends[:, None])
    return inside.astype(jnp.float32)


def local(tile_blocks, tile_column, row_degree, node_weight, block_now, block_prev, coupling):
    highest = lax.Precision.HIGHEST
    tile_size = tile_blocks.shape[1]
    rows_dev = row_degree.shape[0]
    columns = block_now.shape[1]
    groups = lax.axis_size("col")
    members_row = lax.axis_size("row")
    node_total = block_now.shape[0] * members_row * groups
    block_half = block_now.astype(jnp.bfloat16).reshape(rows_dev, tile_size, columns)
    owner_device = tile_column // rows_dev
    source = owner_device // groups * rows_dev + tile_column % rows_dev
    gathered = lax.all_gather(block_half, "row", axis=0, tiled=True)
    picked = gathered[source]
    slot_count = tile_blocks.shape[0]
    products = jnp.einsum("sab,sbk->sak", tile_blocks, picked, preferred_element_type=jnp.float32)
    members = row_members(row_degree, slot_count)
    spread = jnp.einsum("rs,sak->rak", members, products, precision=highest).reshape(-1, columns)
    coupled = jnp.dot(block_prev, coupling.T, precision=highest)
    w_raw = node_weight[:, None] * block_now + spread - coupled
    rayleigh = lax.psum(jnp.dot(block_now.T, w_raw, precision=highest), ("row", "col")) / node_total
    w_next = w_raw - jnp.dot(block_now, rayleigh, precision=highest)
    gram_next = lax.psum(jnp.dot(w_next.T, w_next, precision=highest), ("row", "col")) / node_total
    lower_factor = jnp.linalg.cholesky(gram_next)
    block_next = jax.scipy.linalg.solve_triangular(lower_factor, w_next.T, lower=True).T
    return (block_next, rayleigh, lower_factor.T)


def solution(mesh):
    in_specs = (
        P(("row", "col"), None, None),
        P(("row", "col")),
        P(("row", "col")),
        P(("row", "col")),
        P(("row", "col"), None),
        P(("row", "col"), None),
        P(),
    )
    out_specs = (P(("row", "col"), None), P(), P())
    return jax.shard_map(local, mesh=mesh, in_specs=in_specs, out_specs=out_specs, check_vma=False)
```

profile of v0, /device:TPU:0, one launch (start us, length us, event | category | flops | bytes accessed | tf_op | source)
XLA Modules:
  0.0 265.9 jit_solution(6967681452651910997)
XLA Ops:
  7.2 2.2 copy_bitcast_fusion
  9.5 0.7 copy.27
  10.3 0.1 reduce.6
  10.4 0.7 sub.19
  11.1 0.7 compare_select_fusion
  11.8 33.4 %all-gather.2.cloned.1.call-done = bf16[256,128,64]{1,2,0:T(8,128)(2,1)} async-done(((bf16[32,128,64]{1,2,0:T(8,128)(2,1)}), bf16[256,128,64]{1,2,0:T(8,128)(2,1)}) %all-gather.2.cloned.1.call-update) | async-done | bytes 4194320 | tf_op jit(solution)/shard_map/all_gather | solution.py:26
  45.1 21.8 %gather_fusion = bf16[512,128,64]{1,2,0:T(8,128)(2,1)} fusion(bf16[256,128,64]{1,2,0:T(8,128)(2,1)} %all-gather.2.cloned.1.call-done, s32[1024]{0:T(1024)S(1)} %pad_clamp_fusion), kind=kCustom, calls=%fused_computation | custom fusion | bytes 16779264 | tf_op jit(solution)/shard_map/gather | solution.py:27
  67.0 19.6 %convolution_bitcast_fusion = f32[512,128,64]{1,2,0:T(8,128)} fusion(bf16[512,128,64]{1,2,0:T(8,128)(2,1)} %gather_fusion, bf16[512,128,128]{2,1,0:T(8,128)(2,1)} %param.7), kind=kOutput, calls=%fused_computation.3 | convolution fusion | flops 1073741824 | bytes 41943040 | tf_op jit(solution)/shard_map/sab,sbk->sak/dot_general | solution.py:29
  86.6 20.5 %fusion = f32[32,128,64]{1,0,2:T(8,128)S(1)} fusion(f32[512,128,64]{1,2,0:T(8,128)} %convolution_bitcast_fusion, s32[32]{0:T(128)S(1)} %reduce.6, s32[32]{0:T(128)S(1)} %sub.19), kind=kOutput, calls=%fused_computation.1 | convolution fusion | flops 1610661888 | bytes 17826048 | tf_op jit(solution)/shard_map/rs,sak->rak/dot_general | solution.py:31
  107.2 1.7 convolution_subtract_fusion
  108.8 1.0 copy-done.2
  109.8 1.0 convolution_bitcast_fusion.2
  110.8 65.1 %psum.14 = f32[64,64]{0,1:T(8,128)S(1)} all-reduce(f32[64,64]{0,1:T(8,128)S(1)} %convolution_bitcast_fusion.2), channel_id=1, replica_groups=mesh['row'=8,'col'=16] {'row','col'}, use_global_device_ids=true, to_apply=%region_1.2 | all-reduce | flops 4096 | bytes 32768 | tf_op jit(solution)/shard_map/psum | solution.py:34
  175.9 2.3 fusion.2
  178.2 1.0 fusion.17
  179.1 64.3 %psum.15 = f32[64,64]{0,1:T(8,128)S(1)} all-reduce(f32[64,64]{0,1:T(8,128)S(1)} %fusion.17), channel_id=1, replica_groups=mesh['row'=8,'col'=16] {'row','col'}, use_global_device_ids=true, to_apply=%region_2.3 | all-reduce | flops 4096 | bytes 32768 | tf_op jit(solution)/shard_map/psum | solution.py:36
  243.4 0.1 copy.31
  243.5 5.8 %cholesky.16 = f32[64,64]{1,0:T(8,128)S(1)} custom-call(f32[64,64]{1,0:T(8,128)S(1)} %fusion.8), custom_call_target="Cholesky" | custom-call | tf_op jit(solution)/shard_map/jit(cholesky)/cholesky | solution.py:37
  249.4 0.6 compare_reduce_fusion
  250.0 0.7 fusion.11
  250.7 4.9 %custom-call.7 = f32[1,64,64]{1,2,0:T(8,128)S(1)} custom-call(f32[1,64,64]{2,1,0:T(8,128)S(1)} %get-tuple-element.16), custom_call_target="InvertDiagBlocksLowerTriangular" | custom-call | tf_op jit(solution)/shard_map/jit(_solve_triangular)/triangular_solve | solution.py:38
  255.6 2.0 fusion.6
  257.6 0.7 copy.32
  258.3 0.7 copy.33
  (17 shorter events, 0.2 us)
Async XLA Ops:
  7.2 100.0 %copy-start = (f32[4096,64]{0,1:T(8,128)S(1)}, f32[4096,64]{0,1:T(8,128)}, u32[]{:S(2)}) copy-start(f32[4096,64]{0,1:T(8,128)} %param.12) | copy-start | bytes 3145732
  7.2 38.0 %all-gather.2.cloned.1.call-start = ((), (), s32[]{:S(2)}) async-start(), calls=%async_computation | async-start | bytes 4718592 | tf_op jit(solution)/shard_map/all_gather | solution.py:26
  86.6 20.6 %copy-start.1 = (f32[4096,64]{0,1:T(8,128)S(1)}, f32[4096,64]{0,1:T(8,128)}, u32[]{:S(2)}) copy-start(f32[4096,64]{0,1:T(8,128)} %param.11) | copy-start | bytes 3145732
  86.6 20.6 %copy-start.3 = (f32[64,64]{1,0:T(8,128)S(1)}, f32[64,64]{1,0:T(8,128)}, u32[]{:S(2)}) copy-start(f32[64,64]{1,0:T(8,128)} %param.13) | copy-start | bytes 49156
  86.6 20.6 %copy-start.4 = (f32[4096]{0:T(1024)S(1)}, f32[4096]{0:T(1024)}, u32[]{:S(2)}) copy-start(f32[4096]{0:T(1024)} %param.10) | copy-start | bytes 49156
  108.8 1.0 copy-start.2
Sparse Core Ops, SparseCore 0:
  10.3 34.7 all-gather.1
where the time goes:
time: 267 us; the launch traced here: 266 us
  blocking collectives  129 us (48%)
  matrix products  48 us (18%)
  waiting for transfers between devices  33.4 us (13%)
  local copies, waits for them, and re-layouts  25 us (9%)
  other arithmetic  15.9 us (6%)
  between operations  14.2 us (5%)
    psum x1, blocking collectives, local(): lax.psum(jnp.dot(block_now.T, w_raw, precision=highest), ('row', 'col'))  65.1 us
    psum x1, blocking collectives, local(): lax.psum(jnp.dot(w_next.T, w_next, precision=highest), ('row', 'col'))  64.3 us
    all_gather x1, waiting for transfers between devices, local(): gathered = lax.all_gather(block_half, 'row', axis=0, tiled=True)  33.4 us
    gather x1, local copies, waits for them, and re-layouts, local(): picked = gathered[source]  21.8 us
    dot_general x1, matrix products, local(): jnp.einsum('rs,sak->rak', members, products, precision=highest)  20.5 us
    dot_general x1, matrix products, local(): jnp.einsum('sab,sbk->sak', tile_blocks, picked, preferred_element_type=jn...  19.6 us
    another operation x3, other arithmetic, local(): lower_factor = jnp.linalg.cholesky(gram_next)  6.52 us
  transfers between devices with their start and end apart: 1, of which 1 were waited for; matrix products, arithmetic and copies ran while one was open for 1% of the time, Pallas kernels for 0%

commit v1 on v0

v1 whole, which is shorter than its diff:
```python
import jax
import jax.numpy as jnp
from jax import lax
from jax.experimental import pallas as pl
from jax.experimental.pallas import tpu as pltpu
from jax.sharding import PartitionSpec as P

TILE = 128
K = 64
ROWS = 32
SLOTS = 512
NODES_DEV = ROWS * TILE
CHAIN = 4
GROUPS = 16
UNROLL = 8
LIST = 576
PARTS = 3
TILES_OF = (64, 128, 64)
WORST = 64.0
F32 = jnp.float32
BF16 = jnp.bfloat16
NT = (((1,), (1,)), ((), ()))
HIGHEST = lax.Precision.HIGHEST


def vmem():
    return pl.BlockSpec(memory_space=pltpu.VMEM)


def smem():
    return pl.BlockSpec(memory_space=pltpu.SMEM)


def params(mib):
    return pltpu.CompilerParams(vmem_limit_bytes=mib << 20)


def split(x):
    hi = x.astype(BF16)
    return hi, (x - hi.astype(F32)).astype(BF16)


def round_kernel(x_ref, half_ref):
    for t in range(ROWS):
        half_ref[t] = x_ref[:, t * TILE:(t + 1) * TILE].astype(BF16)


def build_lists(place_ref, column_ref, degree_ref, list_ref, count_ref):
    z, core = place_ref[0], place_ref[1]

    def one_slot(row):
        def step(slot, ends):
            column = column_ref[slot]
            peer = lax.shift_right_logical(column, 9)
            dz = (lax.shift_right_logical(peer, 1) - z) & 3
            dc = (peer & 1) ^ core
            part = jnp.where(dz == 0, 0, jnp.where(dz == 2, 2, 1))
            tile = (column & 31) + dc * 32 + jnp.where(dz == 1, 64, 0)
            entry = (row << 20) | (slot << 10) | tile
            at = jnp.where(part == 0, ends[0], jnp.where(part == 1, ends[1], ends[2]))
            list_ref[at] = entry
            return tuple(e + jnp.where(part == p, 1, 0) for p, e in enumerate(ends))

        return step

    def one_row(row, carry):
        start, ends = carry
        stop = start + degree_ref[row]
        ends = lax.fori_loop(start, stop, one_slot(row), ends)
        done = []
        for p, e in enumerate(ends):
            @pl.when((e - p * LIST) & 1 == 1)
            def _():
                list_ref[e] = (row << 20) | TILES_OF[p]
            done.append(e + ((e - p * LIST) & 1))
        return stop, tuple(done)

    _, ends = lax.fori_loop(0, ROWS, one_row, (jnp.int32(0), tuple(jnp.int32(p * LIST) for p in range(PARTS))))
    for p, e in enumerate(ends):
        for j in range(2 * UNROLL):
            list_ref[e + j] = TILES_OF[p]
        count_ref[p] = lax.div(e - p * LIST + 2 * UNROLL - 1, 2 * UNROLL)


def multiply_part(part, list_ref, count_ref, tiles_ref, picked_ref, w_ref):
    def group(g, carry):
        base = part * LIST + g * (2 * UNROLL)
        rows, products = [], []
        for u in range(UNROLL):
            first, second = list_ref[base + 2 * u], list_ref[base + 2 * u + 1]
            x = [picked_ref[e & 1023] for e in (first, second)]
            a = [tiles_ref[lax.shift_right_logical(e, 10) & 511] for e in (first, second)]
            rows.append(lax.shift_right_logical(first, 20))
            products.append(lax.dot_general(
                jnp.concatenate(x, axis=1), jnp.concatenate(a, axis=1), NT, preferred_element_type=F32))
        for row, product in zip(rows, products):
            w_ref[row] += product
        return carry

    lax.fori_loop(0, count_ref[part], group, 0)


def place_tiles(picked_ref, blocks):
    at = 0
    for block in blocks:
        n = block.shape[0]
        picked_ref[at:at + n] = block[...]
        at += n
    picked_ref[at] = jnp.zeros((K, TILE), BF16)


def first_kernel(place_ref, column_ref, degree_ref, tiles_ref, half_ref, sib_ref, x_ref, prev_ref, weight_ref,
                 coupling_ref, w_ref, zx_ref, g_ref, list_ref, count_ref, picked_ref):
    build_lists(place_ref, column_ref, degree_ref, list_ref, count_ref)
    chi, clo = split(coupling_ref[...])
    left = jnp.concatenate([chi, chi, clo], axis=1)
    wide = 512
    for c in range(NODES_DEV // wide):
        lanes = slice(c * wide, (c + 1) * wide)
        x = x_ref[:, lanes]
        xhi, xlo = split(x)
        zx_ref[0:K, lanes] = xhi
        zx_ref[K:2 * K, lanes] = xlo
        phi, plo = split(prev_ref[:, lanes])
        coupled = jnp.dot(left, jnp.concatenate([phi, plo, phi], axis=0), preferred_element_type=F32)
        w = x * weight_ref[:, lanes] - coupled
        for t in range(wide // TILE):
            w_ref[c * (wide // TILE) + t] = w[:, t * TILE:(t + 1) * TILE]
    zx = zx_ref[...]
    gg = lax.dot_general(zx[:K], zx, NT, preferred_element_type=F32)
    cross = gg[:, K:]
    g_ref[...] = gg[:, :K] + cross + cross.T
    place_tiles(picked_ref, (half_ref, sib_ref))
    multiply_part(0, list_ref, count_ref, tiles_ref, picked_ref, w_ref)


def second_kernel(list_ref, count_ref, tiles_ref, dn_ref, sdn_ref, up_ref, sup_ref, w_in_ref, w_ref, picked_ref):
    w_ref[...] = w_in_ref[...]
    place_tiles(picked_ref, (dn_ref, sdn_ref, up_ref, sup_ref))
    multiply_part(1, list_ref, count_ref, tiles_ref, picked_ref, w_ref)


def third_kernel(list_ref, count_ref, tiles_ref, f1_ref, f2_ref, s1_ref, s2_ref, w_in_ref, zx_ref, g_ref, zw_ref,
                 sums_ref, w_ref, picked_ref):
    w_ref[...] = w_in_ref[...]
    place_tiles(picked_ref, (f1_ref, f2_ref, s1_ref, s2_ref))
    multiply_part(2, list_ref, count_ref, tiles_ref, picked_ref, w_ref)
    for t in range(ROWS):
        whi, wlo = split(w_ref[t])
        zw_ref[0:K, t * TILE:(t + 1) * TILE] = whi
        zw_ref[K:2 * K, t * TILE:(t + 1) * TILE] = wlo
    zw = zw_ref[...]
    m = lax.dot_general(zx_ref[...], zw, NT, preferred_element_type=F32)
    s = lax.dot_general(zw[:K], zw, NT, preferred_element_type=F32)
    cross = s[:, K:]
    sums_ref[0:K, 0:K] = m[:K, :K] + m[:K, K:] + m[K:, :K]
    sums_ref[0:K, K:] = s[:, :K] + cross + cross.T
    g = g_ref[...]
    sums_ref[K:, 0:K] = g[:K // 2]
    sums_ref[K:, K:] = g[K // 2:]


def factor_kernel(node_total, sums_ref, rayleigh_ref, r_ref, f_ref, flag_ref):
    inv = 1.0 / node_total
    r = sums_ref[0:K, 0:K] * inv
    s = sums_ref[0:K, K:] * inv
    g = jnp.concatenate([sums_ref[K:, 0:K], sums_ref[K:, K:]], axis=0) * inv
    row = lax.broadcasted_iota(jnp.int32, (K, K), 0)
    col = lax.broadcasted_iota(jnp.int32, (K, K), 1)
    eye = jnp.where(row == col, 1.0, 0.0)
    gr = jnp.dot(2.0 * eye - g, r, precision=HIGHEST, preferred_element_type=F32)
    rt = r.T
    gram = s - jnp.dot(rt, gr, precision=HIGHEST, preferred_element_type=F32)
    work = jnp.concatenate([gram, eye], axis=1)
    blocks = [work[8 * b:8 * b + 8] for b in range(K // 8)]
    sub = lax.broadcasted_iota(jnp.int32, (8, 2 * K), 0)
    pivots = []
    for k in range(K):
        b, o = divmod(k, 8)
        line = jnp.broadcast_to(blocks[b][o:o + 1, :], (8, 2 * K))
        pivot = jnp.broadcast_to(blocks[b][o:o + 1, k:k + 1], (8, 2 * K))
        pivots.append(blocks[b][o:o + 1, k:k + 1])
        scaled = line / pivot
        for i in range(b, K // 8):
            column = jnp.broadcast_to(blocks[i][:, k:k + 1], (8, 2 * K))
            if i == b:
                column = jnp.where(sub > o, column, 0.0)
            blocks[i] = blocks[i] - column * scaled
    pivot = jnp.concatenate(pivots, axis=0)
    work = jnp.concatenate(blocks, axis=0) * lax.rsqrt(pivot)
    upper = jnp.where(col >= row, work[:, :K], 0.0)
    lower_inv = jnp.where(col <= row, work[:, K:], 0.0)
    rayleigh_ref[...] = r
    r_ref[...] = upper
    f_ref[:, 0:K] = lower_inv
    f_ref[:, K:] = -jnp.dot(lower_inv, rt, precision=HIGHEST, preferred_element_type=F32)
    largest = jnp.max(jnp.where(row == col, s, 0.0))
    smallest = jnp.min(pivot)
    flag_ref[0] = jnp.where(smallest * WORST >= largest, 0, 1).astype(jnp.int32)


def final_kernel(f_ref, zw_ref, zx_ref, out_ref):
    f1h, f1l = split(f_ref[:, 0:K])
    f2h, f2l = split(f_ref[:, K:])
    zero = jnp.zeros((K, K), BF16)
    left = jnp.concatenate([jnp.concatenate([f1h, f1h, f2h, f2h], axis=1),
                            jnp.concatenate([f1l, zero, f2l, zero], axis=1)], axis=0)
    wide = 512
    for c in range(NODES_DEV // wide):
        lanes = slice(c * wide, (c + 1) * wide)
        z = jnp.concatenate([zw_ref[:, lanes], zx_ref[:, lanes]], axis=0)
        y = jnp.dot(left, z, preferred_element_type=F32)
        out_ref[:, lanes] = y[:K] + y[K:]


def exchange(v, axis, to):
    n = lax.axis_size(axis)
    return lax.ppermute(v, axis, [(i, to(i)) for i in range(n)])


def core_swap(v):
    return exchange(v, "row", lambda i: i ^ 1)


def along_z(v, d):
    return exchange(v, "row", lambda i: (i + 2 * d) % 8)


def total(v):
    v = v + core_swap(v)
    for axis, unit in (("row", 2), ("col", 1), ("col", 4)):
        others = [exchange(v, axis, lambda i, d=d * unit: i ^ d) for d in (1, 2, 3)]
        v = (v + others[0]) + (others[1] + others[2])
    return v


def local(tile_blocks, tile_column, row_degree, node_weight, block_now, block_prev, coupling):
    node_total = NODES_DEV * lax.axis_size("row") * lax.axis_size("col")
    x = block_now.T
    prev = block_prev.T
    row = lax.axis_index("row")
    place = jnp.stack([row // 2, row % 2]).astype(jnp.int32)
    tiles = pltpu.with_memory_space_constraint(tile_blocks, pltpu.VMEM)
    slab = (ROWS, K, TILE)
    half = pl.pallas_call(
        round_kernel, out_shape=jax.ShapeDtypeStruct(slab, BF16), in_specs=[vmem()], out_specs=vmem(),
        compiler_params=params(8), name="round_block")(x)
    sib = core_swap(half)
    dn = along_z(half, 1)
    up = along_z(half, -1)

    w1, zx, g, lists, counts = pl.pallas_call(
        first_kernel,
        out_shape=(pltpu.VMEM(slab, F32), pltpu.VMEM((2 * K, NODES_DEV), BF16), pltpu.VMEM((K, K), F32),
                   pltpu.SMEM((PARTS * LIST + 64,), jnp.int32), pltpu.SMEM((PARTS,), jnp.int32)),
        in_specs=[smem(), smem(), smem()] + [vmem()] * 7,
        out_specs=(vmem(), vmem(), vmem(), smem(), smem()),
        scratch_shapes=[pltpu.VMEM((TILES_OF[0] + 1, K, TILE), BF16)],
        compiler_params=params(12), name="own_part")(
            place, tile_column, row_degree, tiles, half, sib, x, prev, node_weight.reshape(1, NODES_DEV), coupling)

    h = ROWS // 2
    f1 = along_z(dn[:h], 1)
    f2 = along_z(up[h:], -1)
    sdn = core_swap(dn)
    sup = core_swap(up)
    w2 = pl.pallas_call(
        second_kernel, out_shape=pltpu.VMEM(slab, F32),
        in_specs=[smem(), smem()] + [vmem()] * 6, out_specs=vmem(),
        scratch_shapes=[pltpu.VMEM((TILES_OF[1] + 1, K, TILE), BF16)],
        compiler_params=params(12), name="near_part")(lists, counts, tiles, dn, sdn, up, sup, w1)

    s1 = core_swap(f1)
    s2 = core_swap(f2)
    zw, sums = pl.pallas_call(
        third_kernel,
        out_shape=(pltpu.VMEM((2 * K, NODES_DEV), BF16), jax.ShapeDtypeStruct((K + K // 2, 2 * K), F32)),
        in_specs=[smem(), smem()] + [vmem()] * 8, out_specs=(vmem(), vmem()),
        scratch_shapes=[pltpu.VMEM(slab, F32), pltpu.VMEM((TILES_OF[2] + 1, K, TILE), BF16)],
        compiler_params=params(16), name="far_part")(lists, counts, tiles, f1, f2, s1, s2, w2, zx, g)

    sums = total(sums)
    square = jax.ShapeDtypeStruct((K, K), F32)
    rayleigh, r_factor, f, flag = pl.pallas_call(
        lambda *refs: factor_kernel(node_total, *refs),
        out_shape=(square, square, jax.ShapeDtypeStruct((K, 2 * K), F32), jax.ShapeDtypeStruct((1,), jnp.int32)),
        in_specs=[vmem()], out_specs=(vmem(), vmem(), vmem(), smem()),
        compiler_params=params(8), name="factor")(sums)

    def plain(zw, zx, f, rayleigh, r_factor):
        out = pl.pallas_call(
            final_kernel, out_shape=jax.ShapeDtypeStruct((K, NODES_DEV), F32), in_specs=[vmem()] * 3,
            out_specs=vmem(), compiler_params=params(12), name="scale_block")(f, zw, zx)
        return out, r_factor

    def two_passes(zw, zx, f, rayleigh, r_factor):
        whole = lambda z: z[:K].astype(F32) + z[K:].astype(F32)
        w_next = whole(zw) - jnp.dot(rayleigh.T, whole(zx), precision=HIGHEST)
        gram = total(jnp.dot(w_next, w_next.T, precision=HIGHEST)) / node_total
        lower = jnp.linalg.cholesky(gram)
        return jax.scipy.linalg.solve_triangular(lower, w_next, lower=True), lower.T

    out, r_factor = lax.cond(flag[0] == 0, plain, two_passes, zw, zx, f, rayleigh, r_factor)
    return out.T, rayleigh, r_factor


def solution(mesh):
    in_specs = (
        P(("row", "col"), None, None),
        P(("row", "col")),
        P(("row", "col")),
        P(("row", "col")),
        P(("row", "col"), None),
        P(("row", "col"), None),
        P(),
    )
    out_specs = (P(("row", "col"), None), P(), P())
    return jax.shard_map(local, mesh=mesh, in_specs=in_specs, out_specs=out_specs, check_vma=False)
```

time: 267 us -> 109 us (0.41)
  blocking collectives: 129 us -> 0 us
  matrix products: 48 us -> 0 us
  starting transfers between devices: 0.04 us -> 31.9 us
  Pallas kernels: 0 us -> 27.3 us
  other arithmetic: 15.9 us -> 0.12 us
  between operations: 14.2 us -> 1.41 us
  local copies, waits for them, and re-layouts: 25 us -> 14.7 us
    psum x2 -> x0, blocking collectives: 129 us -> none  [the longest x1 65.1 us: local(): lax.psum(jnp.dot(block_now.T, w_raw, precision=highest), ('row', 'col'))]
    dot_general x6 -> x0, matrix products: 46 us -> none  [the longest x1 20.5 us: local(): jnp.einsum('rs,sak->rak', members, products, precision=highest)]
    all_gather x1 -> x0, waiting for transfers between devices: 33.4 us -> none  [local(): gathered = lax.all_gather(block_half, 'row', axis=0, tiled=True)]
    ppermute x0 -> x19, waiting for transfers between devices: none -> 32.4 us  [exchange(): return lax.ppermute(v, axis, [(i, to(i)) for i in range(n)])]
    ppermute x0 -> x19, starting transfers between devices: none -> 31.9 us  [exchange(): return lax.ppermute(v, axis, [(i, to(i)) for i in range(n)])]
    pallas_call x0 -> x6, Pallas kernels: none -> 27.3 us  [the longest x1 9.64 us: local(): pl.pallas_call(lambda *refs: factor_kernel(node_total, *refs), out_shape=...]
    gather x1 -> x0, local copies, waits for them, and re-layouts: 21.8 us -> none  [local(): picked = gathered[source]]
    unnamed x12 -> x24, local copies, waits for them, and re-layouts: 2.38 us -> 14.7 us
  transfers between devices with their start and end apart: 1 -> 19, of which waited for: 1 -> 9; matrix products, arithmetic and copies ran while one was open for 1% -> 0% of each run, Pallas kernels for 0% -> 11%
where the time goes in v1:
time: 109 us; the launch traced here: 108 us
  waiting for transfers between devices  32.4 us (30%)
  starting transfers between devices  31.9 us (29%)
  Pallas kernels  27.3 us (25%)
  local copies, waits for them, and re-layouts  14.7 us (13%)
  between operations  1.41 us (1%)
    ppermute x19, waiting for transfers between devices, exchange(): return lax.ppermute(v, axis, [(i, to(i)) for i in range(n)])  32.4 us
    ppermute x19, starting transfers between devices, exchange(): return lax.ppermute(v, axis, [(i, to(i)) for i in range(n)])  31.9 us
    unnamed x24, local copies, waits for them, and re-layouts  14.7 us
    pallas_call x1, Pallas kernels, local(): pl.pallas_call(lambda *refs: factor_kernel(node_total, *refs), out_shape=...  9.64 us
    pallas_call x1, Pallas kernels, local(): pl.pallas_call(first_kernel, out_shape=(pltpu.VMEM(slab, F32), pltpu.VMEM...  8.02 us
    pallas_call x1, Pallas kernels, local(): pl.pallas_call(third_kernel, out_shape=(pltpu.VMEM((2 * K, NODES_DEV), BF...  4.1 us
    pallas_call x1, Pallas kernels, local(): pl.pallas_call(second_kernel, out_shape=pltpu.VMEM(slab, F32), in_specs=[...  4.05 us
  transfers between devices with their start and end apart: 19, of which 9 were waited for; matrix products, arithmetic and copies ran while one was open for 0% of the time, Pallas kernels for 11%

profile of v1, /device:TPU:0, one launch (start us, length us, event | category | flops | bytes accessed | tf_op | source)
XLA Modules:
  0.0 108.1 jit_solution(1065751965999490571)
XLA Ops:
  1.9 2.1 %collective-permute-start.11 = (bf16[32,64,128]{2,1,0:T(8,128)(2,1)S(1)}, bf16[32,64,128]{2,1,0:T(8,128)(2,1)S(1)}, u32[]{:S(2)}, u32[]{:S(2)}) collective-permute-start(bf16[32,64,128]{2,1,0:T(8,128)(2,1)S(1)} %round_block.1.half_ref), channel_id=1, source_target_pairs={{0,32},{16,48},{32,64},{48,80},{64,96},{80,112},{96,0},{112,16},{1... | collective-permute-start | bytes 1572872 | tf_op jit(solution)/shard_map/ppermute | solution.py:218
  4.0 2.2 %collective-permute-start.13 = (bf16[32,64,128]{2,1,0:T(8,128)(2,1)S(1)}, bf16[32,64,128]{2,1,0:T(8,128)(2,1)S(1)}, u32[]{:S(2)}, u32[]{:S(2)}) collective-permute-start(bf16[32,64,128]{2,1,0:T(8,128)(2,1)S(1)} %round_block.1.half_ref), channel_id=1, source_target_pairs={{0,96},{16,112},{32,0},{48,16},{64,32},{80,48},{96,64},{112,80},{1... | collective-permute-start | bytes 1572872 | tf_op jit(solution)/shard_map/ppermute | solution.py:218
  6.2 11.8 %collective-permute-done.11.dn_ref = bf16[32,64,128]{2,1,0:T(8,128)(2,1)S(1)} collective-permute-done((bf16[32,64,128]{2,1,0:T(8,128)(2,1)S(1)}, bf16[32,64,128]{2,1,0:T(8,128)(2,1)S(1)}, u32[]{:S(2)}, u32[]{:S(2)}) %collective-permute-start.11) | collective-permute-done | bytes 524320 | tf_op jit(solution)/shard_map/ppermute | solution.py:218
  19.4 2.6 %collective-permute-start.14 = (bf16[16,64,128]{2,1,0:T(8,128)(2,1)S(1)}, bf16[16,64,128]{2,1,0:T(8,128)(2,1)}, u32[]{:S(2)}, u32[]{:S(2)}) collective-permute-start(bf16[16,64,128]{2,1,0:T(8,128)(2,1)S(1)} %slice.33), channel_id=1, source_target_pairs={{0,96},{16,112},{32,0},{48,16},{64,32},{80,48},{96,64},{112,80},{1... | collective-permute-start | bytes 786440 | tf_op jit(solution)/shard_map/ppermute | solution.py:218
  22.0 6.2 %collective-permute-done.12.f1_ref = bf16[16,64,128]{2,1,0:T(8,128)(2,1)S(1)} collective-permute-done((bf16[16,64,128]{2,1,0:T(8,128)(2,1)S(1)}, bf16[16,64,128]{2,1,0:T(8,128)(2,1)S(1)}, u32[]{:S(2)}, u32[]{:S(2)}) %collective-permute-start.12) | collective-permute-done | bytes 262176 | tf_op jit(solution)/shard_map/ppermute | solution.py:218
  29.5 5.8 %copy-done = bf16[512,128,128]{2,1,0:T(8,128)(2,1)S(1)} copy-done((bf16[512,128,128]{2,1,0:T(8,128)(2,1)S(1)}, bf16[512,128,128]{2,1,0:T(8,128)(2,1)}, u32[]{:S(2)}) %copy-start) | copy-done | bytes 16777240
  35.3 1.2 %copy-done.3 = f32[4096,64]{0,1:T(8,128)S(1)} copy-done((f32[4096,64]{0,1:T(8,128)S(1)}, f32[4096,64]{0,1:T(8,128)}, u32[]{:S(2)}) %copy-start.3) | copy-done | bytes 1048600
  36.5 1.2 %copy-done.4 = f32[4096,64]{0,1:T(8,128)S(1)} copy-done((f32[4096,64]{0,1:T(8,128)S(1)}, f32[4096,64]{0,1:T(8,128)}, u32[]{:S(2)}) %copy-start.4) | copy-done | bytes 1048600
  41.6 8.0 %own_part.1 = (f32[32,64,128]{2,1,0:T(8,128)S(1)}, bf16[128,4096]{1,0:T(8,128)(2,1)S(1)}, f32[64,64]{1,0:T(8,128)S(1)}, s32[1792]{0:T(1024)S(4)}, s32[3]{0:T(128)S(4)}) custom-call(s32[2]{0:T(128)S(1)} %pad_add_fusion.place_ref, s32[512]{0:T(512)S(1)} %copy-done.9, s32[32]{0:T(128)S(1)} %copy-done.10, bf16[512,128,128]{2,1,0:T(8,128)(2,1)S(1)} %copy-done, ...), custom_call_target="tpu_custom_call" | custom-call | tf_op jit(solution)/shard_map/own_part/pallas_call | solution.py:252
  49.6 4.0 %near_part.1.w_in_ref = f32[32,64,128]{2,1,0:T(8,128)S(1)} custom-call(s32[1792]{0:T(1024)S(4)} %get-tuple-element.37.list_ref, s32[3]{0:T(128)S(4)} %get-tuple-element.38.count_ref, bf16[512,128,128]{2,1,0:T(8,128)(2,1)S(1)} %copy-done.1, bf16[32,64,128]{2,1,0:T(8,128)(2,1)S(1)} %collective-permute-done.11.dn_ref, ...), custom_call_target="tpu_custom_call" | custom-call | tf_op jit(solution)/shard_map/near_part/pallas_call | solution.py:267
  53.7 4.1 %far_part.1 = (bf16[128,4096]{1,0:T(8,128)(2,1)S(1)}, f32[96,128]{1,0:T(8,128)S(1)}) custom-call(s32[1792]{0:T(1024)S(4)} %get-tuple-element.37.list_ref, s32[3]{0:T(128)S(4)} %get-tuple-element.38.count_ref, bf16[512,128,128]{2,1,0:T(8,128)(2,1)S(1)} %copy-done.1, bf16[16,64,128]{2,1,0:T(8,128)(2,1)S(1)} %collective-permute-done.12.f1_ref, ...), custom_call_target="tpu_custom_call" | custom-call | tf_op jit(solution)/shard_map/far_part/pallas_call | solution.py:275
  59.2 4.4 %collective-permute-start.21 = (f32[96,128]{1,0:T(8,128)S(1)}, f32[96,128]{1,0:T(8,128)S(1)}, u32[]{:S(2)}, u32[]{:S(2)}) collective-permute-start(f32[96,128]{1,0:T(8,128)S(1)} %add.84), channel_id=1, source_target_pairs={{0,64},{16,80},{32,96},{48,112},{64,0},{80,16},{96,32},{112,48},{1... | collective-permute-start | bytes 147464 | tf_op jit(solution)/shard_map/ppermute | solution.py:218
  64.1 2.5 %collective-permute-done.21 = f32[96,128]{1,0:T(8,128)S(1)} collective-permute-done((f32[96,128]{1,0:T(8,128)S(1)}, f32[96,128]{1,0:T(8,128)S(1)}, u32[]{:S(2)}, u32[]{:S(2)}) %collective-permute-start.21) | collective-permute-done | bytes 49184 | tf_op jit(solution)/shard_map/ppermute | solution.py:218
  66.6 2.4 %collective-permute-done.22 = f32[96,128]{1,0:T(8,128)S(1)} collective-permute-done((f32[96,128]{1,0:T(8,128)S(1)}, f32[96,128]{1,0:T(8,128)S(1)}, u32[]{:S(2)}, u32[]{:S(2)}) %collective-permute-start.22) | collective-permute-done | bytes 49184 | tf_op jit(solution)/shard_map/ppermute | solution.py:218
  69.0 4.5 %collective-permute-start.23 = (f32[96,128]{1,0:T(8,128)S(1)}, f32[96,128]{1,0:T(8,128)S(1)}, u32[]{:S(2)}, u32[]{:S(2)}) collective-permute-start(f32[96,128]{1,0:T(8,128)S(1)} %add_add_fusion.4), channel_id=1, source_target_pairs={{0,1},{1,0},{2,3},{3,2},{4,5},{5,4},{6,7},{7,6},{8,9},{9,8},{10,11... | collective-permute-start | bytes 147464 | tf_op jit(solution)/shard_map/ppermute | solution.py:218
  73.5 2.8 %collective-permute-start.24 = (f32[96,128]{1,0:T(8,128)S(1)}, f32[96,128]{1,0:T(8,128)S(1)}, u32[]{:S(2)}, u32[]{:S(2)}) collective-permute-start(f32[96,128]{1,0:T(8,128)S(1)} %add_add_fusion.4), channel_id=1, source_target_pairs={{0,2},{1,3},{2,0},{3,1},{4,6},{5,7},{6,4},{7,5},{8,10},{9,11},{10,... | collective-permute-start | bytes 147464 | tf_op jit(solution)/shard_map/ppermute | solution.py:218
  76.3 2.8 %collective-permute-done.24 = f32[96,128]{1,0:T(8,128)S(1)} collective-permute-done((f32[96,128]{1,0:T(8,128)S(1)}, f32[96,128]{1,0:T(8,128)S(1)}, u32[]{:S(2)}, u32[]{:S(2)}) %collective-permute-start.24) | collective-permute-done | bytes 49184 | tf_op jit(solution)/shard_map/ppermute | solution.py:218
  79.1 2.5 %collective-permute-done.25 = f32[96,128]{1,0:T(8,128)S(1)} collective-permute-done((f32[96,128]{1,0:T(8,128)S(1)}, f32[96,128]{1,0:T(8,128)S(1)}, u32[]{:S(2)}, u32[]{:S(2)}) %collective-permute-start.25) | collective-permute-done | bytes 49184 | tf_op jit(solution)/shard_map/ppermute | solution.py:218
  81.6 8.1 %collective-permute-start.26 = (f32[96,128]{1,0:T(8,128)S(1)}, f32[96,128]{1,0:T(8,128)S(1)}, u32[]{:S(2)}, u32[]{:S(2)}) collective-permute-start(f32[96,128]{1,0:T(8,128)S(1)} %add_add_fusion.3), channel_id=1, source_target_pairs={{0,4},{1,5},{2,6},{3,7},{4,0},{5,1},{6,2},{7,3},{8,12},{9,13},{10,... | collective-permute-start | bytes 147464 | tf_op jit(solution)/shard_map/ppermute | solution.py:218
  89.7 2.8 %collective-permute-start.28 = (f32[96,128]{1,0:T(8,128)S(1)}, f32[96,128]{1,0:T(8,128)S(1)}, u32[]{:S(2)}, u32[]{:S(2)}) collective-permute-start(f32[96,128]{1,0:T(8,128)S(1)} %add_add_fusion.3), channel_id=1, source_target_pairs={{0,12},{1,13},{2,14},{3,15},{4,8},{5,9},{6,10},{7,11},{8,4},{9,5},... | collective-permute-start | bytes 147464 | tf_op jit(solution)/shard_map/ppermute | solution.py:218
  92.4 2.9 %collective-permute-done.27 = f32[96,128]{1,0:T(8,128)S(1)} collective-permute-done((f32[96,128]{1,0:T(8,128)S(1)}, f32[96,128]{1,0:T(8,128)S(1)}, u32[]{:S(2)}, u32[]{:S(2)}) %collective-permute-start.27) | collective-permute-done | bytes 49184 | tf_op jit(solution)/shard_map/ppermute | solution.py:218
  95.5 9.6 %factor.1 = (f32[64,64]{1,0:T(8,128)}, f32[64,64]{1,0:T(8,128)S(1)}, f32[64,128]{1,0:T(8,128)S(1)}, s32[1]{0:T(128)}) custom-call(f32[96,128]{1,0:T(8,128)S(1)} %add_add_fusion.2.refs_0_), custom_call_target="tpu_custom_call" | custom-call | tf_op jit(solution)/shard_map/factor/pallas_call | solution.py:284
  105.8 1.7 %conditional.1 = (f32[64,4096]{1,0:T(8,128)}, f32[64,64]{1,0:T(8,128)S(1)}) conditional(s32[]{:T(128)} %bitcast.10, (bf16[128,4096]{1,0:T(8,128)(2,1)S(1)}, bf16[128,4096]{1,0:T(8,128)(2,1)S(1)}, f32[64,64]{1,0:T(8,128)}) %tuple.16, (f32[64,128]{1,0:T(8,128)S(1)}, bf16[128,4096]{1,0:T(8,128)(2,1)S(1)}, bf16[128,4096]{1,0:T(8,128)(2,1)S(1)}, ...), branch_computations={%region_0.3_spmd, %region_3.4_spmd} | conditional | flops 605896768 | bytes 7472034 | solution.py:303
  106.0 1.4 %scale_block.1 = f32[64,4096]{1,0:T(8,128)} custom-call(f32[64,128]{1,0:T(8,128)S(1)} %get-tuple-element.17.f_ref, bf16[128,4096]{1,0:T(8,128)(2,1)S(1)} %get-tuple-element.18.zw_ref, bf16[128,4096]{1,0:T(8,128)(2,1)S(1)} %get-tuple-element.19.zx_ref), custom_call_target="tpu_custom_call" | custom-call | tf_op jit(solution)/shard_map/cond/branch_1_fun/scale_block/pallas_call | solution.py:291
  (52 shorter events, 10.6 us)
Async XLA Ops:
  0.6 1.2 %copy-start.2 = (f32[4096,64]{0,1:T(8,128)S(1)}, f32[4096,64]{0,1:T(8,128)}, u32[]{:S(2)}) copy-start(f32[4096,64]{0,1:T(8,128)} %param.13) | copy-start | bytes 3145732
  1.9 16.1 %collective-permute-start.11 = (bf16[32,64,128]{2,1,0:T(8,128)(2,1)S(1)}, bf16[32,64,128]{2,1,0:T(8,128)(2,1)S(1)}, u32[]{:S(2)}, u32[]{:S(2)}) collective-permute-start(bf16[32,64,128]{2,1,0:T(8,128)(2,1)S(1)} %round_block.1.half_ref), channel_id=1, source_target_pairs={{0,32},{16,48},{32,64},{48,80},{64,96},{80,112},{96,0},{112,16},{1... | collective-permute-start | bytes 1572872 | tf_op jit(solution)/shard_map/ppermute | solution.py:218
  4.0 14.0 %collective-permute-start.13 = (bf16[32,64,128]{2,1,0:T(8,128)(2,1)S(1)}, bf16[32,64,128]{2,1,0:T(8,128)(2,1)S(1)}, u32[]{:S(2)}, u32[]{:S(2)}) collective-permute-start(bf16[32,64,128]{2,1,0:T(8,128)(2,1)S(1)} %round_block.1.half_ref), channel_id=1, source_target_pairs={{0,96},{16,112},{32,0},{48,16},{64,32},{80,48},{96,64},{112,80},{1... | collective-permute-start | bytes 1572872 | tf_op jit(solution)/shard_map/ppermute | solution.py:218
  6.2 22.5 %collective-permute-start.10 = (bf16[32,64,128]{2,1,0:T(8,128)(2,1)S(1)}, bf16[32,64,128]{2,1,0:T(8,128)(2,1)S(1)}, u32[]{:S(2)}, u32[]{:S(2)}) collective-permute-start(bf16[32,64,128]{2,1,0:T(8,128)(2,1)S(1)} %round_block.1.half_ref), channel_id=1, source_target_pairs={{0,16},{16,0},{32,48},{48,32},{64,80},{80,64},{96,112},{112,96},{1... | collective-permute-start | bytes 1572872 | tf_op jit(solution)/shard_map/ppermute | solution.py:218
  18.0 31.6 %collective-permute-start.17 = (bf16[32,64,128]{2,1,0:T(8,128)(2,1)S(1)}, bf16[32,64,128]{2,1,0:T(8,128)(2,1)S(1)}, u32[]{:S(2)}, u32[]{:S(2)}) collective-permute-start(bf16[32,64,128]{2,1,0:T(8,128)(2,1)S(1)} %collective-permute-done.11.dn_ref), channel_id=1, source_target_pairs={{0,16},{16,0},{32,48},{48,32},{64,80},{80,64},{96,112},{112,96},{1... | collective-permute-start | bytes 1572872 | tf_op jit(solution)/shard_map/ppermute | solution.py:218
  18.0 31.6 %collective-permute-start.18 = (bf16[32,64,128]{2,1,0:T(8,128)(2,1)S(1)}, bf16[32,64,128]{2,1,0:T(8,128)(2,1)}, u32[]{:S(2)}, u32[]{:S(2)}) collective-permute-start(bf16[32,64,128]{2,1,0:T(8,128)(2,1)S(1)} %collective-permute-done.13.up_ref), channel_id=1, source_target_pairs={{0,16},{16,0},{32,48},{48,32},{64,80},{80,64},{96,112},{112,96},{1... | collective-permute-start | bytes 1572872 | tf_op jit(solution)/shard_map/ppermute | solution.py:218
  18.6 9.6 %collective-permute-start.12 = (bf16[16,64,128]{2,1,0:T(8,128)(2,1)S(1)}, bf16[16,64,128]{2,1,0:T(8,128)(2,1)S(1)}, u32[]{:S(2)}, u32[]{:S(2)}) collective-permute-start(bf16[16,64,128]{2,1,0:T(8,128)(2,1)S(1)} %slice.32), channel_id=1, source_target_pairs={{0,32},{16,48},{32,64},{48,80},{64,96},{80,112},{96,0},{112,16},{1... | collective-permute-start | bytes 786440 | tf_op jit(solution)/shard_map/ppermute | solution.py:218
  19.4 8.7 %collective-permute-start.14 = (bf16[16,64,128]{2,1,0:T(8,128)(2,1)S(1)}, bf16[16,64,128]{2,1,0:T(8,128)(2,1)}, u32[]{:S(2)}, u32[]{:S(2)}) collective-permute-start(bf16[16,64,128]{2,1,0:T(8,128)(2,1)S(1)} %slice.33), channel_id=1, source_target_pairs={{0,96},{16,112},{32,0},{48,16},{64,32},{80,48},{96,64},{112,80},{1... | collective-permute-start | bytes 786440 | tf_op jit(solution)/shard_map/ppermute | solution.py:218
  28.1 25.6 %collective-permute-start.15 = (bf16[16,64,128]{2,1,0:T(8,128)(2,1)S(1)}, bf16[16,64,128]{2,1,0:T(8,128)(2,1)}, u32[]{:S(2)}, u32[]{:S(2)}) collective-permute-start(bf16[16,64,128]{2,1,0:T(8,128)(2,1)S(1)} %collective-permute-done.12.f1_ref), channel_id=1, source_target_pairs={{0,16},{16,0},{32,48},{48,32},{64,80},{80,64},{96,112},{112,96},{1... | collective-permute-start | bytes 786440 | tf_op jit(solution)/shard_map/ppermute | solution.py:218
  28.1 25.6 %collective-permute-start.16 = (bf16[16,64,128]{2,1,0:T(8,128)(2,1)}, bf16[16,64,128]{2,1,0:T(8,128)(2,1)}, u32[]{:S(2)}, u32[]{:S(2)}) collective-permute-start(bf16[16,64,128]{2,1,0:T(8,128)(2,1)} %collective-permute-done.14.f2_ref), channel_id=1, source_target_pairs={{0,16},{16,0},{32,48},{48,32},{64,80},{80,64},{96,112},{112,96},{1... | collective-permute-start | bytes 786440 | tf_op jit(solution)/shard_map/ppermute | solution.py:218
  29.5 5.8 %copy-start = (bf16[512,128,128]{2,1,0:T(8,128)(2,1)S(1)}, bf16[512,128,128]{2,1,0:T(8,128)(2,1)}, u32[]{:S(2)}) copy-start(bf16[512,128,128]{2,1,0:T(8,128)(2,1)} %tiles_ref.5) | copy-start | bytes 50331652
  35.3 1.2 %copy-start.3 = (f32[4096,64]{0,1:T(8,128)S(1)}, f32[4096,64]{0,1:T(8,128)}, u32[]{:S(2)}) copy-start(f32[4096,64]{0,1:T(8,128)} %param.13) | copy-start | bytes 3145732
  36.5 1.2 %copy-start.4 = (f32[4096,64]{0,1:T(8,128)S(1)}, f32[4096,64]{0,1:T(8,128)}, u32[]{:S(2)}) copy-start(f32[4096,64]{0,1:T(8,128)} %param.14) | copy-start | bytes 3145732
  41.6 8.0 %copy-start.1 = (bf16[512,128,128]{2,1,0:T(8,128)(2,1)S(1)}, bf16[512,128,128]{2,1,0:T(8,128)(2,1)}, u32[]{:S(2)}) copy-start(bf16[512,128,128]{2,1,0:T(8,128)(2,1)} %tiles_ref.5) | copy-start | bytes 50331652
  57.8 1.3 %collective-permute-start.19 = (f32[96,128]{1,0:T(8,128)S(1)}, f32[96,128]{1,0:T(8,128)S(1)}, u32[]{:S(2)}, u32[]{:S(2)}) collective-permute-start(f32[96,128]{1,0:T(8,128)S(1)} %get-tuple-element.42), channel_id=1, source_target_pairs={{0,16},{16,0},{32,48},{48,32},{64,80},{80,64},{96,112},{112,96},{1... | collective-permute-start | bytes 147464 | tf_op jit(solution)/shard_map/ppermute | solution.py:218
  59.1 5.0 %collective-permute-start.20 = (f32[96,128]{1,0:T(8,128)S(1)}, f32[96,128]{1,0:T(8,128)S(1)}, u32[]{:S(2)}, u32[]{:S(2)}) collective-permute-start(f32[96,128]{1,0:T(8,128)S(1)} %add.84), channel_id=1, source_target_pairs={{0,32},{16,48},{32,0},{48,16},{64,96},{80,112},{96,64},{112,80},{1... | collective-permute-start | bytes 147464 | tf_op jit(solution)/shard_map/ppermute | solution.py:218
  59.2 7.4 %collective-permute-start.21 = (f32[96,128]{1,0:T(8,128)S(1)}, f32[96,128]{1,0:T(8,128)S(1)}, u32[]{:S(2)}, u32[]{:S(2)}) collective-permute-start(f32[96,128]{1,0:T(8,128)S(1)} %add.84), channel_id=1, source_target_pairs={{0,64},{16,80},{32,96},{48,112},{64,0},{80,16},{96,32},{112,48},{1... | collective-permute-start | bytes 147464 | tf_op jit(solution)/shard_map/ppermute | solution.py:218
  63.6 5.3 %collective-permute-start.22 = (f32[96,128]{1,0:T(8,128)S(1)}, f32[96,128]{1,0:T(8,128)S(1)}, u32[]{:S(2)}, u32[]{:S(2)}) collective-permute-start(f32[96,128]{1,0:T(8,128)S(1)} %add.84), channel_id=1, source_target_pairs={{0,96},{16,112},{32,64},{48,80},{64,32},{80,48},{96,0},{112,16},{1... | collective-permute-start | bytes 147464 | tf_op jit(solution)/shard_map/ppermute | solution.py:218
  69.0 7.3 %collective-permute-start.23 = (f32[96,128]{1,0:T(8,128)S(1)}, f32[96,128]{1,0:T(8,128)S(1)}, u32[]{:S(2)}, u32[]{:S(2)}) collective-permute-start(f32[96,128]{1,0:T(8,128)S(1)} %add_add_fusion.4), channel_id=1, source_target_pairs={{0,1},{1,0},{2,3},{3,2},{4,5},{5,4},{6,7},{7,6},{8,9},{9,8},{10,11... | collective-permute-start | bytes 147464 | tf_op jit(solution)/shard_map/ppermute | solution.py:218
  73.5 5.6 %collective-permute-start.24 = (f32[96,128]{1,0:T(8,128)S(1)}, f32[96,128]{1,0:T(8,128)S(1)}, u32[]{:S(2)}, u32[]{:S(2)}) collective-permute-start(f32[96,128]{1,0:T(8,128)S(1)} %add_add_fusion.4), channel_id=1, source_target_pairs={{0,2},{1,3},{2,0},{3,1},{4,6},{5,7},{6,4},{7,5},{8,10},{9,11},{10,... | collective-permute-start | bytes 147464 | tf_op jit(solution)/shard_map/ppermute | solution.py:218
  76.3 5.3 %collective-permute-start.25 = (f32[96,128]{1,0:T(8,128)S(1)}, f32[96,128]{1,0:T(8,128)S(1)}, u32[]{:S(2)}, u32[]{:S(2)}) collective-permute-start(f32[96,128]{1,0:T(8,128)S(1)} %add_add_fusion.4), channel_id=1, source_target_pairs={{0,3},{1,2},{2,1},{3,0},{4,7},{5,6},{6,5},{7,4},{8,11},{9,10},{10,... | collective-permute-start | bytes 147464 | tf_op jit(solution)/shard_map/ppermute | solution.py:218
  81.6 10.8 %collective-permute-start.26 = (f32[96,128]{1,0:T(8,128)S(1)}, f32[96,128]{1,0:T(8,128)S(1)}, u32[]{:S(2)}, u32[]{:S(2)}) collective-permute-start(f32[96,128]{1,0:T(8,128)S(1)} %add_add_fusion.3), channel_id=1, source_target_pairs={{0,4},{1,5},{2,6},{3,7},{4,0},{5,1},{6,2},{7,3},{8,12},{9,13},{10,... | collective-permute-start | bytes 147464 | tf_op jit(solution)/shard_map/ppermute | solution.py:218
  89.7 5.7 %collective-permute-start.27 = (f32[96,128]{1,0:T(8,128)S(1)}, f32[96,128]{1,0:T(8,128)S(1)}, u32[]{:S(2)}, u32[]{:S(2)}) collective-permute-start(f32[96,128]{1,0:T(8,128)S(1)} %add_add_fusion.3), channel_id=1, source_target_pairs={{0,8},{1,9},{2,10},{3,11},{4,12},{5,13},{6,14},{7,15},{8,0},{9,1},... | collective-permute-start | bytes 147464 | tf_op jit(solution)/shard_map/ppermute | solution.py:218
  89.7 5.8 %collective-permute-start.28 = (f32[96,128]{1,0:T(8,128)S(1)}, f32[96,128]{1,0:T(8,128)S(1)}, u32[]{:S(2)}, u32[]{:S(2)}) collective-permute-start(f32[96,128]{1,0:T(8,128)S(1)} %add_add_fusion.3), channel_id=1, source_target_pairs={{0,12},{1,13},{2,14},{3,15},{4,8},{5,9},{6,10},{7,11},{8,4},{9,5},... | collective-permute-start | bytes 147464 | tf_op jit(solution)/shard_map/ppermute | solution.py:218
  (7 other events, 5.3 us)

commit v2 on v1

v2 whole, which is shorter than its diff:
```python
import functools
import jax
import jax.numpy as jnp
from jax import lax
from jax.experimental import pallas as pl
from jax.experimental.pallas import tpu as pltpu
from jax.sharding import PartitionSpec as P

TILE = 128
K = 64
ROWS = 32
SLOTS = 512
NODES_DEV = ROWS * TILE
UNROLL = 8
LIST = 576
PARTS = 4
PART_TILES = 64
CHUNKS = 8
WORST = 32.0
F32 = jnp.float32
BF16 = jnp.bfloat16
NT = (((1,), (1,)), ((), ()))
HIGHEST = lax.Precision.HIGHEST
SLAB = (ROWS, K, TILE)


def vmem():
    return pl.BlockSpec(memory_space=pltpu.VMEM)


def smem():
    return pl.BlockSpec(memory_space=pltpu.SMEM)


def hbm():
    return pl.BlockSpec(memory_space=pltpu.HBM)


def in_hbm(x):
    return pltpu.with_memory_space_constraint(x, pltpu.HBM)


def call(kernel, name, out_shape, in_specs, out_specs, mib, us, scratch=()):
    return pl.pallas_call(
        kernel, out_shape=out_shape, in_specs=in_specs, out_specs=out_specs, scratch_shapes=list(scratch), name=name,
        compiler_params=pltpu.CompilerParams(vmem_limit_bytes=mib << 20),
        cost_estimate=pl.CostEstimate(flops=int(us * 1e9), bytes_accessed=int(us * 3e6), transcendentals=0))


def split(x):
    hi = x.astype(BF16)
    return hi, (x - hi.astype(F32)).astype(BF16)


def dot3(a, b):
    ah, al = split(a)
    bh, bl = split(b)
    return jnp.dot(jnp.concatenate([ah, ah, al], axis=1), jnp.concatenate([bh, bl, bh], axis=0),
                   preferred_element_type=F32)


def round_kernel(x_hbm, half_ref, x_ref, sems):
    wide = NODES_DEV // 4
    copies = [pltpu.make_async_copy(x_hbm.at[:, c * wide:(c + 1) * wide], x_ref.at[:, c * wide:(c + 1) * wide],
                                    sems.at[c]) for c in range(4)]
    for copy in copies:
        copy.start()
    for c, copy in enumerate(copies):
        copy.wait()
        for t in range(c * wide // TILE, (c + 1) * wide // TILE):
            half_ref[t] = x_ref[:, t * TILE:(t + 1) * TILE].astype(BF16)


def build_lists(column, degree, table_ref, count_ref):
    member_row = lax.axis_index("row")
    z = lax.shift_right_logical(member_row, 1)
    core = member_row & 1
    from_z = (z + 3 + 2 * core) & 3
    peer = lax.shift_right_logical(column, 9)
    peer_z = lax.shift_right_logical(peer, 1)
    dz = (peer_z - z) & 3
    dc = (peer & 1) ^ core
    side = jnp.where(peer_z == from_z, 1, 0)
    odd = (dz & 1) == 1
    part = jnp.where(odd, jnp.where(side == 1 - dc, 1, 2), jnp.where(dz == 0, 0, 3))
    tile = (column & 31) + 32 * jnp.where(odd, 1 - side, dc)
    r_i = lax.broadcasted_iota(jnp.int32, (ROWS, ROWS), 0)
    r_j = lax.broadcasted_iota(jnp.int32, (ROWS, ROWS), 1)
    degrees = jnp.broadcast_to(degree, (ROWS, ROWS))
    starts = jnp.sum(jnp.where(r_j < r_i, degrees, 0), axis=1, keepdims=True)
    ends = jnp.sum(jnp.where(r_j <= r_i, degrees, 0), axis=1, keepdims=True)
    s = lax.broadcasted_iota(jnp.int32, (ROWS, SLOTS), 1)
    member = jnp.where((s >= starts) & (s < ends), 1.0, 0.0)
    row = jnp.sum(member * lax.broadcasted_iota(jnp.int32, (ROWS, SLOTS), 0).astype(F32), axis=0, keepdims=True)
    used = jnp.sum(member, axis=0, keepdims=True)
    member = member.astype(BF16)
    line = lax.broadcasted_iota(jnp.int32, (8, SLOTS), 0)
    mine = jnp.where((line == part) & (used > 0.5), 1.0, 0.0)
    mine_half = mine.astype(BF16)
    s_i = lax.broadcasted_iota(jnp.int32, (SLOTS, SLOTS), 0)
    s_j = lax.broadcasted_iota(jnp.int32, (SLOTS, SLOTS), 1)
    before = jnp.where(s_i < s_j, 1.0, 0.0).astype(BF16)
    rank = jnp.dot(mine_half, before, preferred_element_type=F32)
    per_row = lax.dot_general(mine_half, member, NT, preferred_element_type=F32).astype(jnp.int32)
    pad = per_row & 1
    earlier = jnp.where(r_i < r_j, 1.0, 0.0).astype(BF16)
    pads = jnp.dot(pad.astype(F32).astype(BF16), earlier, preferred_element_type=F32)
    shift = jnp.dot(pads.astype(BF16), member, preferred_element_type=F32)
    base = (line * LIST).astype(F32)
    place = (jnp.sum(mine * (rank + shift + base + 1.0), axis=0, keepdims=True) - 1.0).astype(jnp.int32)
    slot = lax.broadcasted_iota(jnp.int32, (1, SLOTS), 1)
    values = jnp.where(line == 0, tile, jnp.where(line == 1, slot & 31, jnp.where(
        line == 2, lax.shift_right_logical(slot, 5), jnp.where(line == 3, row.astype(jnp.int32), 1))))
    values = values.astype(F32).astype(BF16)
    for c in range(PARTS * LIST // 256):
        at = lax.broadcasted_iota(jnp.int32, (256, SLOTS), 0) + c * 256
        hot = jnp.where(at == place, 1.0, 0.0).astype(BF16)
        got = lax.dot_general(values, hot, NT, preferred_element_type=F32).astype(jnp.int32)
        entry = got[0:1] | (got[1:2] << 10) | (got[2:3] << 15) | (got[3:4] << 20)
        table_ref[0:1, c * 256:(c + 1) * 256] = jnp.where(got[4:5] > 0, entry, PART_TILES)
    length = jnp.sum(per_row + pad, axis=1, keepdims=True)
    first = lax.broadcasted_iota(jnp.int32, (8, 1), 0)
    for p in range(PARTS):
        n = jnp.sum(jnp.where(first == p, length, 0))
        count_ref[p] = lax.div(n + 2 * UNROLL - 1, 2 * UNROLL)


def multiply_part(part, list_ref, count_ref, tiles_ref, picked_ref, w_ref):
    def group(g, carry):
        base = part * LIST + g * (2 * UNROLL)
        rows, products = [], []
        for u in range(UNROLL):
            first, second = list_ref[0, base + 2 * u], list_ref[0, base + 2 * u + 1]
            x = [picked_ref[e & 127] for e in (first, second)]
            a = [tiles_ref[lax.shift_right_logical(e, 10) & 511] for e in (first, second)]
            rows.append(lax.shift_right_logical(first, 20))
            products.append(lax.dot_general(
                jnp.concatenate(x, axis=1), jnp.concatenate(a, axis=1), NT, preferred_element_type=F32))
        for row, product in zip(rows, products):
            w_ref[row] += product
        return carry

    lax.fori_loop(0, count_ref[part], group, 0)


def place_tiles(picked_ref, first_ref, second_ref):
    picked_ref[0:ROWS] = first_ref[...]
    picked_ref[ROWS:2 * ROWS] = second_ref[...]
    picked_ref[PART_TILES] = jnp.zeros((K, TILE), BF16)


def prepare_kernel(tiles_hbm, column_hbm, degree_hbm, prev_hbm, weight_hbm, coupling_hbm, x_ref,
                   tiles_ref, w_ref, zx_ref, g_ref, list_ref, count_ref,
                   column_ref, degree_ref, prev_ref, weight_ref, coupling_ref, table_ref, sems, tile_sems):
    small = [pltpu.make_async_copy(a, b, sems.at[i]) for i, (a, b) in enumerate((
        (column_hbm, column_ref), (degree_hbm, degree_ref), (coupling_hbm, coupling_ref), (weight_hbm, weight_ref),
        (prev_hbm, prev_ref)))]
    n = SLOTS // CHUNKS
    large = [pltpu.make_async_copy(tiles_hbm.at[c * n:(c + 1) * n], tiles_ref.at[c * n:(c + 1) * n], tile_sems.at[c])
             for c in range(CHUNKS)]
    for copy in small + large:
        copy.start()
    small[0].wait()
    small[1].wait()
    build_lists(column_ref[...], degree_ref[...], table_ref, count_ref)
    table = pltpu.make_async_copy(table_ref, list_ref, sems.at[5])
    table.start()
    for copy in small[2:]:
        copy.wait()
    chi, clo = split(coupling_ref[...])
    left = jnp.concatenate([chi, chi, clo], axis=1)
    wide = 512
    for c in range(NODES_DEV // wide):
        lanes = slice(c * wide, (c + 1) * wide)
        x = x_ref[:, lanes]
        xhi, xlo = split(x)
        zx_ref[0:K, lanes] = xhi
        zx_ref[K:2 * K, lanes] = xlo
        phi, plo = split(prev_ref[:, lanes])
        coupled = jnp.dot(left, jnp.concatenate([phi, plo, phi], axis=0), preferred_element_type=F32)
        w = x * weight_ref[:, lanes] - coupled
        for t in range(wide // TILE):
            w_ref[c * (wide // TILE) + t] = w[:, t * TILE:(t + 1) * TILE]
    zx = zx_ref[...]
    gg = lax.dot_general(zx[:K], zx, NT, preferred_element_type=F32)
    cross = gg[:, K:]
    g_ref[...] = gg[:, :K] + cross + cross.T
    table.wait()
    for copy in large:
        copy.wait()


def near_kernel(list_ref, count_ref, tiles_ref, half_ref, sib_ref, a_ref, b_ref, w_in_ref, w_ref, picked_ref):
    w_ref[...] = w_in_ref[...]
    place_tiles(picked_ref, half_ref, sib_ref)
    multiply_part(0, list_ref, count_ref, tiles_ref, picked_ref, w_ref)
    place_tiles(picked_ref, a_ref, b_ref)
    multiply_part(1, list_ref, count_ref, tiles_ref, picked_ref, w_ref)


def middle_kernel(list_ref, count_ref, tiles_ref, a_ref, b_ref, w_in_ref, w_ref, picked_ref):
    w_ref[...] = w_in_ref[...]
    place_tiles(picked_ref, a_ref, b_ref)
    multiply_part(2, list_ref, count_ref, tiles_ref, picked_ref, w_ref)


def far_kernel(list_ref, count_ref, tiles_ref, a_ref, b_ref, w_in_ref, zx_ref, g_ref, zw_ref, sums_ref, w_ref,
               picked_ref):
    w_ref[...] = w_in_ref[...]
    place_tiles(picked_ref, a_ref, b_ref)
    multiply_part(3, list_ref, count_ref, tiles_ref, picked_ref, w_ref)
    for t in range(ROWS):
        whi, wlo = split(w_ref[t])
        zw_ref[0:K, t * TILE:(t + 1) * TILE] = whi
        zw_ref[K:2 * K, t * TILE:(t + 1) * TILE] = wlo
    zw = zw_ref[...]
    m = lax.dot_general(zx_ref[...], zw, NT, preferred_element_type=F32)
    s = lax.dot_general(zw[:K], zw, NT, preferred_element_type=F32)
    cross = s[:, K:]
    sums_ref[0:K, 0:K] = m[:K, :K] + m[:K, K:] + m[K:, :K]
    sums_ref[0:K, K:] = s[:, :K] + cross + cross.T
    g = g_ref[...]
    sums_ref[K:, 0:K] = g[:K // 2]
    sums_ref[K:, K:] = g[K // 2:]


def eliminate(blocks):
    shape = blocks[0].shape
    count = len(blocks)
    sub = lax.broadcasted_iota(jnp.int32, shape, 0)
    wide = lambda v: jnp.broadcast_to(v, shape)
    done, pivots = [None] * count, []
    for start in range(0, 8 * count, 4):
        b, o = divmod(start, 8)
        head = blocks[b]
        line = [wide(head[o + j:o + j + 1, :]) for j in range(4)]
        column = [[wide(blocks[i][:, start + j:start + j + 1]) for j in range(4)] for i in range(b, count)]
        a = [[wide(column[0][l][o + j:o + j + 1, :]) for l in range(4)] for j in range(4)]
        inverse, m = [None] * 4, {}
        for j in range(4):
            inverse[j] = 1.0 / a[j][j]
            for t in range(j + 1, 4):
                m[t, j] = a[j][t] * inverse[j]
                for l in range(t, 4):
                    a[t][l] = a[t][l] - m[t, j] * a[j][l]
            for t in range(j + 1, 4):
                line[t] = line[t] - m[t, j] * line[j]
        scaled = [line[j] * inverse[j] for j in range(4)]
        for i in range(b, count):
            if i == b and o == 4:
                continue
            c = column[i - b]
            for j in range(4):
                for t in range(j + 1, 4):
                    c[t] = c[t] - m[t, j] * c[j]
            blocks[i] = blocks[i] - ((c[0] * scaled[0] + c[1] * scaled[1]) + (c[2] * scaled[2] + c[3] * scaled[3]))
        rows = blocks[b] if done[b] is None else done[b]
        for j in range(4):
            rows = jnp.where(sub == o + j, line[j] * lax.rsqrt(a[j][j]), rows)
            pivots.append(a[j][j])
        done[b] = rows
    return done, pivots


def factor_kernel(node_total, sums_ref, rayleigh_ref, r_ref, f_ref, flag_ref):
    inv = 1.0 / node_total
    r = sums_ref[0:K, 0:K] * inv
    s = sums_ref[0:K, K:] * inv
    g = jnp.concatenate([sums_ref[K:, 0:K], sums_ref[K:, K:]], axis=0) * inv
    row = lax.broadcasted_iota(jnp.int32, (K, K), 0)
    col = lax.broadcasted_iota(jnp.int32, (K, K), 1)
    eye = jnp.where(row == col, 1.0, 0.0)
    rt = r.T
    gram = s - dot3(rt, dot3(2.0 * eye - g, r))
    work = jnp.concatenate([gram, eye], axis=1)
    done, pivots = eliminate([work[8 * b:8 * b + 8] for b in range(K // 8)])
    work = jnp.concatenate(done, axis=0)
    lower_inv = jnp.where(col <= row, work[:, K:], 0.0)
    rayleigh_ref[...] = r
    r_ref[...] = jnp.where(col >= row, work[:, :K], 0.0)
    f_ref[:, 0:K] = lower_inv
    f_ref[:, K:] = -dot3(lower_inv, rt)
    largest = jnp.max(jnp.where(row == col, s, 0.0))
    smallest = jnp.min(functools.reduce(jnp.minimum, pivots))
    flag_ref[0] = jnp.where(smallest * WORST >= largest, 0, 1).astype(jnp.int32)


def final_kernel(f_ref, zw_ref, zx_ref, out_ref):
    f1h, f1l = split(f_ref[:, 0:K])
    f2h, f2l = split(f_ref[:, K:])
    zero = jnp.zeros((K, K), BF16)
    left = jnp.concatenate([jnp.concatenate([f1h, f1h, f2h, f2h], axis=1),
                            jnp.concatenate([f1l, zero, f2l, zero], axis=1)], axis=0)
    wide = 512
    for c in range(NODES_DEV // wide):
        lanes = slice(c * wide, (c + 1) * wide)
        z = jnp.concatenate([zw_ref[:, lanes], zx_ref[:, lanes]], axis=0)
        y = jnp.dot(left, z, preferred_element_type=F32)
        out_ref[:, lanes] = y[:K] + y[K:]


def exchange(v, axis, to):
    n = lax.axis_size(axis)
    return lax.ppermute(v, axis, [(i, to(i)) for i in range(n)])


def core_swap(v):
    return exchange(v, "row", lambda i: i ^ 1)


def onward(v):
    return exchange(v, "row", lambda i: (i + (2 if i % 2 == 0 else 6)) % 8)


def total(v):
    v = v + core_swap(v)
    for axis, unit in (("row", 2), ("col", 1), ("col", 4)):
        others = [exchange(v, axis, lambda i, d=d * unit: i ^ d) for d in (1, 2, 3)]
        v = (v + others[0]) + (others[1] + others[2])
    return v


def local(tile_blocks, tile_column, row_degree, node_weight, block_now, block_prev, coupling):
    node_total = NODES_DEV * lax.axis_size("row") * lax.axis_size("col")
    after = lax.optimization_barrier
    slab_vmem = pltpu.VMEM(SLAB, F32)
    picked = pltpu.VMEM((PART_TILES + 1, K, TILE), BF16)
    pair_vmem = pltpu.VMEM((2 * K, NODES_DEV), BF16)
    square = jax.ShapeDtypeStruct((K, K), F32)

    half, x = call(
        round_kernel, "round_block", (pltpu.VMEM(SLAB, BF16), pltpu.VMEM((K, NODES_DEV), F32)), [hbm()],
        (vmem(), vmem()), 8, 1, [pltpu.SemaphoreType.DMA((4,))])(in_hbm(block_now.T))
    a1 = onward(half)
    sib = core_swap(half)
    sib, x = after((sib, x))
    a2 = onward(sib)
    tiles, w1, zx, g, lists, counts = call(
        prepare_kernel, "prepare",
        (pltpu.VMEM((SLOTS, TILE, TILE), BF16), slab_vmem, pair_vmem, pltpu.VMEM((K, K), F32),
         pltpu.SMEM((1, PARTS * LIST), jnp.int32), pltpu.SMEM((PARTS,), jnp.int32)),
        [hbm()] * 6 + [vmem()], (vmem(), vmem(), vmem(), vmem(), smem(), smem()), 16, 7,
        [pltpu.VMEM((1, SLOTS), jnp.int32), pltpu.VMEM((1, ROWS), jnp.int32), pltpu.VMEM((K, NODES_DEV), F32),
         pltpu.VMEM((1, NODES_DEV), F32), pltpu.VMEM((K, K), F32), pltpu.VMEM((1, PARTS * LIST), jnp.int32),
         pltpu.SemaphoreType.DMA((6,)), pltpu.SemaphoreType.DMA((CHUNKS,))])(
            in_hbm(tile_blocks), in_hbm(tile_column.reshape(1, SLOTS)), in_hbm(row_degree.reshape(1, ROWS)),
            in_hbm(block_prev.T), in_hbm(node_weight.reshape(1, NODES_DEV)), in_hbm(coupling), x)

    a1, w1 = after((a1, w1))
    a3 = onward(a1)
    b1 = core_swap(a1)
    w2 = call(near_kernel, "near_parts", slab_vmem, [smem(), smem()] + [vmem()] * 6, vmem(), 12, 5, [picked])(
        lists, counts, tiles, half, sib, a1, b1, w1)
    a2, w2 = after((a2, w2))
    b2 = core_swap(a2)
    w3 = call(middle_kernel, "middle_part", slab_vmem, [smem(), smem()] + [vmem()] * 4, vmem(), 12, 3, [picked])(
        lists, counts, tiles, a2, b2, w2)
    a3, w3 = after((a3, w3))
    b3 = core_swap(a3)
    zw, sums = call(
        far_kernel, "far_part", (pair_vmem, jax.ShapeDtypeStruct((K + K // 2, 2 * K), F32)),
        [smem(), smem()] + [vmem()] * 6, (vmem(), vmem()), 16, 5, [slab_vmem, picked])(
            lists, counts, tiles, a3, b3, w3, zx, g)

    sums = total(sums)
    rayleigh, r_factor, f, flag = call(
        functools.partial(factor_kernel, node_total), "factor",
        (square, square, jax.ShapeDtypeStruct((K, 2 * K), F32), jax.ShapeDtypeStruct((1,), jnp.int32)),
        [vmem()], (vmem(), vmem(), vmem(), smem()), 8, 5)(sums)

    def plain(zw, zx, f, sums, r_factor):
        out = call(final_kernel, "scale_block", jax.ShapeDtypeStruct((K, NODES_DEV), F32), [vmem()] * 3, vmem(), 12, 2)(
            f, zw, zx)
        return out, r_factor

    def two_passes(zw, zx, f, sums, r_factor):
        whole = lambda z: z[:K].astype(F32) + z[K:].astype(F32)
        rayleigh_t = sums[:K, :K].T / node_total
        w_next = whole(zw) - jnp.dot(rayleigh_t, whole(zx), precision=HIGHEST)
        gram = total(jnp.dot(w_next, w_next.T, precision=HIGHEST)) / node_total
        lower = jnp.linalg.cholesky(gram)
        return jax.scipy.linalg.solve_triangular(lower, w_next, lower=True), lower.T

    out, r_factor = lax.cond(flag[0] == 0, plain, two_passes, zw, zx, f, sums, r_factor)
    return out.T, rayleigh, r_factor


def solution(mesh):
    in_specs = (
        P(("row", "col"), None, None),
        P(("row", "col")),
        P(("row", "col")),
        P(("row", "col")),
        P(("row", "col"), None),
        P(("row", "col"), None),
        P(),
    )
    out_specs = (P(("row", "col"), None), P(), P())
    return jax.shard_map(local, mesh=mesh, in_specs=in_specs, out_specs=out_specs, check_vma=False)
```

time: 109 us -> 74.3 us (0.68)
  starting transfers between devices: 31.9 us -> 16.6 us
  local copies, waits for them, and re-layouts: 14.7 us -> 0.61 us
  Pallas kernels: 27.3 us -> 23.9 us
    ppermute x19 -> x17, starting transfers between devices: 31.9 us -> 16.6 us  [exchange(): return lax.ppermute(v, axis, [(i, to(i)) for i in range(n)])]
    unnamed x24 -> x2, local copies, waits for them, and re-layouts: 14.7 us -> 0.61 us
    pallas_call x6 -> x7, Pallas kernels: 27.3 us -> 23.9 us  [the longest x1 6.92 us: local(): call(prepare_kernel, 'prepare', (pltpu.VMEM((SLOTS, TILE, TILE), BF16), s...]
    ppermute x19 -> x17, waiting for transfers between devices: 32.4 us -> 31.4 us  [exchange(): return lax.ppermute(v, axis, [(i, to(i)) for i in range(n)])]
  transfers between devices with their start and end apart: 19 -> 17, of which waited for: 9 -> 13; matrix products, arithmetic and copies ran while one was open for 0% -> 0% of each run, Pallas kernels for 11% -> 19%
where the time goes in v2:
time: 74.3 us; the launch traced here: 74.1 us
  waiting for transfers between devices  31.4 us (42%)
  Pallas kernels  23.9 us (32%)
  starting transfers between devices  16.6 us (22%)
  between operations  1.37 us (2%)
    ppermute x17, waiting for transfers between devices, exchange(): return lax.ppermute(v, axis, [(i, to(i)) for i in range(n)])  31.4 us
    ppermute x17, starting transfers between devices, exchange(): return lax.ppermute(v, axis, [(i, to(i)) for i in range(n)])  16.6 us
    pallas_call x1, Pallas kernels, local(): call(prepare_kernel, 'prepare', (pltpu.VMEM((SLOTS, TILE, TILE), BF16), s...  6.92 us
    pallas_call x1, Pallas kernels, local(): call(near_kernel, 'near_parts', slab_vmem, [smem(), smem()] + [vmem()] *...  4.54 us
    pallas_call x1, Pallas kernels, local(): call(functools.partial(factor_kernel, node_total), 'factor', (square, squ...  4.11 us
    pallas_call x1, Pallas kernels, local(): call(far_kernel, 'far_part', (pair_vmem, jax.ShapeDtypeStruct((K + K // 2...  2.98 us
    pallas_call x1, Pallas kernels, local(): call(middle_kernel, 'middle_part', slab_vmem, [smem(), smem()] + [vmem()]...  2.62 us
  transfers between devices with their start and end apart: 17, of which 13 were waited for; matrix products, arithmetic and copies ran while one was open for 0% of the time, Pallas kernels for 19%

profile of v2, /device:TPU:0, one launch (start us, length us, event | category | flops | bytes accessed | tf_op | source)
XLA Modules:
  0.0 74.1 jit_solution(7314832340658392999)
XLA Ops:
  2.0 2.1 %collective-permute-start.11 = (bf16[32,64,128]{2,1,0:T(8,128)(2,1)S(1)}, bf16[32,64,128]{2,1,0:T(8,128)(2,1)S(1)}, u32[]{:S(2)}, u32[]{:S(2)}) collective-permute-start(bf16[32,64,128]{2,1,0:T(8,128)(2,1)S(1)} %get-tuple-element.48.half_ref), channel_id=1, source_target_pairs={{0,32},{16,112},{32,64},{48,16},{64,96},{80,48},{96,0},{112,80},{1... | collective-permute-start | bytes 1572872 | tf_op jit(solution)/shard_map/ppermute | solution.py:304
  4.0 6.9 %prepare.1 = (bf16[512,128,128]{2,1,0:T(8,128)(2,1)S(1)}, f32[32,64,128]{2,1,0:T(8,128)S(1)}, bf16[128,4096]{1,0:T(8,128)(2,1)S(1)}, f32[64,64]{1,0:T(8,128)S(1)}, s32[1,2304]{1,0:T(1,128)S(4)}, /*index=5*/s32[4]{0:T(128)S(4)}) custom-call(bf16[512,128,128]{2,1,0:T(8,128)(2,1)} %tiles_hbm.1, s32[1,512]{1,0:T(1,128)} %bitcast.24, s32[1,32]{1,0:T(1,128)} %bitcast.25, ...), custom_call_target="tpu_custom_call" | custom-call | flops 7000000000 | bytes 21000000 | tf_op jit(solution)/shard_map/prepare/pallas_call | solution.py:338
  11.0 2.3 %collective-permute-done.11.a_ref = bf16[32,64,128]{2,1,0:T(8,128)(2,1)S(1)} collective-permute-done((bf16[32,64,128]{2,1,0:T(8,128)(2,1)S(1)}, bf16[32,64,128]{2,1,0:T(8,128)(2,1)S(1)}, u32[]{:S(2)}, u32[]{:S(2)}) %collective-permute-start.11) | collective-permute-done | bytes 524320 | tf_op jit(solution)/shard_map/ppermute | solution.py:304
  13.3 1.9 %collective-permute-done.14.b_ref = bf16[32,64,128]{2,1,0:T(8,128)(2,1)S(1)} collective-permute-done((bf16[32,64,128]{2,1,0:T(8,128)(2,1)S(1)}, bf16[32,64,128]{2,1,0:T(8,128)(2,1)S(1)}, u32[]{:S(2)}, u32[]{:S(2)}) %collective-permute-start.14) | collective-permute-done | bytes 524320 | tf_op jit(solution)/shard_map/ppermute | solution.py:304
  15.2 4.5 %near_parts.1.w_in_ref = f32[32,64,128]{2,1,0:T(8,128)S(1)} custom-call(s32[1,2304]{1,0:T(1,128)S(4)} %get-tuple-element.51.list_ref, s32[4]{0:T(128)S(4)} %get-tuple-element.52.count_ref, bf16[512,128,128]{2,1,0:T(8,128)(2,1)S(1)} %get-tuple-element.53.tiles_ref, bf16[32,64,128]{2,1,0:T(8,128)(2,1)S(1)} %get-tuple-element.48.half_ref, ...), custom_call_target="tpu_custom_call" | custom-call | flops 5000000000 | bytes 15000000 | tf_op jit(solution)/shard_map/near_parts/pallas_call | solution.py:352
  19.8 3.9 %collective-permute-done.13.a_ref = bf16[32,64,128]{2,1,0:T(8,128)(2,1)S(1)} collective-permute-done((bf16[32,64,128]{2,1,0:T(8,128)(2,1)S(1)}, bf16[32,64,128]{2,1,0:T(8,128)(2,1)S(1)}, u32[]{:S(2)}, u32[]{:S(2)}) %collective-permute-start.13) | collective-permute-done | bytes 524320 | tf_op jit(solution)/shard_map/ppermute | solution.py:304
  23.7 1.9 %collective-permute-done.15.b_ref = bf16[32,64,128]{2,1,0:T(8,128)(2,1)S(1)} collective-permute-done((bf16[32,64,128]{2,1,0:T(8,128)(2,1)S(1)}, bf16[32,64,128]{2,1,0:T(8,128)(2,1)S(1)}, u32[]{:S(2)}, u32[]{:S(2)}) %collective-permute-start.15) | collective-permute-done | bytes 524320 | tf_op jit(solution)/shard_map/ppermute | solution.py:304
  25.6 2.6 %middle_part.1.w_in_ref = f32[32,64,128]{2,1,0:T(8,128)S(1)} custom-call(s32[1,2304]{1,0:T(1,128)S(4)} %get-tuple-element.51.list_ref, s32[4]{0:T(128)S(4)} %get-tuple-element.52.count_ref, bf16[512,128,128]{2,1,0:T(8,128)(2,1)S(1)} %get-tuple-element.53.tiles_ref, bf16[32,64,128]{2,1,0:T(8,128)(2,1)S(1)} %collective-permute-done.13.a_ref, ...), custom_call_target="tpu_custom_call" | custom-call | flops 3000000000 | bytes 9000000 | tf_op jit(solution)/shard_map/middle_part/pallas_call | solution.py:356
  28.3 5.9 %collective-permute-done.12.a_ref = bf16[32,64,128]{2,1,0:T(8,128)(2,1)S(1)} collective-permute-done((bf16[32,64,128]{2,1,0:T(8,128)(2,1)S(1)}, bf16[32,64,128]{2,1,0:T(8,128)(2,1)S(1)}, u32[]{:S(2)}, u32[]{:S(2)}) %collective-permute-start.12) | collective-permute-done | bytes 524320 | tf_op jit(solution)/shard_map/ppermute | solution.py:304
  34.1 1.9 %collective-permute-done.16.b_ref = bf16[32,64,128]{2,1,0:T(8,128)(2,1)S(1)} collective-permute-done((bf16[32,64,128]{2,1,0:T(8,128)(2,1)S(1)}, bf16[32,64,128]{2,1,0:T(8,128)(2,1)S(1)}, u32[]{:S(2)}, u32[]{:S(2)}) %collective-permute-start.16) | collective-permute-done | bytes 524320 | tf_op jit(solution)/shard_map/ppermute | solution.py:304
  36.0 3.0 %far_part.1 = (bf16[128,4096]{1,0:T(8,128)(2,1)S(1)}, f32[96,128]{1,0:T(8,128)S(1)}) custom-call(s32[1,2304]{1,0:T(1,128)S(4)} %get-tuple-element.51.list_ref, s32[4]{0:T(128)S(4)} %get-tuple-element.52.count_ref, bf16[512,128,128]{2,1,0:T(8,128)(2,1)S(1)} %get-tuple-element.53.tiles_ref, bf16[32,64,128]{2,1,0:T(8,128)(2,1)S(1)} %collective-permute-done.12.a_ref, ...), custom_call_target="tpu_custom_call" | custom-call | flops 5000000000 | bytes 15000000 | tf_op jit(solution)/shard_map/far_part/pallas_call | solution.py:360
  40.4 2.3 %collective-permute-start.19 = (f32[96,128]{1,0:T(8,128)S(1)}, f32[96,128]{1,0:T(8,128)S(1)}, u32[]{:S(2)}, u32[]{:S(2)}) collective-permute-start(f32[96,128]{1,0:T(8,128)S(1)} %add.78), channel_id=1, source_target_pairs={{0,64},{16,80},{32,96},{48,112},{64,0},{80,16},{96,32},{112,48},{1... | collective-permute-start | bytes 147464 | tf_op jit(solution)/shard_map/ppermute | solution.py:304
  42.7 2.4 %collective-permute-start.20 = (f32[96,128]{1,0:T(8,128)S(1)}, f32[96,128]{1,0:T(8,128)S(1)}, u32[]{:S(2)}, u32[]{:S(2)}) collective-permute-start(f32[96,128]{1,0:T(8,128)S(1)} %add.78), channel_id=1, source_target_pairs={{0,96},{16,112},{32,64},{48,80},{64,32},{80,48},{96,0},{112,16},{1... | collective-permute-start | bytes 147464 | tf_op jit(solution)/shard_map/ppermute | solution.py:304
  46.1 1.9 %collective-permute-done.20 = f32[96,128]{1,0:T(8,128)S(1)} collective-permute-done((f32[96,128]{1,0:T(8,128)S(1)}, f32[96,128]{1,0:T(8,128)S(1)}, u32[]{:S(2)}, u32[]{:S(2)}) %collective-permute-start.20) | collective-permute-done | bytes 49184 | tf_op jit(solution)/shard_map/ppermute | solution.py:304
  49.4 2.7 %collective-permute-start.22 = (f32[96,128]{1,0:T(8,128)S(1)}, f32[96,128]{1,0:T(8,128)S(1)}, u32[]{:S(2)}, u32[]{:S(2)}) collective-permute-start(f32[96,128]{1,0:T(8,128)S(1)} %add_add_fusion.4), channel_id=1, source_target_pairs={{0,2},{1,3},{2,0},{3,1},{4,6},{5,7},{6,4},{7,5},{8,10},{9,11},{10,... | collective-permute-start | bytes 147464 | tf_op jit(solution)/shard_map/ppermute | solution.py:304
  52.8 2.2 %collective-permute-done.22 = f32[96,128]{1,0:T(8,128)S(1)} collective-permute-done((f32[96,128]{1,0:T(8,128)S(1)}, f32[96,128]{1,0:T(8,128)S(1)}, u32[]{:S(2)}, u32[]{:S(2)}) %collective-permute-start.22) | collective-permute-done | bytes 49184 | tf_op jit(solution)/shard_map/ppermute | solution.py:304
  55.0 2.3 %collective-permute-done.23 = f32[96,128]{1,0:T(8,128)S(1)} collective-permute-done((f32[96,128]{1,0:T(8,128)S(1)}, f32[96,128]{1,0:T(8,128)S(1)}, u32[]{:S(2)}, u32[]{:S(2)}) %collective-permute-start.23) | collective-permute-done | bytes 49184 | tf_op jit(solution)/shard_map/ppermute | solution.py:304
  57.4 1.9 %collective-permute-start.24 = (f32[96,128]{1,0:T(8,128)S(1)}, f32[96,128]{1,0:T(8,128)S(1)}, u32[]{:S(2)}, u32[]{:S(2)}) collective-permute-start(f32[96,128]{1,0:T(8,128)S(1)} %add_add_fusion.3), channel_id=1, source_target_pairs={{0,4},{1,5},{2,6},{3,7},{4,0},{5,1},{6,2},{7,3},{8,12},{9,13},{10,... | collective-permute-start | bytes 147464 | tf_op jit(solution)/shard_map/ppermute | solution.py:304
  59.3 2.4 %collective-permute-start.25 = (f32[96,128]{1,0:T(8,128)S(1)}, f32[96,128]{1,0:T(8,128)S(1)}, u32[]{:S(2)}, u32[]{:S(2)}) collective-permute-start(f32[96,128]{1,0:T(8,128)S(1)} %add_add_fusion.3), channel_id=1, source_target_pairs={{0,8},{1,9},{2,10},{3,11},{4,12},{5,13},{6,14},{7,15},{8,0},{9,1},... | collective-permute-start | bytes 147464 | tf_op jit(solution)/shard_map/ppermute | solution.py:304
  62.1 2.7 %collective-permute-done.25 = f32[96,128]{1,0:T(8,128)S(1)} collective-permute-done((f32[96,128]{1,0:T(8,128)S(1)}, f32[96,128]{1,0:T(8,128)S(1)}, u32[]{:S(2)}, u32[]{:S(2)}) %collective-permute-start.25) | collective-permute-done | bytes 49184 | tf_op jit(solution)/shard_map/ppermute | solution.py:304
  64.8 2.1 %collective-permute-done.26 = f32[96,128]{1,0:T(8,128)S(1)} collective-permute-done((f32[96,128]{1,0:T(8,128)S(1)}, f32[96,128]{1,0:T(8,128)S(1)}, u32[]{:S(2)}, u32[]{:S(2)}) %collective-permute-start.26) | collective-permute-done | bytes 49184 | tf_op jit(solution)/shard_map/ppermute | solution.py:304
  67.0 4.1 %factor.1 = (f32[64,64]{1,0:T(8,128)}, f32[64,64]{1,0:T(8,128)S(1)}, f32[64,128]{1,0:T(8,128)S(1)}, s32[1]{0:T(128)}) custom-call(f32[96,128]{1,0:T(8,128)S(1)} %add_add_fusion.2.sums_ref), custom_call_target="tpu_custom_call" | custom-call | flops 5000000000 | bytes 15000000 | tf_op jit(solution)/shard_map/factor/pallas_call | solution.py:366
  71.8 1.7 %conditional.1 = (f32[64,4096]{1,0:T(8,128)}, f32[64,64]{1,0:T(8,128)S(1)}) conditional(s32[]{:T(128)} %bitcast.9, (bf16[128,4096]{1,0:T(8,128)(2,1)S(1)}, f32[96,128]{1,0:T(8,128)S(1)}, bf16[128,4096]{1,0:T(8,128)(2,1)S(1)}) %tuple.24, (f32[64,128]{1,0:T(8,128)S(1)}, bf16[128,4096]{1,0:T(8,128)(2,1)S(1)}, bf16[128,4096]{1,0:T(8,128)(2,1)S(1)}, ...), branch_computations={%region_0.0_spmd, %region_3.4_spmd} | conditional | flops 2000000000 | bytes 7586722 | solution.py:384
  72.0 1.5 %scale_block.1 = f32[64,4096]{1,0:T(8,128)} custom-call(f32[64,128]{1,0:T(8,128)S(1)} %get-tuple-element.17.f_ref, bf16[128,4096]{1,0:T(8,128)(2,1)S(1)} %get-tuple-element.18.zw_ref, bf16[128,4096]{1,0:T(8,128)(2,1)S(1)} %get-tuple-element.19.zx_ref), custom_call_target="tpu_custom_call" | custom-call | flops 2000000000 | bytes 6000000 | tf_op jit(solution)/shard_map/cond/branch_1_fun/scale_block/pallas_call | solution.py:372
  (24 shorter events, 7.0 us)
Async XLA Ops:
  1.9 2.2 %collective-permute-start.10 = (bf16[32,64,128]{2,1,0:T(8,128)(2,1)S(1)}, bf16[32,64,128]{2,1,0:T(8,128)(2,1)S(1)}, u32[]{:S(2)}, u32[]{:S(2)}) collective-permute-start(bf16[32,64,128]{2,1,0:T(8,128)(2,1)S(1)} %get-tuple-element.48.half_ref), channel_id=1, source_target_pairs={{0,16},{16,0},{32,48},{48,32},{64,80},{80,64},{96,112},{112,96},{1... | collective-permute-start | bytes 1572872 | tf_op jit(solution)/shard_map/ppermute | solution.py:304
  2.0 11.3 %collective-permute-start.11 = (bf16[32,64,128]{2,1,0:T(8,128)(2,1)S(1)}, bf16[32,64,128]{2,1,0:T(8,128)(2,1)S(1)}, u32[]{:S(2)}, u32[]{:S(2)}) collective-permute-start(bf16[32,64,128]{2,1,0:T(8,128)(2,1)S(1)} %get-tuple-element.48.half_ref), channel_id=1, source_target_pairs={{0,32},{16,112},{32,64},{48,16},{64,96},{80,48},{96,0},{112,80},{1... | collective-permute-start | bytes 1572872 | tf_op jit(solution)/shard_map/ppermute | solution.py:304
  13.3 1.9 %collective-permute-start.14 = (bf16[32,64,128]{2,1,0:T(8,128)(2,1)S(1)}, bf16[32,64,128]{2,1,0:T(8,128)(2,1)S(1)}, u32[]{:S(2)}, u32[]{:S(2)}) collective-permute-start(bf16[32,64,128]{2,1,0:T(8,128)(2,1)S(1)} %collective-permute-done.11.a_ref), channel_id=1, source_target_pairs={{0,16},{16,0},{32,48},{48,32},{64,80},{80,64},{96,112},{112,96},{1... | collective-permute-start | bytes 1572872 | tf_op jit(solution)/shard_map/ppermute | solution.py:304
  13.3 10.4 %collective-permute-start.13 = (bf16[32,64,128]{2,1,0:T(8,128)(2,1)S(1)}, bf16[32,64,128]{2,1,0:T(8,128)(2,1)S(1)}, u32[]{:S(2)}, u32[]{:S(2)}) collective-permute-start(bf16[32,64,128]{2,1,0:T(8,128)(2,1)S(1)} %collective-permute-done.10.sib_ref), channel_id=1, source_target_pairs={{0,32},{16,112},{32,64},{48,16},{64,96},{80,48},{96,0},{112,80},{1... | collective-permute-start | bytes 1572872 | tf_op jit(solution)/shard_map/ppermute | solution.py:304
  23.7 1.9 %collective-permute-start.15 = (bf16[32,64,128]{2,1,0:T(8,128)(2,1)S(1)}, bf16[32,64,128]{2,1,0:T(8,128)(2,1)S(1)}, u32[]{:S(2)}, u32[]{:S(2)}) collective-permute-start(bf16[32,64,128]{2,1,0:T(8,128)(2,1)S(1)} %collective-permute-done.13.a_ref), channel_id=1, source_target_pairs={{0,16},{16,0},{32,48},{48,32},{64,80},{80,64},{96,112},{112,96},{1... | collective-permute-start | bytes 1572872 | tf_op jit(solution)/shard_map/ppermute | solution.py:304
  23.7 10.4 %collective-permute-start.12 = (bf16[32,64,128]{2,1,0:T(8,128)(2,1)S(1)}, bf16[32,64,128]{2,1,0:T(8,128)(2,1)S(1)}, u32[]{:S(2)}, u32[]{:S(2)}) collective-permute-start(bf16[32,64,128]{2,1,0:T(8,128)(2,1)S(1)} %collective-permute-done.11.a_ref), channel_id=1, source_target_pairs={{0,32},{16,112},{32,64},{48,16},{64,96},{80,48},{96,0},{112,80},{1... | collective-permute-start | bytes 1572872 | tf_op jit(solution)/shard_map/ppermute | solution.py:304
  34.1 1.9 %collective-permute-start.16 = (bf16[32,64,128]{2,1,0:T(8,128)(2,1)S(1)}, bf16[32,64,128]{2,1,0:T(8,128)(2,1)S(1)}, u32[]{:S(2)}, u32[]{:S(2)}) collective-permute-start(bf16[32,64,128]{2,1,0:T(8,128)(2,1)S(1)} %collective-permute-done.12.a_ref), channel_id=1, source_target_pairs={{0,16},{16,0},{32,48},{48,32},{64,80},{80,64},{96,112},{112,96},{1... | collective-permute-start | bytes 1572872 | tf_op jit(solution)/shard_map/ppermute | solution.py:304
  39.0 1.3 %collective-permute-start.17 = (f32[96,128]{1,0:T(8,128)S(1)}, f32[96,128]{1,0:T(8,128)S(1)}, u32[]{:S(2)}, u32[]{:S(2)}) collective-permute-start(f32[96,128]{1,0:T(8,128)S(1)} %get-tuple-element.64), channel_id=1, source_target_pairs={{0,16},{16,0},{32,48},{48,32},{64,80},{80,64},{96,112},{112,96},{1... | collective-permute-start | bytes 147464 | tf_op jit(solution)/shard_map/ppermute | solution.py:304
  40.3 4.8 %collective-permute-start.18 = (f32[96,128]{1,0:T(8,128)S(1)}, f32[96,128]{1,0:T(8,128)S(1)}, u32[]{:S(2)}, u32[]{:S(2)}) collective-permute-start(f32[96,128]{1,0:T(8,128)S(1)} %add.78), channel_id=1, source_target_pairs={{0,32},{16,48},{32,0},{48,16},{64,96},{80,112},{96,64},{112,80},{1... | collective-permute-start | bytes 147464 | tf_op jit(solution)/shard_map/ppermute | solution.py:304
  40.4 5.7 %collective-permute-start.19 = (f32[96,128]{1,0:T(8,128)S(1)}, f32[96,128]{1,0:T(8,128)S(1)}, u32[]{:S(2)}, u32[]{:S(2)}) collective-permute-start(f32[96,128]{1,0:T(8,128)S(1)} %add.78), channel_id=1, source_target_pairs={{0,64},{16,80},{32,96},{48,112},{64,0},{80,16},{96,32},{112,48},{1... | collective-permute-start | bytes 147464 | tf_op jit(solution)/shard_map/ppermute | solution.py:304
  42.7 5.3 %collective-permute-start.20 = (f32[96,128]{1,0:T(8,128)S(1)}, f32[96,128]{1,0:T(8,128)S(1)}, u32[]{:S(2)}, u32[]{:S(2)}) collective-permute-start(f32[96,128]{1,0:T(8,128)S(1)} %add.78), channel_id=1, source_target_pairs={{0,96},{16,112},{32,64},{48,80},{64,32},{80,48},{96,0},{112,16},{1... | collective-permute-start | bytes 147464 | tf_op jit(solution)/shard_map/ppermute | solution.py:304
  48.0 4.8 %collective-permute-start.21 = (f32[96,128]{1,0:T(8,128)S(1)}, f32[96,128]{1,0:T(8,128)S(1)}, u32[]{:S(2)}, u32[]{:S(2)}) collective-permute-start(f32[96,128]{1,0:T(8,128)S(1)} %add_add_fusion.4), channel_id=1, source_target_pairs={{0,1},{1,0},{2,3},{3,2},{4,5},{5,4},{6,7},{7,6},{8,9},{9,8},{10,11... | collective-permute-start | bytes 147464 | tf_op jit(solution)/shard_map/ppermute | solution.py:304
  49.4 5.6 %collective-permute-start.22 = (f32[96,128]{1,0:T(8,128)S(1)}, f32[96,128]{1,0:T(8,128)S(1)}, u32[]{:S(2)}, u32[]{:S(2)}) collective-permute-start(f32[96,128]{1,0:T(8,128)S(1)} %add_add_fusion.4), channel_id=1, source_target_pairs={{0,2},{1,3},{2,0},{3,1},{4,6},{5,7},{6,4},{7,5},{8,10},{9,11},{10,... | collective-permute-start | bytes 147464 | tf_op jit(solution)/shard_map/ppermute | solution.py:304
  52.0 5.3 %collective-permute-start.23 = (f32[96,128]{1,0:T(8,128)S(1)}, f32[96,128]{1,0:T(8,128)S(1)}, u32[]{:S(2)}, u32[]{:S(2)}) collective-permute-start(f32[96,128]{1,0:T(8,128)S(1)} %add_add_fusion.4), channel_id=1, source_target_pairs={{0,3},{1,2},{2,1},{3,0},{4,7},{5,6},{6,5},{7,4},{8,11},{9,10},{10,... | collective-permute-start | bytes 147464 | tf_op jit(solution)/shard_map/ppermute | solution.py:304
  57.4 4.8 %collective-permute-start.24 = (f32[96,128]{1,0:T(8,128)S(1)}, f32[96,128]{1,0:T(8,128)S(1)}, u32[]{:S(2)}, u32[]{:S(2)}) collective-permute-start(f32[96,128]{1,0:T(8,128)S(1)} %add_add_fusion.3), channel_id=1, source_target_pairs={{0,4},{1,5},{2,6},{3,7},{4,0},{5,1},{6,2},{7,3},{8,12},{9,13},{10,... | collective-permute-start | bytes 147464 | tf_op jit(solution)/shard_map/ppermute | solution.py:304
  59.3 5.6 %collective-permute-start.25 = (f32[96,128]{1,0:T(8,128)S(1)}, f32[96,128]{1,0:T(8,128)S(1)}, u32[]{:S(2)}, u32[]{:S(2)}) collective-permute-start(f32[96,128]{1,0:T(8,128)S(1)} %add_add_fusion.3), channel_id=1, source_target_pairs={{0,8},{1,9},{2,10},{3,11},{4,12},{5,13},{6,14},{7,15},{8,0},{9,1},... | collective-permute-start | bytes 147464 | tf_op jit(solution)/shard_map/ppermute | solution.py:304
  61.7 5.3 %collective-permute-start.26 = (f32[96,128]{1,0:T(8,128)S(1)}, f32[96,128]{1,0:T(8,128)S(1)}, u32[]{:S(2)}, u32[]{:S(2)}) collective-permute-start(f32[96,128]{1,0:T(8,128)S(1)} %add_add_fusion.3), channel_id=1, source_target_pairs={{0,12},{1,13},{2,14},{3,15},{4,8},{5,9},{6,10},{7,11},{8,4},{9,5},... | collective-permute-start | bytes 147464 | tf_op jit(solution)/shard_map/ppermute | solution.py:304
  73.5 0.6 copy-start

commit v3 on v2

--- a/solution.py
+++ b/solution.py
@@ -14,7 +14,6 @@
 UNROLL = 8
 LIST = 576
 PARTS = 4
-PART_TILES = 64
 CHUNKS = 8
 WORST = 32.0
 F32 = jnp.float32
@@ -40,11 +39,12 @@
     return pltpu.with_memory_space_constraint(x, pltpu.HBM)
 
 
-def call(kernel, name, out_shape, in_specs, out_specs, mib, us, scratch=()):
+def call(kernel, name, out_shape, in_specs, out_specs, mib, us, scratch=(), aliases=None):
     return pl.pallas_call(
         kernel, out_shape=out_shape, in_specs=in_specs, out_specs=out_specs, scratch_shapes=list(scratch), name=name,
+        input_output_aliases=aliases or {},
         compiler_params=pltpu.CompilerParams(vmem_limit_bytes=mib << 20),
-        cost_estimate=pl.CostEstimate(flops=int(us * 1e9), bytes_accessed=int(us * 3e6), transcendentals=0))
+        cost_estimate=pl.CostEstimate(flops=int(us * 1e5), bytes_accessed=int(us * 1e3), transcendentals=0))
 
 
 def split(x):
@@ -82,8 +82,10 @@
     dc = (peer & 1) ^ core
     side = jnp.where(peer_z == from_z, 1, 0)
     odd = (dz & 1) == 1
-    part = jnp.where(odd, jnp.where(side == 1 - dc, 1, 2), jnp.where(dz == 0, 0, 3))
-    tile = (column & 31) + 32 * jnp.where(odd, 1 - side, dc)
+    late = odd & (side == dc)
+    far = dz == 2
+    part = jnp.where(far, 2 + dc, jnp.where(late, 1, 0))
+    tile = 1 + (column & 31) + jnp.where(far, 0, 32 * dc) + jnp.where(odd & (side != dc), 64, 0)
     r_i = lax.broadcasted_iota(jnp.int32, (ROWS, ROWS), 0)
     r_j = lax.broadcasted_iota(jnp.int32, (ROWS, ROWS), 1)
     degrees = jnp.broadcast_to(degree, (ROWS, ROWS))
@@ -110,14 +112,13 @@
     place = (jnp.sum(mine * (rank + shift + base + 1.0), axis=0, keepdims=True) - 1.0).astype(jnp.int32)
     slot = lax.broadcasted_iota(jnp.int32, (1, SLOTS), 1)
     values = jnp.where(line == 0, tile, jnp.where(line == 1, slot & 31, jnp.where(
-        line == 2, lax.shift_right_logical(slot, 5), jnp.where(line == 3, row.astype(jnp.int32), 1))))
+        line == 2, lax.shift_right_logical(slot, 5), row.astype(jnp.int32))))
     values = values.astype(F32).astype(BF16)
     for c in range(PARTS * LIST // 256):
         at = lax.broadcasted_iota(jnp.int32, (256, SLOTS), 0) + c * 256
         hot = jnp.where(at == place, 1.0, 0.0).astype(BF16)
         got = lax.dot_general(values, hot, NT, preferred_element_type=F32).astype(jnp.int32)
-        entry = got[0:1] | (got[1:2] << 10) | (got[2:3] << 15) | (got[3:4] << 20)
-        table_ref[0:1, c * 256:(c + 1) * 256] = jnp.where(got[4:5] > 0, entry, PART_TILES)
+        table_ref[0:1, c * 256:(c + 1) * 256] = got[0:1] | (got[1:2] << 10) | (got[2:3] << 15) | (got[3:4] << 20)
     length = jnp.sum(per_row + pad, axis=1, keepdims=True)
     first = lax.broadcasted_iota(jnp.int32, (8, 1), 0)
     for p in range(PARTS):
@@ -131,7 +132,7 @@
         rows, products = [], []
         for u in range(UNROLL):
             first, second = list_ref[0, base + 2 * u], list_ref[0, base + 2 * u + 1]
-            x = [picked_ref[e & 127] for e in (first, second)]
+            x = [picked_ref[e & 255] for e in (first, second)]
             a = [tiles_ref[lax.shift_right_logical(e, 10) & 511] for e in (first, second)]
             rows.append(lax.shift_right_logical(first, 20))
             products.append(lax.dot_general(
@@ -143,10 +144,18 @@
     lax.fori_loop(0, count_ref[part], group, 0)
 
 
-def place_tiles(picked_ref, first_ref, second_ref):
-    picked_ref[0:ROWS] = first_ref[...]
-    picked_ref[ROWS:2 * ROWS] = second_ref[...]
-    picked_ref[PART_TILES] = jnp.zeros((K, TILE), BF16)
+def place_tiles(picked_ref, *blocks):
+    picked_ref[0] = jnp.zeros((K, TILE), BF16)
+    at = 1
+    for block in blocks:
+        picked_ref[at:at + block.shape[0]] = block[...]
+        at += block.shape[0]
+
+
+def tile_copies(tiles_hbm, tiles_ref, sems):
+    n = SLOTS // CHUNKS
+    spans = [slice(c * n, (c + 1) * n) for c in range(CHUNKS)]
+    return [pltpu.make_async_copy(tiles_hbm.at[span], tiles_ref.at[span], sems.at[c]) for c, span in enumerate(spans)]
 
 
 def prepare_kernel(tiles_hbm, column_hbm, degree_hbm, prev_hbm, weight_hbm, coupling_hbm, x_ref,
@@ -155,9 +164,7 @@
     small = [pltpu.make_async_copy(a, b, sems.at[i]) for i, (a, b) in enumerate((
         (column_hbm, column_ref), (degree_hbm, degree_ref), (coupling_hbm, coupling_ref), (weight_hbm, weight_ref),
         (prev_hbm, prev_ref)))]
-    n = SLOTS // CHUNKS
-    large = [pltpu.make_async_copy(tiles_hbm.at[c * n:(c + 1) * n], tiles_ref.at[c * n:(c + 1) * n], tile_sems.at[c])
-             for c in range(CHUNKS)]
+    large = tile_copies(tiles_hbm, tiles_ref, tile_sems)
     for copy in small + large:
         copy.start()
     small[0].wait()
@@ -190,24 +197,14 @@
         copy.wait()
 
 
-def near_kernel(list_ref, count_ref, tiles_ref, half_ref, sib_ref, a_ref, b_ref, w_in_ref, w_ref, picked_ref):
-    w_ref[...] = w_in_ref[...]
-    place_tiles(picked_ref, half_ref, sib_ref)
-    multiply_part(0, list_ref, count_ref, tiles_ref, picked_ref, w_ref)
-    place_tiles(picked_ref, a_ref, b_ref)
-    multiply_part(1, list_ref, count_ref, tiles_ref, picked_ref, w_ref)
-
-
-def middle_kernel(list_ref, count_ref, tiles_ref, a_ref, b_ref, w_in_ref, w_ref, picked_ref):
-    w_ref[...] = w_in_ref[...]
-    place_tiles(picked_ref, a_ref, b_ref)
-    multiply_part(2, list_ref, count_ref, tiles_ref, picked_ref, w_ref)
-
-
-def far_kernel(list_ref, count_ref, tiles_ref, a_ref, b_ref, w_in_ref, zx_ref, g_ref, zw_ref, sums_ref, w_ref,
-               picked_ref):
-    w_ref[...] = w_in_ref[...]
-    place_tiles(picked_ref, a_ref, b_ref)
+def part_kernel(part, list_ref, count_ref, tiles_ref, *refs):
+    *blocks, w_in_ref, w_ref, picked_ref = refs
+    place_tiles(picked_ref, *blocks)
+    multiply_part(part, list_ref, count_ref, tiles_ref, picked_ref, w_ref)
+
+
+def last_kernel(list_ref, count_ref, tiles_ref, block_ref, w_in_ref, zx_ref, g_ref, w_ref, zw_ref, sums_ref, picked_ref):
+    place_tiles(picked_ref, block_ref)
     multiply_part(3, list_ref, count_ref, tiles_ref, picked_ref, w_ref)
     for t in range(ROWS):
         whi, wlo = split(w_ref[t])
@@ -218,10 +215,12 @@
     s = lax.dot_general(zw[:K], zw, NT, preferred_element_type=F32)
     cross = s[:, K:]
     sums_ref[0:K, 0:K] = m[:K, :K] + m[:K, K:] + m[K:, :K]
-    sums_ref[0:K, K:] = s[:, :K] + cross + cross.T
+    row = lax.broadcasted_iota(jnp.int32, (K, K), 0)
+    col = lax.broadcasted_iota(jnp.int32, (K, K), 1)
     g = g_ref[...]
-    sums_ref[K:, 0:K] = g[:K // 2]
-    sums_ref[K:, K:] = g[K // 2:]
+    sums_ref[0:K, K:] = jnp.where(col >= row, s[:, :K] + cross + cross.T, g)
+    sums_ref[K:, 0:K] = jnp.broadcast_to(jnp.sum(jnp.where(col == row, g, 0.0), axis=0, keepdims=True), (8, K))
+    sums_ref[K:, K:] = jnp.zeros((8, K), F32)
 
 
 def eliminate(blocks):
@@ -265,12 +264,15 @@
 def factor_kernel(node_total, sums_ref, rayleigh_ref, r_ref, f_ref, flag_ref):
     inv = 1.0 / node_total
     r = sums_ref[0:K, 0:K] * inv
-    s = sums_ref[0:K, K:] * inv
-    g = jnp.concatenate([sums_ref[K:, 0:K], sums_ref[K:, K:]], axis=0) * inv
+    both = sums_ref[0:K, K:] * inv
+    diagonal = sums_ref[K:K + 1, 0:K] * inv
     row = lax.broadcasted_iota(jnp.int32, (K, K), 0)
     col = lax.broadcasted_iota(jnp.int32, (K, K), 1)
     eye = jnp.where(row == col, 1.0, 0.0)
     rt = r.T
+    flip = both.T
+    s = jnp.where(col >= row, both, flip)
+    g = jnp.where(col < row, both, jnp.where(col > row, flip, diagonal))
     gram = s - dot3(rt, dot3(2.0 * eye - g, r))
     work = jnp.concatenate([gram, eye], axis=1)
     done, pivots = eliminate([work[8 * b:8 * b + 8] for b in range(K // 8)])
@@ -285,18 +287,24 @@
     flag_ref[0] = jnp.where(smallest * WORST >= largest, 0, 1).astype(jnp.int32)
 
 
-def final_kernel(f_ref, zw_ref, zx_ref, out_ref):
+def final_kernel(f_ref, zw_ref, zx_ref, r_ref, out_hbm, r_hbm, out_ref, sems):
+    copies = [pltpu.make_async_copy(r_ref, r_hbm, sems.at[CHUNKS])]
+    copies[0].start()
     f1h, f1l = split(f_ref[:, 0:K])
     f2h, f2l = split(f_ref[:, K:])
     zero = jnp.zeros((K, K), BF16)
     left = jnp.concatenate([jnp.concatenate([f1h, f1h, f2h, f2h], axis=1),
                             jnp.concatenate([f1l, zero, f2l, zero], axis=1)], axis=0)
-    wide = 512
-    for c in range(NODES_DEV // wide):
+    wide = NODES_DEV // CHUNKS
+    for c in range(CHUNKS):
         lanes = slice(c * wide, (c + 1) * wide)
         z = jnp.concatenate([zw_ref[:, lanes], zx_ref[:, lanes]], axis=0)
         y = jnp.dot(left, z, preferred_element_type=F32)
         out_ref[:, lanes] = y[:K] + y[K:]
+        copies.append(pltpu.make_async_copy(out_ref.at[:, lanes], out_hbm.at[:, lanes], sems.at[c]))
+        copies[-1].start()
+    for copy in copies:
+        copy.wait()
 
 
 def exchange(v, axis, to):
@@ -308,8 +316,8 @@
     return exchange(v, "row", lambda i: i ^ 1)
 
 
-def onward(v):
-    return exchange(v, "row", lambda i: (i + (2 if i % 2 == 0 else 6)) % 8)
+def onward(v, way):
+    return exchange(v, "row", lambda i: (i + (2 * way if i % 2 == 0 else -2 * way)) % 8)
 
 
 def total(v):
@@ -324,18 +332,16 @@
     node_total = NODES_DEV * lax.axis_size("row") * lax.axis_size("col")
     after = lax.optimization_barrier
     slab_vmem = pltpu.VMEM(SLAB, F32)
-    picked = pltpu.VMEM((PART_TILES + 1, K, TILE), BF16)
     pair_vmem = pltpu.VMEM((2 * K, NODES_DEV), BF16)
     square = jax.ShapeDtypeStruct((K, K), F32)
 
     half, x = call(
         round_kernel, "round_block", (pltpu.VMEM(SLAB, BF16), pltpu.VMEM((K, NODES_DEV), F32)), [hbm()],
         (vmem(), vmem()), 8, 1, [pltpu.SemaphoreType.DMA((4,))])(in_hbm(block_now.T))
-    a1 = onward(half)
+    a1 = onward(half, 1)
+    a2 = onward(half, -1)
     sib = core_swap(half)
-    sib, x = after((sib, x))
-    a2 = onward(sib)
-    tiles, w1, zx, g, lists, counts = call(
+    tiles, w, zx, g, lists, counts = call(
         prepare_kernel, "prepare",
         (pltpu.VMEM((SLOTS, TILE, TILE), BF16), slab_vmem, pair_vmem, pltpu.VMEM((K, K), F32),
          pltpu.SMEM((1, PARTS * LIST), jnp.int32), pltpu.SMEM((PARTS,), jnp.int32)),
@@ -346,21 +352,27 @@
             in_hbm(tile_blocks), in_hbm(tile_column.reshape(1, SLOTS)), in_hbm(row_degree.reshape(1, ROWS)),
             in_hbm(block_prev.T), in_hbm(node_weight.reshape(1, NODES_DEV)), in_hbm(coupling), x)
 
-    a1, w1 = after((a1, w1))
-    a3 = onward(a1)
-    b1 = core_swap(a1)
-    w2 = call(near_kernel, "near_parts", slab_vmem, [smem(), smem()] + [vmem()] * 6, vmem(), 12, 5, [picked])(
-        lists, counts, tiles, half, sib, a1, b1, w1)
-    a2, w2 = after((a2, w2))
-    b2 = core_swap(a2)
-    w3 = call(middle_kernel, "middle_part", slab_vmem, [smem(), smem()] + [vmem()] * 4, vmem(), 12, 3, [picked])(
-        lists, counts, tiles, a2, b2, w2)
-    a3, w3 = after((a3, w3))
+    def add_part(part, name, blocks, w, us):
+        n = len(blocks)
+        count = sum(block.shape[0] for block in blocks)
+        return call(functools.partial(part_kernel, part), name, slab_vmem, [smem(), smem()] + [vmem()] * (n + 2),
+                    vmem(), 12, us, [pltpu.VMEM((1 + count, K, TILE), BF16)], {3 + n: 0})(
+                        lists, counts, tiles, *blocks, w)
+
+    a1, a2, w = after((a1, a2, w))
+    a3 = onward(a1, 1)
+    h = ROWS // 2
+    b1 = [core_swap(a1[:h]), core_swap(a1[h:])]
+    b2 = [core_swap(a2[:h]), core_swap(a2[h:])]
+    w = add_part(0, "near_parts", [half, sib, a1] + b1, w, 5)
+    w = add_part(1, "late_part", [a2] + b2, w, 3)
+    a3, w = after((a3, w))
     b3 = core_swap(a3)
-    zw, sums = call(
-        far_kernel, "far_part", (pair_vmem, jax.ShapeDtypeStruct((K + K // 2, 2 * K), F32)),
-        [smem(), smem()] + [vmem()] * 6, (vmem(), vmem()), 16, 5, [slab_vmem, picked])(
-            lists, counts, tiles, a3, b3, w3, zx, g)
+    w = add_part(2, "far_part", [a3], w, 2)
+    _, zw, sums = call(
+        last_kernel, "last_part", (slab_vmem, pair_vmem, jax.ShapeDtypeStruct((K + 8, 2 * K), F32)),
+        [smem(), smem()] + [vmem()] * 5, (vmem(), vmem(), vmem()), 16, 4,
+        [pltpu.VMEM((1 + ROWS, K, TILE), BF16)], {4: 0})(lists, counts, tiles, b3, w, zx, g)
 
     sums = total(sums)
     rayleigh, r_factor, f, flag = call(
@@ -369,9 +381,10 @@
         [vmem()], (vmem(), vmem(), vmem(), smem()), 8, 5)(sums)
 
     def plain(zw, zx, f, sums, r_factor):
-        out = call(final_kernel, "scale_block", jax.ShapeDtypeStruct((K, NODES_DEV), F32), [vmem()] * 3, vmem(), 12, 2)(
-            f, zw, zx)
-        return out, r_factor
+        return call(
+            final_kernel, "scale_block", (pltpu.HBM((K, NODES_DEV), F32), pltpu.HBM((K, K), F32)), [vmem()] * 4,
+            (hbm(), hbm()), 12, 2, [pltpu.VMEM((K, NODES_DEV), F32), pltpu.SemaphoreType.DMA((CHUNKS + 1,))])(
+                f, zw, zx, r_factor)
 
     def two_passes(zw, zx, f, sums, r_factor):
         whole = lambda z: z[:K].astype(F32) + z[K:].astype(F32)

time: 74.3 us -> 68.1 us (0.917)
  waiting for transfers between devices: 31.4 us -> 20.9 us
  starting transfers between devices: 16.6 us -> 22.6 us
  Pallas kernels: 23.9 us -> 22.9 us
    ppermute x17 -> x19, waiting for transfers between devices: 31.4 us -> 20.9 us  [exchange(): return lax.ppermute(v, axis, [(i, to(i)) for i in range(n)])]
    ppermute x17 -> x19, starting transfers between devices: 16.6 us -> 22.6 us  [exchange(): return lax.ppermute(v, axis, [(i, to(i)) for i in range(n)])]
    pallas_call x4 -> x5, Pallas kernels: 11.6 us -> 10.9 us  [the longest x3 7.71 us: add_part(): call(functools.partial(part_kernel, part), name, slab_vmem, [smem(), smem...]
  transfers between devices with their start and end apart: 17 -> 19, of which waited for: 13 -> 13; matrix products, arithmetic and copies ran while one was open for 0% -> 0% of each run, Pallas kernels for 19% -> 21%
where the time goes in v3:
time: 68.1 us; the launch traced here: 68.2 us
  Pallas kernels  22.9 us (34%)
  starting transfers between devices  22.6 us (33%)
  waiting for transfers between devices  20.9 us (31%)
  between operations  1.55 us (2%)
    ppermute x19, starting transfers between devices, exchange(): return lax.ppermute(v, axis, [(i, to(i)) for i in range(n)])  22.6 us
    ppermute x19, waiting for transfers between devices, exchange(): return lax.ppermute(v, axis, [(i, to(i)) for i in range(n)])  20.9 us
    pallas_call x3, Pallas kernels, add_part(): call(functools.partial(part_kernel, part), name, slab_vmem, [smem(), smem...  7.71 us
    pallas_call x1, Pallas kernels, local(): call(prepare_kernel, 'prepare', (pltpu.VMEM((SLOTS, TILE, TILE), BF16), s...  6.92 us
    pallas_call x1, Pallas kernels, local(): call(functools.partial(factor_kernel, node_total), 'factor', (square, squ...  3.84 us
    pallas_call x1, Pallas kernels, local(): call(last_kernel, 'last_part', (slab_vmem, pair_vmem, jax.ShapeDtypeStruc...  1.95 us
  transfers between devices with their start and end apart: 19, of which 13 were waited for; matrix products, arithmetic and copies ran while one was open for 0% of the time, Pallas kernels for 21%

profile of v3, /device:TPU:0, one launch (start us, length us, event | category | flops | bytes accessed | tf_op | source)
XLA Modules:
  0.0 68.2 jit_solution(13814502819486145058)
XLA Ops:
  1.9 2.1 %collective-permute-start.10 = (bf16[32,64,128]{2,1,0:T(8,128)(2,1)S(1)}, bf16[32,64,128]{2,1,0:T(8,128)(2,1)S(1)}, u32[]{:S(2)}, u32[]{:S(2)}) collective-permute-start(bf16[32,64,128]{2,1,0:T(8,128)(2,1)S(1)} %get-tuple-element.49.refs_0_), channel_id=1, source_target_pairs={{0,32},{16,112},{32,64},{48,16},{64,96},{80,48},{96,0},{112,80},{1... | collective-permute-start | bytes 1572872 | tf_op jit(solution)/shard_map/ppermute | solution.py:312
  3.9 2.2 %collective-permute-start.11 = (bf16[32,64,128]{2,1,0:T(8,128)(2,1)S(1)}, bf16[32,64,128]{2,1,0:T(8,128)(2,1)S(1)}, u32[]{:S(2)}, u32[]{:S(2)}) collective-permute-start(bf16[32,64,128]{2,1,0:T(8,128)(2,1)S(1)} %get-tuple-element.49.refs_0_), channel_id=1, source_target_pairs={{0,96},{16,48},{32,0},{48,80},{64,32},{80,112},{96,64},{112,16},{1... | collective-permute-start | bytes 1572872 | tf_op jit(solution)/shard_map/ppermute | solution.py:312
  6.2 6.9 %prepare.1 = (bf16[512,128,128]{2,1,0:T(8,128)(2,1)S(1)}, f32[32,64,128]{2,1,0:T(8,128)S(1)}, bf16[128,4096]{1,0:T(8,128)(2,1)S(1)}, f32[64,64]{1,0:T(8,128)S(1)}, s32[1,2304]{1,0:T(1,128)S(4)}, /*index=5*/s32[4]{0:T(128)S(4)}) custom-call(bf16[512,128,128]{2,1,0:T(8,128)(2,1)} %tiles_hbm.1, s32[1,512]{1,0:T(1,128)} %bitcast.24, s32[1,32]{1,0:T(1,128)} %bitcast.25, ...), custom_call_target="tpu_custom_call" | custom-call | flops 700000 | bytes 7000 | tf_op jit(solution)/shard_map/prepare/pallas_call | solution.py:344
  13.1 3.9 %collective-permute-done.10.refs_2_ = bf16[32,64,128]{2,1,0:T(8,128)(2,1)S(1)} collective-permute-done((bf16[32,64,128]{2,1,0:T(8,128)(2,1)S(1)}, bf16[32,64,128]{2,1,0:T(8,128)(2,1)S(1)}, u32[]{:S(2)}, u32[]{:S(2)}) %collective-permute-start.10) | collective-permute-done | bytes 524320 | tf_op jit(solution)/shard_map/ppermute | solution.py:312
  17.8 1.8 %collective-permute-start.16 = (bf16[16,64,128]{2,1,0:T(8,128)(2,1)S(1)}, bf16[16,64,128]{2,1,0:T(8,128)(2,1)S(1)}, u32[]{:S(2)}, u32[]{:S(2)}) collective-permute-start(bf16[16,64,128]{2,1,0:T(8,128)(2,1)S(1)} %get-tuple-element.78), channel_id=1, source_target_pairs={{0,16},{16,0},{32,48},{48,32},{64,80},{80,64},{96,112},{112,96},{1... | collective-permute-start | bytes 786440 | tf_op jit(solution)/shard_map/ppermute | solution.py:312
  21.2 4.2 %near_parts.1.refs_3_ = f32[32,64,128]{2,1,0:T(8,128)S(1)} custom-call(s32[1,2304]{1,0:T(1,128)S(4)} %get-tuple-element.46.list_ref, s32[4]{0:T(128)S(4)} %get-tuple-element.47.count_ref, bf16[512,128,128]{2,1,0:T(8,128)(2,1)S(1)} %get-tuple-element.48.tiles_ref, bf16[32,64,128]{2,1,0:T(8,128)(2,1)S(1)} %get-tuple-element.49.refs_0_, ...), custom_call_target="tpu_custom_call", output_to_operand_aliasing={{}: (8, {})} | custom-call | flops 500000 | bytes 5000 | tf_op jit(solution)/shard_map/near_parts/pallas_call | solution.py:358
  25.4 2.2 %late_part.1.refs_1_ = f32[32,64,128]{2,1,0:T(8,128)S(1)} custom-call(s32[1,2304]{1,0:T(1,128)S(4)} %get-tuple-element.46.list_ref, s32[4]{0:T(128)S(4)} %get-tuple-element.47.count_ref, bf16[512,128,128]{2,1,0:T(8,128)(2,1)S(1)} %get-tuple-element.48.tiles_ref, ...), custom_call_target="tpu_custom_call", output_to_operand_aliasing={{}: (6, {})} | custom-call | flops 300000 | bytes 3000 | tf_op jit(solution)/shard_map/late_part/pallas_call | solution.py:358
  28.1 1.3 %far_part.1.w_in_ref = f32[32,64,128]{2,1,0:T(8,128)S(1)} custom-call(s32[1,2304]{1,0:T(1,128)S(4)} %get-tuple-element.46.list_ref, s32[4]{0:T(128)S(4)} %get-tuple-element.47.count_ref, bf16[512,128,128]{2,1,0:T(8,128)(2,1)S(1)} %get-tuple-element.48.tiles_ref, ...), custom_call_target="tpu_custom_call", output_to_operand_aliasing={{}: (4, {})} | custom-call | flops 200000 | bytes 2000 | tf_op jit(solution)/shard_map/far_part/pallas_call | solution.py:358
  30.0 1.9 %last_part.1 = (f32[32,64,128]{2,1,0:T(8,128)S(1)}, bf16[128,4096]{1,0:T(8,128)(2,1)S(1)}, f32[72,128]{1,0:T(8,128)S(1)}) custom-call(s32[1,2304]{1,0:T(1,128)S(4)} %get-tuple-element.46.list_ref, s32[4]{0:T(128)S(4)} %get-tuple-element.47.count_ref, bf16[512,128,128]{2,1,0:T(8,128)(2,1)S(1)} %get-tuple-element.48.tiles_ref, ...), custom_call_target="tpu_custom_call", output_to_operand_aliasing={{0}: (4, {})} | custom-call | flops 400000 | bytes 4000 | tf_op jit(solution)/shard_map/last_part/pallas_call | solution.py:372
  34.1 2.4 %collective-permute-start.21 = (f32[72,128]{1,0:T(8,128)S(1)}, f32[72,128]{1,0:T(8,128)S(1)}, u32[]{:S(2)}, u32[]{:S(2)}) collective-permute-start(f32[72,128]{1,0:T(8,128)S(1)} %add.78), channel_id=1, source_target_pairs={{0,64},{16,80},{32,96},{48,112},{64,0},{80,16},{96,32},{112,48},{1... | collective-permute-start | bytes 110600 | tf_op jit(solution)/shard_map/ppermute | solution.py:312
  36.5 1.4 %collective-permute-start.22 = (f32[72,128]{1,0:T(8,128)S(1)}, f32[72,128]{1,0:T(8,128)S(1)}, u32[]{:S(2)}, u32[]{:S(2)}) collective-permute-start(f32[72,128]{1,0:T(8,128)S(1)} %add.78), channel_id=1, source_target_pairs={{0,96},{16,112},{32,64},{48,80},{64,32},{80,48},{96,0},{112,16},{1... | collective-permute-start | bytes 110600 | tf_op jit(solution)/shard_map/ppermute | solution.py:312
  37.9 1.6 %collective-permute-done.21 = f32[72,128]{1,0:T(8,128)S(1)} collective-permute-done((f32[72,128]{1,0:T(8,128)S(1)}, f32[72,128]{1,0:T(8,128)S(1)}, u32[]{:S(2)}, u32[]{:S(2)}) %collective-permute-start.21) | collective-permute-done | bytes 36896 | tf_op jit(solution)/shard_map/ppermute | solution.py:312
  39.5 2.1 %collective-permute-done.22 = f32[72,128]{1,0:T(8,128)S(1)} collective-permute-done((f32[72,128]{1,0:T(8,128)S(1)}, f32[72,128]{1,0:T(8,128)S(1)}, u32[]{:S(2)}, u32[]{:S(2)}) %collective-permute-start.22) | collective-permute-done | bytes 36896 | tf_op jit(solution)/shard_map/ppermute | solution.py:312
  41.7 2.0 %collective-permute-start.23 = (f32[72,128]{1,0:T(8,128)S(1)}, f32[72,128]{1,0:T(8,128)S(1)}, u32[]{:S(2)}, u32[]{:S(2)}) collective-permute-start(f32[72,128]{1,0:T(8,128)S(1)} %add_add_fusion.4), channel_id=1, source_target_pairs={{0,1},{1,0},{2,3},{3,2},{4,5},{5,4},{6,7},{7,6},{8,9},{9,8},{10,11... | collective-permute-start | bytes 110600 | tf_op jit(solution)/shard_map/ppermute | solution.py:312
  43.6 3.4 %collective-permute-start.24 = (f32[72,128]{1,0:T(8,128)S(1)}, f32[72,128]{1,0:T(8,128)S(1)}, u32[]{:S(2)}, u32[]{:S(2)}) collective-permute-start(f32[72,128]{1,0:T(8,128)S(1)} %add_add_fusion.4), channel_id=1, source_target_pairs={{0,2},{1,3},{2,0},{3,1},{4,6},{5,7},{6,4},{7,5},{8,10},{9,11},{10,... | collective-permute-start | bytes 110600 | tf_op jit(solution)/shard_map/ppermute | solution.py:312
  47.1 2.4 %collective-permute-done.24 = f32[72,128]{1,0:T(8,128)S(1)} collective-permute-done((f32[72,128]{1,0:T(8,128)S(1)}, f32[72,128]{1,0:T(8,128)S(1)}, u32[]{:S(2)}, u32[]{:S(2)}) %collective-permute-start.24) | collective-permute-done | bytes 36896 | tf_op jit(solution)/shard_map/ppermute | solution.py:312
  49.5 2.7 %collective-permute-done.25 = f32[72,128]{1,0:T(8,128)S(1)} collective-permute-done((f32[72,128]{1,0:T(8,128)S(1)}, f32[72,128]{1,0:T(8,128)S(1)}, u32[]{:S(2)}, u32[]{:S(2)}) %collective-permute-start.25) | collective-permute-done | bytes 36896 | tf_op jit(solution)/shard_map/ppermute | solution.py:312
  52.3 1.6 %collective-permute-start.26 = (f32[72,128]{1,0:T(8,128)S(1)}, f32[72,128]{1,0:T(8,128)S(1)}, u32[]{:S(2)}, u32[]{:S(2)}) collective-permute-start(f32[72,128]{1,0:T(8,128)S(1)} %add_add_fusion.3), channel_id=1, source_target_pairs={{0,4},{1,5},{2,6},{3,7},{4,0},{5,1},{6,2},{7,3},{8,12},{9,13},{10,... | collective-permute-start | bytes 110600 | tf_op jit(solution)/shard_map/ppermute | solution.py:312
  53.8 3.0 %collective-permute-start.27 = (f32[72,128]{1,0:T(8,128)S(1)}, f32[72,128]{1,0:T(8,128)S(1)}, u32[]{:S(2)}, u32[]{:S(2)}) collective-permute-start(f32[72,128]{1,0:T(8,128)S(1)} %add_add_fusion.3), channel_id=1, source_target_pairs={{0,8},{1,9},{2,10},{3,11},{4,12},{5,13},{6,14},{7,15},{8,0},{9,1},... | collective-permute-start | bytes 110600 | tf_op jit(solution)/shard_map/ppermute | solution.py:312
  57.3 1.9 %collective-permute-done.27 = f32[72,128]{1,0:T(8,128)S(1)} collective-permute-done((f32[72,128]{1,0:T(8,128)S(1)}, f32[72,128]{1,0:T(8,128)S(1)}, u32[]{:S(2)}, u32[]{:S(2)}) %collective-permute-start.27) | collective-permute-done | bytes 36896 | tf_op jit(solution)/shard_map/ppermute | solution.py:312
  59.3 2.7 %collective-permute-done.28 = f32[72,128]{1,0:T(8,128)S(1)} collective-permute-done((f32[72,128]{1,0:T(8,128)S(1)}, f32[72,128]{1,0:T(8,128)S(1)}, u32[]{:S(2)}, u32[]{:S(2)}) %collective-permute-start.28) | collective-permute-done | bytes 36896 | tf_op jit(solution)/shard_map/ppermute | solution.py:312
  62.1 3.8 %factor.1 = (f32[64,64]{1,0:T(8,128)}, f32[64,64]{1,0:T(8,128)S(1)}, f32[64,128]{1,0:T(8,128)S(1)}, s32[1]{0:T(128)}) custom-call(f32[72,128]{1,0:T(8,128)S(1)} %add_add_fusion.2.sums_ref), custom_call_target="tpu_custom_call" | custom-call | flops 500000 | bytes 5000 | tf_op jit(solution)/shard_map/factor/pallas_call | solution.py:378
  66.5 1.5 %conditional.1 = ((f32[64,4096]{1,0:T(8,128)}, f32[64,64]{1,0:T(8,128)})) conditional(s32[]{:T(128)} %bitcast.9, (bf16[128,4096]{1,0:T(8,128)(2,1)S(1)}, f32[72,128]{1,0:T(8,128)S(1)}, bf16[128,4096]{1,0:T(8,128)(2,1)S(1)}) %tuple.19, (f32[64,128]{1,0:T(8,128)S(1)}, bf16[128,4096]{1,0:T(8,128)(2,1)S(1)}, bf16[128,4096]{1,0:T(8,128)(2,1)S(1)}, ...), branch_computations={%region_0.0_spmd, %region_3.4_spmd} | conditional | flops 605900864 | bytes 7562154 | solution.py:397
  66.8 1.3 %scale_block.1 = (f32[64,4096]{1,0:T(8,128)}, f32[64,64]{1,0:T(8,128)}) custom-call(f32[64,128]{1,0:T(8,128)S(1)} %get-tuple-element.17.f_ref, bf16[128,4096]{1,0:T(8,128)(2,1)S(1)} %get-tuple-element.18.zw_ref, bf16[128,4096]{1,0:T(8,128)(2,1)S(1)} %get-tuple-element.19.zx_ref, f32[64,64]{1,0:T(8,128)S(1)} %get-tuple-element.20.r_ref), custom_call_target="tpu_custom_call" | custom-call | flops 200000 | bytes 2000 | tf_op jit(solution)/shard_map/cond/branch_1_fun/scale_block/pallas_call | solution.py:384
  (29 shorter events, 7.3 us)
Async XLA Ops:
  1.9 15.1 %collective-permute-start.10 = (bf16[32,64,128]{2,1,0:T(8,128)(2,1)S(1)}, bf16[32,64,128]{2,1,0:T(8,128)(2,1)S(1)}, u32[]{:S(2)}, u32[]{:S(2)}) collective-permute-start(bf16[32,64,128]{2,1,0:T(8,128)(2,1)S(1)} %get-tuple-element.49.refs_0_), channel_id=1, source_target_pairs={{0,32},{16,112},{32,64},{48,16},{64,96},{80,48},{96,0},{112,80},{1... | collective-permute-start | bytes 1572872 | tf_op jit(solution)/shard_map/ppermute | solution.py:312
  3.9 13.3 %collective-permute-start.11 = (bf16[32,64,128]{2,1,0:T(8,128)(2,1)S(1)}, bf16[32,64,128]{2,1,0:T(8,128)(2,1)S(1)}, u32[]{:S(2)}, u32[]{:S(2)}) collective-permute-start(bf16[32,64,128]{2,1,0:T(8,128)(2,1)S(1)} %get-tuple-element.49.refs_0_), channel_id=1, source_target_pairs={{0,96},{16,48},{32,0},{48,80},{64,32},{80,112},{96,64},{112,16},{1... | collective-permute-start | bytes 1572872 | tf_op jit(solution)/shard_map/ppermute | solution.py:312
  6.1 14.1 %collective-permute-start.15 = (bf16[32,64,128]{2,1,0:T(8,128)(2,1)S(1)}, bf16[32,64,128]{2,1,0:T(8,128)(2,1)S(1)}, u32[]{:S(2)}, u32[]{:S(2)}) collective-permute-start(bf16[32,64,128]{2,1,0:T(8,128)(2,1)S(1)} %get-tuple-element.49.refs_0_), channel_id=1, source_target_pairs={{0,16},{16,0},{32,48},{48,32},{64,80},{80,64},{96,112},{112,96},{1... | collective-permute-start | bytes 1572872 | tf_op jit(solution)/shard_map/ppermute | solution.py:312
  17.2 10.8 %collective-permute-start.12 = (bf16[32,64,128]{2,1,0:T(8,128)(2,1)S(1)}, bf16[32,64,128]{2,1,0:T(8,128)(2,1)S(1)}, u32[]{:S(2)}, u32[]{:S(2)}) collective-permute-start(bf16[32,64,128]{2,1,0:T(8,128)(2,1)S(1)} %collective-permute-done.10.refs_2_), channel_id=1, source_target_pairs={{0,32},{16,112},{32,64},{48,16},{64,96},{80,48},{96,0},{112,80},{1... | collective-permute-start | bytes 1572872 | tf_op jit(solution)/shard_map/ppermute | solution.py:312
  17.8 3.0 %collective-permute-start.16 = (bf16[16,64,128]{2,1,0:T(8,128)(2,1)S(1)}, bf16[16,64,128]{2,1,0:T(8,128)(2,1)S(1)}, u32[]{:S(2)}, u32[]{:S(2)}) collective-permute-start(bf16[16,64,128]{2,1,0:T(8,128)(2,1)S(1)} %get-tuple-element.78), channel_id=1, source_target_pairs={{0,16},{16,0},{32,48},{48,32},{64,80},{80,64},{96,112},{112,96},{1... | collective-permute-start | bytes 786440 | tf_op jit(solution)/shard_map/ppermute | solution.py:312
  19.7 1.5 %collective-permute-start.17 = (bf16[16,64,128]{2,1,0:T(8,128)(2,1)S(1)}, bf16[16,64,128]{2,1,0:T(8,128)(2,1)S(1)}, u32[]{:S(2)}, u32[]{:S(2)}) collective-permute-start(bf16[16,64,128]{2,1,0:T(8,128)(2,1)S(1)} %get-tuple-element.77), channel_id=1, source_target_pairs={{0,16},{16,0},{32,48},{48,32},{64,80},{80,64},{96,112},{112,96},{1... | collective-permute-start | bytes 786440 | tf_op jit(solution)/shard_map/ppermute | solution.py:312
  19.8 5.6 %collective-permute-start.13 = (bf16[16,64,128]{2,1,0:T(8,128)(2,1)S(1)}, bf16[16,64,128]{2,1,0:T(8,128)(2,1)S(1)}, u32[]{:S(2)}, u32[]{:S(2)}) collective-permute-start(bf16[16,64,128]{2,1,0:T(8,128)(2,1)S(1)} %get-tuple-element.80), channel_id=1, source_target_pairs={{0,16},{16,0},{32,48},{48,32},{64,80},{80,64},{96,112},{112,96},{1... | collective-permute-start | bytes 786440 | tf_op jit(solution)/shard_map/ppermute | solution.py:312
  20.3 5.1 %collective-permute-start.14 = (bf16[16,64,128]{2,1,0:T(8,128)(2,1)S(1)}, bf16[16,64,128]{2,1,0:T(8,128)(2,1)S(1)}, u32[]{:S(2)}, u32[]{:S(2)}) collective-permute-start(bf16[16,64,128]{2,1,0:T(8,128)(2,1)S(1)} %get-tuple-element.79), channel_id=1, source_target_pairs={{0,16},{16,0},{32,48},{48,32},{64,80},{80,64},{96,112},{112,96},{1... | collective-permute-start | bytes 786440 | tf_op jit(solution)/shard_map/ppermute | solution.py:312
  28.1 1.9 %collective-permute-start.18 = (bf16[32,64,128]{2,1,0:T(8,128)(2,1)S(1)}, bf16[32,64,128]{2,1,0:T(8,128)(2,1)S(1)}, u32[]{:S(2)}, u32[]{:S(2)}) collective-permute-start(bf16[32,64,128]{2,1,0:T(8,128)(2,1)S(1)} %collective-permute-done.12.refs_0_), channel_id=1, source_target_pairs={{0,16},{16,0},{32,48},{48,32},{64,80},{80,64},{96,112},{112,96},{1... | collective-permute-start | bytes 1572872 | tf_op jit(solution)/shard_map/ppermute | solution.py:312
  32.0 1.3 %collective-permute-start.19 = (f32[72,128]{1,0:T(8,128)S(1)}, f32[72,128]{1,0:T(8,128)S(1)}, u32[]{:S(2)}, u32[]{:S(2)}) collective-permute-start(f32[72,128]{1,0:T(8,128)S(1)} %get-tuple-element.58), channel_id=1, source_target_pairs={{0,16},{16,0},{32,48},{48,32},{64,80},{80,64},{96,112},{112,96},{1... | collective-permute-start | bytes 110600 | tf_op jit(solution)/shard_map/ppermute | solution.py:312
  33.2 4.7 %collective-permute-start.20 = (f32[72,128]{1,0:T(8,128)S(1)}, f32[72,128]{1,0:T(8,128)S(1)}, u32[]{:S(2)}, u32[]{:S(2)}) collective-permute-start(f32[72,128]{1,0:T(8,128)S(1)} %add.78), channel_id=1, source_target_pairs={{0,32},{16,48},{32,0},{48,16},{64,96},{80,112},{96,64},{112,80},{1... | collective-permute-start | bytes 110600 | tf_op jit(solution)/shard_map/ppermute | solution.py:312
  34.1 5.5 %collective-permute-start.21 = (f32[72,128]{1,0:T(8,128)S(1)}, f32[72,128]{1,0:T(8,128)S(1)}, u32[]{:S(2)}, u32[]{:S(2)}) collective-permute-start(f32[72,128]{1,0:T(8,128)S(1)} %add.78), channel_id=1, source_target_pairs={{0,64},{16,80},{32,96},{48,112},{64,0},{80,16},{96,32},{112,48},{1... | collective-permute-start | bytes 110600 | tf_op jit(solution)/shard_map/ppermute | solution.py:312
  36.5 5.2 %collective-permute-start.22 = (f32[72,128]{1,0:T(8,128)S(1)}, f32[72,128]{1,0:T(8,128)S(1)}, u32[]{:S(2)}, u32[]{:S(2)}) collective-permute-start(f32[72,128]{1,0:T(8,128)S(1)} %add.78), channel_id=1, source_target_pairs={{0,96},{16,112},{32,64},{48,80},{64,32},{80,48},{96,0},{112,16},{1... | collective-permute-start | bytes 110600 | tf_op jit(solution)/shard_map/ppermute | solution.py:312
  41.7 5.4 %collective-permute-start.23 = (f32[72,128]{1,0:T(8,128)S(1)}, f32[72,128]{1,0:T(8,128)S(1)}, u32[]{:S(2)}, u32[]{:S(2)}) collective-permute-start(f32[72,128]{1,0:T(8,128)S(1)} %add_add_fusion.4), channel_id=1, source_target_pairs={{0,1},{1,0},{2,3},{3,2},{4,5},{5,4},{6,7},{7,6},{8,9},{9,8},{10,11... | collective-permute-start | bytes 110600 | tf_op jit(solution)/shard_map/ppermute | solution.py:312
  43.6 5.9 %collective-permute-start.24 = (f32[72,128]{1,0:T(8,128)S(1)}, f32[72,128]{1,0:T(8,128)S(1)}, u32[]{:S(2)}, u32[]{:S(2)}) collective-permute-start(f32[72,128]{1,0:T(8,128)S(1)} %add_add_fusion.4), channel_id=1, source_target_pairs={{0,2},{1,3},{2,0},{3,1},{4,6},{5,7},{6,4},{7,5},{8,10},{9,11},{10,... | collective-permute-start | bytes 110600 | tf_op jit(solution)/shard_map/ppermute | solution.py:312
  47.1 5.2 %collective-permute-start.25 = (f32[72,128]{1,0:T(8,128)S(1)}, f32[72,128]{1,0:T(8,128)S(1)}, u32[]{:S(2)}, u32[]{:S(2)}) collective-permute-start(f32[72,128]{1,0:T(8,128)S(1)} %add_add_fusion.4), channel_id=1, source_target_pairs={{0,3},{1,2},{2,1},{3,0},{4,7},{5,6},{6,5},{7,4},{8,11},{9,10},{10,... | collective-permute-start | bytes 110600 | tf_op jit(solution)/shard_map/ppermute | solution.py:312
  52.3 5.1 %collective-permute-start.26 = (f32[72,128]{1,0:T(8,128)S(1)}, f32[72,128]{1,0:T(8,128)S(1)}, u32[]{:S(2)}, u32[]{:S(2)}) collective-permute-start(f32[72,128]{1,0:T(8,128)S(1)} %add_add_fusion.3), channel_id=1, source_target_pairs={{0,4},{1,5},{2,6},{3,7},{4,0},{5,1},{6,2},{7,3},{8,12},{9,13},{10,... | collective-permute-start | bytes 110600 | tf_op jit(solution)/shard_map/ppermute | solution.py:312
  53.8 5.5 %collective-permute-start.27 = (f32[72,128]{1,0:T(8,128)S(1)}, f32[72,128]{1,0:T(8,128)S(1)}, u32[]{:S(2)}, u32[]{:S(2)}) collective-permute-start(f32[72,128]{1,0:T(8,128)S(1)} %add_add_fusion.3), channel_id=1, source_target_pairs={{0,8},{1,9},{2,10},{3,11},{4,12},{5,13},{6,14},{7,15},{8,0},{9,1},... | collective-permute-start | bytes 110600 | tf_op jit(solution)/shard_map/ppermute | solution.py:312
  56.9 5.2 %collective-permute-start.28 = (f32[72,128]{1,0:T(8,128)S(1)}, f32[72,128]{1,0:T(8,128)S(1)}, u32[]{:S(2)}, u32[]{:S(2)}) collective-permute-start(f32[72,128]{1,0:T(8,128)S(1)} %add_add_fusion.3), channel_id=1, source_target_pairs={{0,12},{1,13},{2,14},{3,15},{4,8},{5,9},{6,10},{7,11},{8,4},{9,5},... | collective-permute-start | bytes 110600 | tf_op jit(solution)/shard_map/ppermute | solution.py:312

commit v4 on v3

--- a/solution.py
+++ b/solution.py
@@ -12,8 +12,9 @@
 SLOTS = 512
 NODES_DEV = ROWS * TILE
 UNROLL = 8
-LIST = 576
-PARTS = 4
+LIST = 614
+PARTS = 5
+TABLE = 3072
 CHUNKS = 8
 WORST = 32.0
 F32 = jnp.float32
@@ -44,7 +45,7 @@
         kernel, out_shape=out_shape, in_specs=in_specs, out_specs=out_specs, scratch_shapes=list(scratch), name=name,
         input_output_aliases=aliases or {},
         compiler_params=pltpu.CompilerParams(vmem_limit_bytes=mib << 20),
-        cost_estimate=pl.CostEstimate(flops=int(us * 1e5), bytes_accessed=int(us * 1e3), transcendentals=0))
+        cost_estimate=pl.CostEstimate(flops=int(us * 1e9), bytes_accessed=int(us * 3e6), transcendentals=0))
 
 
 def split(x):
@@ -82,10 +83,9 @@
     dc = (peer & 1) ^ core
     side = jnp.where(peer_z == from_z, 1, 0)
     odd = (dz & 1) == 1
-    late = odd & (side == dc)
-    far = dz == 2
-    part = jnp.where(far, 2 + dc, jnp.where(late, 1, 0))
-    tile = 1 + (column & 31) + jnp.where(far, 0, 32 * dc) + jnp.where(odd & (side != dc), 64, 0)
+    part = jnp.where(odd, 1 + dc, jnp.where(dz == 0, 0, 3 + dc))
+    offset = jnp.where(odd, jnp.where(side == dc, 32, 0), jnp.where(dz == 0, 32 * dc, 0))
+    tile = 1 + (column & 31) + offset
     r_i = lax.broadcasted_iota(jnp.int32, (ROWS, ROWS), 0)
     r_j = lax.broadcasted_iota(jnp.int32, (ROWS, ROWS), 1)
     degrees = jnp.broadcast_to(degree, (ROWS, ROWS))
@@ -114,7 +114,7 @@
     values = jnp.where(line == 0, tile, jnp.where(line == 1, slot & 31, jnp.where(
         line == 2, lax.shift_right_logical(slot, 5), row.astype(jnp.int32))))
     values = values.astype(F32).astype(BF16)
-    for c in range(PARTS * LIST // 256):
+    for c in range(TABLE // 256):
         at = lax.broadcasted_iota(jnp.int32, (256, SLOTS), 0) + c * 256
         hot = jnp.where(at == place, 1.0, 0.0).astype(BF16)
         got = lax.dot_general(values, hot, NT, preferred_element_type=F32).astype(jnp.int32)
@@ -159,8 +159,9 @@
 
 
 def prepare_kernel(tiles_hbm, column_hbm, degree_hbm, prev_hbm, weight_hbm, coupling_hbm, x_ref,
-                   tiles_ref, w_ref, zx_ref, g_ref, list_ref, count_ref,
-                   column_ref, degree_ref, prev_ref, weight_ref, coupling_ref, table_ref, sems, tile_sems):
+                   half_ref, sib_ref, tiles_ref, w_ref, zx_ref, g_ref, list_ref, count_ref,
+                   column_ref, degree_ref, prev_ref, weight_ref, coupling_ref, table_ref, picked_ref, sems,
+                   tile_sems):
     small = [pltpu.make_async_copy(a, b, sems.at[i]) for i, (a, b) in enumerate((
         (column_hbm, column_ref), (degree_hbm, degree_ref), (coupling_hbm, coupling_ref), (weight_hbm, weight_ref),
         (prev_hbm, prev_ref)))]
@@ -192,9 +193,11 @@
     gg = lax.dot_general(zx[:K], zx, NT, preferred_element_type=F32)
     cross = gg[:, K:]
     g_ref[...] = gg[:, :K] + cross + cross.T
+    place_tiles(picked_ref, half_ref, sib_ref)
     table.wait()
     for copy in large:
         copy.wait()
+    multiply_part(0, list_ref, count_ref, tiles_ref, picked_ref, w_ref)
 
 
 def part_kernel(part, list_ref, count_ref, tiles_ref, *refs):
@@ -205,7 +208,7 @@
 
 def last_kernel(list_ref, count_ref, tiles_ref, block_ref, w_in_ref, zx_ref, g_ref, w_ref, zw_ref, sums_ref, picked_ref):
     place_tiles(picked_ref, block_ref)
-    multiply_part(3, list_ref, count_ref, tiles_ref, picked_ref, w_ref)
+    multiply_part(4, list_ref, count_ref, tiles_ref, picked_ref, w_ref)
     for t in range(ROWS):
         whi, wlo = split(w_ref[t])
         zw_ref[0:K, t * TILE:(t + 1) * TILE] = whi
@@ -344,13 +347,13 @@
     tiles, w, zx, g, lists, counts = call(
         prepare_kernel, "prepare",
         (pltpu.VMEM((SLOTS, TILE, TILE), BF16), slab_vmem, pair_vmem, pltpu.VMEM((K, K), F32),
-         pltpu.SMEM((1, PARTS * LIST), jnp.int32), pltpu.SMEM((PARTS,), jnp.int32)),
-        [hbm()] * 6 + [vmem()], (vmem(), vmem(), vmem(), vmem(), smem(), smem()), 16, 7,
+         pltpu.SMEM((1, TABLE), jnp.int32), pltpu.SMEM((PARTS,), jnp.int32)),
+        [hbm()] * 6 + [vmem()] * 3, (vmem(), vmem(), vmem(), vmem(), smem(), smem()), 16, 9,
         [pltpu.VMEM((1, SLOTS), jnp.int32), pltpu.VMEM((1, ROWS), jnp.int32), pltpu.VMEM((K, NODES_DEV), F32),
-         pltpu.VMEM((1, NODES_DEV), F32), pltpu.VMEM((K, K), F32), pltpu.VMEM((1, PARTS * LIST), jnp.int32),
-         pltpu.SemaphoreType.DMA((6,)), pltpu.SemaphoreType.DMA((CHUNKS,))])(
+         pltpu.VMEM((1, NODES_DEV), F32), pltpu.VMEM((K, K), F32), pltpu.VMEM((1, TABLE), jnp.int32),
+         pltpu.VMEM((1 + 2 * ROWS, K, TILE), BF16), pltpu.SemaphoreType.DMA((6,)), pltpu.SemaphoreType.DMA((CHUNKS,))])(
             in_hbm(tile_blocks), in_hbm(tile_column.reshape(1, SLOTS)), in_hbm(row_degree.reshape(1, ROWS)),
-            in_hbm(block_prev.T), in_hbm(node_weight.reshape(1, NODES_DEV)), in_hbm(coupling), x)
+            in_hbm(block_prev.T), in_hbm(node_weight.reshape(1, NODES_DEV)), in_hbm(coupling), x, half, sib)
 
     def add_part(part, name, blocks, w, us):
         n = len(blocks)
@@ -361,14 +364,13 @@
 
     a1, a2, w = after((a1, a2, w))
     a3 = onward(a1, 1)
-    h = ROWS // 2
-    b1 = [core_swap(a1[:h]), core_swap(a1[h:])]
-    b2 = [core_swap(a2[:h]), core_swap(a2[h:])]
-    w = add_part(0, "near_parts", [half, sib, a1] + b1, w, 5)
-    w = add_part(1, "late_part", [a2] + b2, w, 3)
+    b1 = core_swap(a1)
+    b2 = core_swap(a2)
+    w = add_part(1, "near_part", [a1, a2], w, 8)
+    w = add_part(2, "near_swapped", [b1, b2], w, 0)
     a3, w = after((a3, w))
     b3 = core_swap(a3)
-    w = add_part(2, "far_part", [a3], w, 2)
+    w = add_part(3, "far_part", [a3], w, 2)
     _, zw, sums = call(
         last_kernel, "last_part", (slab_vmem, pair_vmem, jax.ShapeDtypeStruct((K + 8, 2 * K), F32)),
         [smem(), smem()] + [vmem()] * 5, (vmem(), vmem(), vmem()), 16, 4,

time: 68.1 us -> 68.4 us (level)
  Pallas kernels: 22.9 us -> 26.9 us
  waiting for transfers between devices: 20.9 us -> 16.9 us
    ppermute x19 -> x17, waiting for transfers between devices: 20.9 us -> 16.9 us  [exchange(): return lax.ppermute(v, axis, [(i, to(i)) for i in range(n)])]
    pallas_call x1, Pallas kernels: 6.92 us -> 10 us  [local(): call(prepare_kernel, 'prepare', (pltpu.VMEM((SLOTS, TILE, TILE), BF16), s...]
    ppermute x19 -> x17, starting transfers between devices: 22.6 us -> 22.6 us  [exchange(): return lax.ppermute(v, axis, [(i, to(i)) for i in range(n)])]
  transfers between devices with their start and end apart: 19 -> 17, of which waited for: 13 -> 10; matrix products, arithmetic and copies ran while one was open for 0% -> 0% of each run, Pallas kernels for 21% -> 26%
where the time goes in v4:
time: 68.4 us; the launch traced here: 68.2 us
  Pallas kernels  26.9 us (39%)
  starting transfers between devices  22.6 us (33%)
  waiting for transfers between devices  16.9 us (25%)
  between operations  1.57 us (2%)
    ppermute x17, starting transfers between devices, exchange(): return lax.ppermute(v, axis, [(i, to(i)) for i in range(n)])  22.6 us
    ppermute x17, waiting for transfers between devices, exchange(): return lax.ppermute(v, axis, [(i, to(i)) for i in range(n)])  16.9 us
    pallas_call x1, Pallas kernels, local(): call(prepare_kernel, 'prepare', (pltpu.VMEM((SLOTS, TILE, TILE), BF16), s...  10 us
    pallas_call x3, Pallas kernels, add_part(): call(functools.partial(part_kernel, part), name, slab_vmem, [smem(), smem...  7.95 us
    pallas_call x1, Pallas kernels, local(): call(functools.partial(factor_kernel, node_total), 'factor', (square, squ...  3.84 us
    pallas_call x1, Pallas kernels, local(): call(last_kernel, 'last_part', (slab_vmem, pair_vmem, jax.ShapeDtypeStruc...  2.58 us
  transfers between devices with their start and end apart: 17, of which 10 were waited for; matrix products, arithmetic and copies ran while one was open for 0% of the time, Pallas kernels for 26%

profile of v4, /device:TPU:0, one launch (start us, length us, event | category | flops | bytes accessed | tf_op | source)
XLA Modules:
  0.0 68.2 jit_solution(10316798572677846684)
XLA Ops:
  0.6 1.2 %round_block.1 = (bf16[32,64,128]{2,1,0:T(8,128)(2,1)S(1)}, f32[64,4096]{1,0:T(8,128)S(1)}) custom-call(f32[64,4096]{1,0:T(8,128)} %bitcast.21), custom_call_target="tpu_custom_call" | custom-call | flops 1000000000 | bytes 3000000 | tf_op jit(solution)/shard_map/round_block/pallas_call | solution.py:341
  2.0 2.1 %collective-permute-start.11 = (bf16[32,64,128]{2,1,0:T(8,128)(2,1)S(1)}, bf16[32,64,128]{2,1,0:T(8,128)(2,1)S(1)}, u32[]{:S(2)}, u32[]{:S(2)}) collective-permute-start(bf16[32,64,128]{2,1,0:T(8,128)(2,1)S(1)} %get-tuple-element.46.half_ref), channel_id=1, source_target_pairs={{0,32},{16,112},{32,64},{48,16},{64,96},{80,48},{96,0},{112,80},{1... | collective-permute-start | bytes 1572872 | tf_op jit(solution)/shard_map/ppermute | solution.py:315
  4.0 2.2 %collective-permute-start.12 = (bf16[32,64,128]{2,1,0:T(8,128)(2,1)S(1)}, bf16[32,64,128]{2,1,0:T(8,128)(2,1)S(1)}, u32[]{:S(2)}, u32[]{:S(2)}) collective-permute-start(bf16[32,64,128]{2,1,0:T(8,128)(2,1)S(1)} %get-tuple-element.46.half_ref), channel_id=1, source_target_pairs={{0,96},{16,48},{32,0},{48,80},{64,32},{80,112},{96,64},{112,16},{1... | collective-permute-start | bytes 1572872 | tf_op jit(solution)/shard_map/ppermute | solution.py:315
  6.2 10.0 %prepare.1 = (bf16[512,128,128]{2,1,0:T(8,128)(2,1)S(1)}, f32[32,64,128]{2,1,0:T(8,128)S(1)}, bf16[128,4096]{1,0:T(8,128)(2,1)S(1)}, f32[64,64]{1,0:T(8,128)S(1)}, s32[1,3072]{1,0:T(1,128)S(4)}, /*index=5*/s32[5]{0:T(128)S(4)}) custom-call(bf16[512,128,128]{2,1,0:T(8,128)(2,1)} %tiles_hbm.1, s32[1,512]{1,0:T(1,128)} %bitcast.24, s32[1,32]{1,0:T(1,128)} %bitcast.25, ...), custom_call_target="tpu_custom_call" | custom-call | flops 8999999488 | bytes 27000000 | tf_op jit(solution)/shard_map/prepare/pallas_call | solution.py:347
  16.5 1.5 %collective-permute-done.12.refs_1_ = bf16[32,64,128]{2,1,0:T(8,128)(2,1)S(1)} collective-permute-done((bf16[32,64,128]{2,1,0:T(8,128)(2,1)S(1)}, bf16[32,64,128]{2,1,0:T(8,128)(2,1)S(1)}, u32[]{:S(2)}, u32[]{:S(2)}) %collective-permute-start.12) | collective-permute-done | bytes 524320 | tf_op jit(solution)/shard_map/ppermute | solution.py:315
  18.8 3.1 %collective-permute-start.15 = (bf16[32,64,128]{2,1,0:T(8,128)(2,1)S(1)}, bf16[32,64,128]{2,1,0:T(8,128)(2,1)S(1)}, u32[]{:S(2)}, u32[]{:S(2)}) collective-permute-start(bf16[32,64,128]{2,1,0:T(8,128)(2,1)S(1)} %collective-permute-done.12.refs_1_), channel_id=1, source_target_pairs={{0,16},{16,0},{32,48},{48,32},{64,80},{80,64},{96,112},{112,96},{1... | collective-permute-start | bytes 1572872 | tf_op jit(solution)/shard_map/ppermute | solution.py:315
  21.9 3.2 %near_part.1.refs_2_ = f32[32,64,128]{2,1,0:T(8,128)S(1)} custom-call(s32[1,3072]{1,0:T(1,128)S(4)} %get-tuple-element.47.list_ref, s32[5]{0:T(128)S(4)} %get-tuple-element.48.count_ref, bf16[512,128,128]{2,1,0:T(8,128)(2,1)S(1)} %get-tuple-element.49.tiles_ref, ...), custom_call_target="tpu_custom_call", output_to_operand_aliasing={{}: (5, {})} | custom-call | flops 8000000000 | bytes 24000000 | tf_op jit(solution)/shard_map/near_part/pallas_call | solution.py:361
  25.1 2.9 %near_swapped.1.refs_1_ = f32[32,64,128]{2,1,0:T(8,128)S(1)} custom-call(s32[1,3072]{1,0:T(1,128)S(4)} %get-tuple-element.47.list_ref, s32[5]{0:T(128)S(4)} %get-tuple-element.48.count_ref, bf16[512,128,128]{2,1,0:T(8,128)(2,1)S(1)} %get-tuple-element.49.tiles_ref, ...), custom_call_target="tpu_custom_call", output_to_operand_aliasing={{}: (5, {})} | custom-call | tf_op jit(solution)/shard_map/near_swapped/pallas_call | solution.py:361
  27.9 1.2 %collective-permute-done.13.refs_0_ = bf16[32,64,128]{2,1,0:T(8,128)(2,1)S(1)} collective-permute-done((bf16[32,64,128]{2,1,0:T(8,128)(2,1)S(1)}, bf16[32,64,128]{2,1,0:T(8,128)(2,1)S(1)}, u32[]{:S(2)}, u32[]{:S(2)}) %collective-permute-start.13) | collective-permute-done | bytes 524320 | tf_op jit(solution)/shard_map/ppermute | solution.py:315
  29.2 1.9 %far_part.1.w_in_ref = f32[32,64,128]{2,1,0:T(8,128)S(1)} custom-call(s32[1,3072]{1,0:T(1,128)S(4)} %get-tuple-element.47.list_ref, s32[5]{0:T(128)S(4)} %get-tuple-element.48.count_ref, bf16[512,128,128]{2,1,0:T(8,128)(2,1)S(1)} %get-tuple-element.49.tiles_ref, ...), custom_call_target="tpu_custom_call", output_to_operand_aliasing={{}: (4, {})} | custom-call | flops 2000000000 | bytes 6000000 | tf_op jit(solution)/shard_map/far_part/pallas_call | solution.py:361
  31.1 2.6 %last_part.1 = (f32[32,64,128]{2,1,0:T(8,128)S(1)}, bf16[128,4096]{1,0:T(8,128)(2,1)S(1)}, f32[72,128]{1,0:T(8,128)S(1)}) custom-call(s32[1,3072]{1,0:T(1,128)S(4)} %get-tuple-element.47.list_ref, s32[5]{0:T(128)S(4)} %get-tuple-element.48.count_ref, bf16[512,128,128]{2,1,0:T(8,128)(2,1)S(1)} %get-tuple-element.49.tiles_ref, ...), custom_call_target="tpu_custom_call", output_to_operand_aliasing={{0}: (4, {})} | custom-call | flops 4000000000 | bytes 12000000 | tf_op jit(solution)/shard_map/last_part/pallas_call | solution.py:374
  34.9 3.0 %collective-permute-start.19 = (f32[72,128]{1,0:T(8,128)S(1)}, f32[72,128]{1,0:T(8,128)S(1)}, u32[]{:S(2)}, u32[]{:S(2)}) collective-permute-start(f32[72,128]{1,0:T(8,128)S(1)} %add.78), channel_id=1, source_target_pairs={{0,64},{16,80},{32,96},{48,112},{64,0},{80,16},{96,32},{112,48},{1... | collective-permute-start | bytes 110600 | tf_op jit(solution)/shard_map/ppermute | solution.py:315
  37.9 1.7 %collective-permute-start.20 = (f32[72,128]{1,0:T(8,128)S(1)}, f32[72,128]{1,0:T(8,128)S(1)}, u32[]{:S(2)}, u32[]{:S(2)}) collective-permute-start(f32[72,128]{1,0:T(8,128)S(1)} %add.78), channel_id=1, source_target_pairs={{0,96},{16,112},{32,64},{48,80},{64,32},{80,48},{96,0},{112,16},{1... | collective-permute-start | bytes 110600 | tf_op jit(solution)/shard_map/ppermute | solution.py:315
  40.5 2.6 %collective-permute-done.20 = f32[72,128]{1,0:T(8,128)S(1)} collective-permute-done((f32[72,128]{1,0:T(8,128)S(1)}, f32[72,128]{1,0:T(8,128)S(1)}, u32[]{:S(2)}, u32[]{:S(2)}) %collective-permute-start.20) | collective-permute-done | bytes 36896 | tf_op jit(solution)/shard_map/ppermute | solution.py:315
  44.1 3.5 %collective-permute-start.22 = (f32[72,128]{1,0:T(8,128)S(1)}, f32[72,128]{1,0:T(8,128)S(1)}, u32[]{:S(2)}, u32[]{:S(2)}) collective-permute-start(f32[72,128]{1,0:T(8,128)S(1)} %add_add_fusion.4), channel_id=1, source_target_pairs={{0,2},{1,3},{2,0},{3,1},{4,6},{5,7},{6,4},{7,5},{8,10},{9,11},{10,... | collective-permute-start | bytes 110600 | tf_op jit(solution)/shard_map/ppermute | solution.py:315
  47.9 2.2 %collective-permute-done.22 = f32[72,128]{1,0:T(8,128)S(1)} collective-permute-done((f32[72,128]{1,0:T(8,128)S(1)}, f32[72,128]{1,0:T(8,128)S(1)}, u32[]{:S(2)}, u32[]{:S(2)}) %collective-permute-start.22) | collective-permute-done | bytes 36896 | tf_op jit(solution)/shard_map/ppermute | solution.py:315
  50.1 2.7 %collective-permute-done.23 = f32[72,128]{1,0:T(8,128)S(1)} collective-permute-done((f32[72,128]{1,0:T(8,128)S(1)}, f32[72,128]{1,0:T(8,128)S(1)}, u32[]{:S(2)}, u32[]{:S(2)}) %collective-permute-start.23) | collective-permute-done | bytes 36896 | tf_op jit(solution)/shard_map/ppermute | solution.py:315
  52.9 1.6 %collective-permute-start.24 = (f32[72,128]{1,0:T(8,128)S(1)}, f32[72,128]{1,0:T(8,128)S(1)}, u32[]{:S(2)}, u32[]{:S(2)}) collective-permute-start(f32[72,128]{1,0:T(8,128)S(1)} %add_add_fusion.3), channel_id=1, source_target_pairs={{0,4},{1,5},{2,6},{3,7},{4,0},{5,1},{6,2},{7,3},{8,12},{9,13},{10,... | collective-permute-start | bytes 110600 | tf_op jit(solution)/shard_map/ppermute | solution.py:315
  54.4 2.4 %collective-permute-start.25 = (f32[72,128]{1,0:T(8,128)S(1)}, f32[72,128]{1,0:T(8,128)S(1)}, u32[]{:S(2)}, u32[]{:S(2)}) collective-permute-start(f32[72,128]{1,0:T(8,128)S(1)} %add_add_fusion.3), channel_id=1, source_target_pairs={{0,8},{1,9},{2,10},{3,11},{4,12},{5,13},{6,14},{7,15},{8,0},{9,1},... | collective-permute-start | bytes 110600 | tf_op jit(solution)/shard_map/ppermute | solution.py:315
  57.6 2.2 %collective-permute-done.25 = f32[72,128]{1,0:T(8,128)S(1)} collective-permute-done((f32[72,128]{1,0:T(8,128)S(1)}, f32[72,128]{1,0:T(8,128)S(1)}, u32[]{:S(2)}, u32[]{:S(2)}) %collective-permute-start.25) | collective-permute-done | bytes 36896 | tf_op jit(solution)/shard_map/ppermute | solution.py:315
  59.9 2.1 %collective-permute-done.26 = f32[72,128]{1,0:T(8,128)S(1)} collective-permute-done((f32[72,128]{1,0:T(8,128)S(1)}, f32[72,128]{1,0:T(8,128)S(1)}, u32[]{:S(2)}, u32[]{:S(2)}) %collective-permute-start.26) | collective-permute-done | bytes 36896 | tf_op jit(solution)/shard_map/ppermute | solution.py:315
  62.0 3.8 %factor.1 = (f32[64,64]{1,0:T(8,128)}, f32[64,64]{1,0:T(8,128)S(1)}, f32[64,128]{1,0:T(8,128)S(1)}, s32[1]{0:T(128)}) custom-call(f32[72,128]{1,0:T(8,128)S(1)} %add_add_fusion.2.sums_ref), custom_call_target="tpu_custom_call" | custom-call | flops 5000000000 | bytes 15000000 | tf_op jit(solution)/shard_map/factor/pallas_call | solution.py:380
  66.5 1.5 %conditional.1 = ((f32[64,4096]{1,0:T(8,128)}, f32[64,64]{1,0:T(8,128)})) conditional(s32[]{:T(128)} %bitcast.9, (bf16[128,4096]{1,0:T(8,128)(2,1)S(1)}, f32[72,128]{1,0:T(8,128)S(1)}, bf16[128,4096]{1,0:T(8,128)(2,1)S(1)}) %tuple.19, (f32[64,128]{1,0:T(8,128)S(1)}, bf16[128,4096]{1,0:T(8,128)(2,1)S(1)}, bf16[128,4096]{1,0:T(8,128)(2,1)S(1)}, ...), branch_computations={%region_0.0_spmd, %region_3.4_spmd} | conditional | flops 2000000000 | bytes 7562154 | solution.py:399
  66.8 1.3 %scale_block.1 = (f32[64,4096]{1,0:T(8,128)}, f32[64,64]{1,0:T(8,128)}) custom-call(f32[64,128]{1,0:T(8,128)S(1)} %get-tuple-element.17.f_ref, bf16[128,4096]{1,0:T(8,128)(2,1)S(1)} %get-tuple-element.18.zw_ref, bf16[128,4096]{1,0:T(8,128)(2,1)S(1)} %get-tuple-element.19.zx_ref, f32[64,64]{1,0:T(8,128)S(1)} %get-tuple-element.20.r_ref), custom_call_target="tpu_custom_call" | custom-call | flops 2000000000 | bytes 6000000 | tf_op jit(solution)/shard_map/cond/branch_1_fun/scale_block/pallas_call | solution.py:386
  (23 shorter events, 5.3 us)
Async XLA Ops:
  1.9 4.4 %collective-permute-start.10 = (bf16[32,64,128]{2,1,0:T(8,128)(2,1)S(1)}, bf16[32,64,128]{2,1,0:T(8,128)(2,1)S(1)}, u32[]{:S(2)}, u32[]{:S(2)}) collective-permute-start(bf16[32,64,128]{2,1,0:T(8,128)(2,1)S(1)} %get-tuple-element.46.half_ref), channel_id=1, source_target_pairs={{0,16},{16,0},{32,48},{48,32},{64,80},{80,64},{96,112},{112,96},{1... | collective-permute-start | bytes 1572872 | tf_op jit(solution)/shard_map/ppermute | solution.py:315
  2.0 14.5 %collective-permute-start.11 = (bf16[32,64,128]{2,1,0:T(8,128)(2,1)S(1)}, bf16[32,64,128]{2,1,0:T(8,128)(2,1)S(1)}, u32[]{:S(2)}, u32[]{:S(2)}) collective-permute-start(bf16[32,64,128]{2,1,0:T(8,128)(2,1)S(1)} %get-tuple-element.46.half_ref), channel_id=1, source_target_pairs={{0,32},{16,112},{32,64},{48,16},{64,96},{80,48},{96,0},{112,80},{1... | collective-permute-start | bytes 1572872 | tf_op jit(solution)/shard_map/ppermute | solution.py:315
  4.0 13.9 %collective-permute-start.12 = (bf16[32,64,128]{2,1,0:T(8,128)(2,1)S(1)}, bf16[32,64,128]{2,1,0:T(8,128)(2,1)S(1)}, u32[]{:S(2)}, u32[]{:S(2)}) collective-permute-start(bf16[32,64,128]{2,1,0:T(8,128)(2,1)S(1)} %get-tuple-element.46.half_ref), channel_id=1, source_target_pairs={{0,96},{16,48},{32,0},{48,80},{64,32},{80,112},{96,64},{112,16},{1... | collective-permute-start | bytes 1572872 | tf_op jit(solution)/shard_map/ppermute | solution.py:315
  17.9 7.1 %collective-permute-start.14 = (bf16[32,64,128]{2,1,0:T(8,128)(2,1)S(1)}, bf16[32,64,128]{2,1,0:T(8,128)(2,1)S(1)}, u32[]{:S(2)}, u32[]{:S(2)}) collective-permute-start(bf16[32,64,128]{2,1,0:T(8,128)(2,1)S(1)} %collective-permute-done.11.refs_0_), channel_id=1, source_target_pairs={{0,16},{16,0},{32,48},{48,32},{64,80},{80,64},{96,112},{112,96},{1... | collective-permute-start | bytes 1572872 | tf_op jit(solution)/shard_map/ppermute | solution.py:315
  18.8 10.4 %collective-permute-start.13 = (bf16[32,64,128]{2,1,0:T(8,128)(2,1)S(1)}, bf16[32,64,128]{2,1,0:T(8,128)(2,1)S(1)}, u32[]{:S(2)}, u32[]{:S(2)}) collective-permute-start(bf16[32,64,128]{2,1,0:T(8,128)(2,1)S(1)} %collective-permute-done.11.refs_0_), channel_id=1, source_target_pairs={{0,32},{16,112},{32,64},{48,16},{64,96},{80,48},{96,0},{112,80},{1... | collective-permute-start | bytes 1572872 | tf_op jit(solution)/shard_map/ppermute | solution.py:315
  18.8 6.3 %collective-permute-start.15 = (bf16[32,64,128]{2,1,0:T(8,128)(2,1)S(1)}, bf16[32,64,128]{2,1,0:T(8,128)(2,1)S(1)}, u32[]{:S(2)}, u32[]{:S(2)}) collective-permute-start(bf16[32,64,128]{2,1,0:T(8,128)(2,1)S(1)} %collective-permute-done.12.refs_1_), channel_id=1, source_target_pairs={{0,16},{16,0},{32,48},{48,32},{64,80},{80,64},{96,112},{112,96},{1... | collective-permute-start | bytes 1572872 | tf_op jit(solution)/shard_map/ppermute | solution.py:315
  29.2 1.9 %collective-permute-start.16 = (bf16[32,64,128]{2,1,0:T(8,128)(2,1)S(1)}, bf16[32,64,128]{2,1,0:T(8,128)(2,1)S(1)}, u32[]{:S(2)}, u32[]{:S(2)}) collective-permute-start(bf16[32,64,128]{2,1,0:T(8,128)(2,1)S(1)} %collective-permute-done.13.refs_0_), channel_id=1, source_target_pairs={{0,16},{16,0},{32,48},{48,32},{64,80},{80,64},{96,112},{112,96},{1... | collective-permute-start | bytes 1572872 | tf_op jit(solution)/shard_map/ppermute | solution.py:315
  33.6 1.3 %collective-permute-start.17 = (f32[72,128]{1,0:T(8,128)S(1)}, f32[72,128]{1,0:T(8,128)S(1)}, u32[]{:S(2)}, u32[]{:S(2)}) collective-permute-start(f32[72,128]{1,0:T(8,128)S(1)} %get-tuple-element.58), channel_id=1, source_target_pairs={{0,16},{16,0},{32,48},{48,32},{64,80},{80,64},{96,112},{112,96},{1... | collective-permute-start | bytes 110600 | tf_op jit(solution)/shard_map/ppermute | solution.py:315
  34.9 4.7 %collective-permute-start.18 = (f32[72,128]{1,0:T(8,128)S(1)}, f32[72,128]{1,0:T(8,128)S(1)}, u32[]{:S(2)}, u32[]{:S(2)}) collective-permute-start(f32[72,128]{1,0:T(8,128)S(1)} %add.78), channel_id=1, source_target_pairs={{0,32},{16,48},{32,0},{48,16},{64,96},{80,112},{96,64},{112,80},{1... | collective-permute-start | bytes 110600 | tf_op jit(solution)/shard_map/ppermute | solution.py:315
  34.9 5.5 %collective-permute-start.19 = (f32[72,128]{1,0:T(8,128)S(1)}, f32[72,128]{1,0:T(8,128)S(1)}, u32[]{:S(2)}, u32[]{:S(2)}) collective-permute-start(f32[72,128]{1,0:T(8,128)S(1)} %add.78), channel_id=1, source_target_pairs={{0,64},{16,80},{32,96},{48,112},{64,0},{80,16},{96,32},{112,48},{1... | collective-permute-start | bytes 110600 | tf_op jit(solution)/shard_map/ppermute | solution.py:315
  37.9 5.2 %collective-permute-start.20 = (f32[72,128]{1,0:T(8,128)S(1)}, f32[72,128]{1,0:T(8,128)S(1)}, u32[]{:S(2)}, u32[]{:S(2)}) collective-permute-start(f32[72,128]{1,0:T(8,128)S(1)} %add.78), channel_id=1, source_target_pairs={{0,96},{16,112},{32,64},{48,80},{64,32},{80,48},{96,0},{112,16},{1... | collective-permute-start | bytes 110600 | tf_op jit(solution)/shard_map/ppermute | solution.py:315
  43.1 4.8 %collective-permute-start.21 = (f32[72,128]{1,0:T(8,128)S(1)}, f32[72,128]{1,0:T(8,128)S(1)}, u32[]{:S(2)}, u32[]{:S(2)}) collective-permute-start(f32[72,128]{1,0:T(8,128)S(1)} %add_add_fusion.4), channel_id=1, source_target_pairs={{0,1},{1,0},{2,3},{3,2},{4,5},{5,4},{6,7},{7,6},{8,9},{9,8},{10,11... | collective-permute-start | bytes 110600 | tf_op jit(solution)/shard_map/ppermute | solution.py:315
  44.1 6.0 %collective-permute-start.22 = (f32[72,128]{1,0:T(8,128)S(1)}, f32[72,128]{1,0:T(8,128)S(1)}, u32[]{:S(2)}, u32[]{:S(2)}) collective-permute-start(f32[72,128]{1,0:T(8,128)S(1)} %add_add_fusion.4), channel_id=1, source_target_pairs={{0,2},{1,3},{2,0},{3,1},{4,6},{5,7},{6,4},{7,5},{8,10},{9,11},{10,... | collective-permute-start | bytes 110600 | tf_op jit(solution)/shard_map/ppermute | solution.py:315
  47.7 5.2 %collective-permute-start.23 = (f32[72,128]{1,0:T(8,128)S(1)}, f32[72,128]{1,0:T(8,128)S(1)}, u32[]{:S(2)}, u32[]{:S(2)}) collective-permute-start(f32[72,128]{1,0:T(8,128)S(1)} %add_add_fusion.4), channel_id=1, source_target_pairs={{0,3},{1,2},{2,1},{3,0},{4,7},{5,6},{6,5},{7,4},{8,11},{9,10},{10,... | collective-permute-start | bytes 110600 | tf_op jit(solution)/shard_map/ppermute | solution.py:315
  52.9 4.8 %collective-permute-start.24 = (f32[72,128]{1,0:T(8,128)S(1)}, f32[72,128]{1,0:T(8,128)S(1)}, u32[]{:S(2)}, u32[]{:S(2)}) collective-permute-start(f32[72,128]{1,0:T(8,128)S(1)} %add_add_fusion.3), channel_id=1, source_target_pairs={{0,4},{1,5},{2,6},{3,7},{4,0},{5,1},{6,2},{7,3},{8,12},{9,13},{10,... | collective-permute-start | bytes 110600 | tf_op jit(solution)/shard_map/ppermute | solution.py:315
  54.4 5.5 %collective-permute-start.25 = (f32[72,128]{1,0:T(8,128)S(1)}, f32[72,128]{1,0:T(8,128)S(1)}, u32[]{:S(2)}, u32[]{:S(2)}) collective-permute-start(f32[72,128]{1,0:T(8,128)S(1)} %add_add_fusion.3), channel_id=1, source_target_pairs={{0,8},{1,9},{2,10},{3,11},{4,12},{5,13},{6,14},{7,15},{8,0},{9,1},... | collective-permute-start | bytes 110600 | tf_op jit(solution)/shard_map/ppermute | solution.py:315
  56.8 5.2 %collective-permute-start.26 = (f32[72,128]{1,0:T(8,128)S(1)}, f32[72,128]{1,0:T(8,128)S(1)}, u32[]{:S(2)}, u32[]{:S(2)}) collective-permute-start(f32[72,128]{1,0:T(8,128)S(1)} %add_add_fusion.3), channel_id=1, source_target_pairs={{0,12},{1,13},{2,14},{3,15},{4,8},{5,9},{6,10},{7,11},{8,4},{9,5},... | collective-permute-start | bytes 110600 | tf_op jit(solution)/shard_map/ppermute | solution.py:315

commit v5 on v4

--- a/solution.py
+++ b/solution.py
@@ -11,7 +11,7 @@
 ROWS = 32
 SLOTS = 512
 NODES_DEV = ROWS * TILE
-UNROLL = 8
+UNROLL = 16
 LIST = 614
 PARTS = 5
 TABLE = 3072
@@ -22,6 +22,7 @@
 NT = (((1,), (1,)), ((), ()))
 HIGHEST = lax.Precision.HIGHEST
 SLAB = (ROWS, K, TILE)
+NODE_ROWS = (ROWS, TILE, K)
 
 
 def vmem():
@@ -83,8 +84,8 @@
     dc = (peer & 1) ^ core
     side = jnp.where(peer_z == from_z, 1, 0)
     odd = (dz & 1) == 1
-    part = jnp.where(odd, 1 + dc, jnp.where(dz == 0, 0, 3 + dc))
-    offset = jnp.where(odd, jnp.where(side == dc, 32, 0), jnp.where(dz == 0, 32 * dc, 0))
+    part = jnp.where(odd, 1 + dc, jnp.where(dz == 0, dc, 3 + dc))
+    offset = jnp.where(odd, jnp.where(side == dc, 32, 0), jnp.where(dz == 0, 64 * dc, 0))
     tile = 1 + (column & 31) + offset
     r_i = lax.broadcasted_iota(jnp.int32, (ROWS, ROWS), 0)
     r_j = lax.broadcasted_iota(jnp.int32, (ROWS, ROWS), 1)
@@ -136,7 +137,7 @@
             a = [tiles_ref[lax.shift_right_logical(e, 10) & 511] for e in (first, second)]
             rows.append(lax.shift_right_logical(first, 20))
             products.append(lax.dot_general(
-                jnp.concatenate(x, axis=1), jnp.concatenate(a, axis=1), NT, preferred_element_type=F32))
+                jnp.concatenate(a, axis=1), jnp.concatenate(x, axis=1), NT, preferred_element_type=F32))
         for row, product in zip(rows, products):
             w_ref[row] += product
         return carry
@@ -159,7 +160,7 @@
 
 
 def prepare_kernel(tiles_hbm, column_hbm, degree_hbm, prev_hbm, weight_hbm, coupling_hbm, x_ref,
-                   half_ref, sib_ref, tiles_ref, w_ref, zx_ref, g_ref, list_ref, count_ref,
+                   half_ref, tiles_ref, w_ref, zx_ref, g_ref, list_ref, count_ref,
                    column_ref, degree_ref, prev_ref, weight_ref, coupling_ref, table_ref, picked_ref, sems,
                    tile_sems):
     small = [pltpu.make_async_copy(a, b, sems.at[i]) for i, (a, b) in enumerate((
@@ -188,12 +189,12 @@
         coupled = jnp.dot(left, jnp.concatenate([phi, plo, phi], axis=0), preferred_element_type=F32)
         w = x * weight_ref[:, lanes] - coupled
         for t in range(wide // TILE):
-            w_ref[c * (wide // TILE) + t] = w[:, t * TILE:(t + 1) * TILE]
+            w_ref[c * (wide // TILE) + t] = w[:, t * TILE:(t + 1) * TILE].T
     zx = zx_ref[...]
     gg = lax.dot_general(zx[:K], zx, NT, preferred_element_type=F32)
     cross = gg[:, K:]
     g_ref[...] = gg[:, :K] + cross + cross.T
-    place_tiles(picked_ref, half_ref, sib_ref)
+    place_tiles(picked_ref, half_ref)
     table.wait()
     for copy in large:
         copy.wait()
@@ -206,16 +207,17 @@
     multiply_part(part, list_ref, count_ref, tiles_ref, picked_ref, w_ref)
 
 
-def last_kernel(list_ref, count_ref, tiles_ref, block_ref, w_in_ref, zx_ref, g_ref, w_ref, zw_ref, sums_ref, picked_ref):
-    place_tiles(picked_ref, block_ref)
+def last_kernel(list_ref, count_ref, tiles_ref, first_ref, second_ref, w_in_ref, zx_ref, g_ref, w_ref, zw_ref, sums_ref, picked_ref,
+                whi_ref):
+    place_tiles(picked_ref, first_ref, second_ref)
     multiply_part(4, list_ref, count_ref, tiles_ref, picked_ref, w_ref)
     for t in range(ROWS):
         whi, wlo = split(w_ref[t])
-        zw_ref[0:K, t * TILE:(t + 1) * TILE] = whi
-        zw_ref[K:2 * K, t * TILE:(t + 1) * TILE] = wlo
+        zw_ref[t * TILE:(t + 1) * TILE, :] = jnp.concatenate([whi, wlo], axis=1)
+        whi_ref[:, t * TILE:(t + 1) * TILE] = whi.T
     zw = zw_ref[...]
-    m = lax.dot_general(zx_ref[...], zw, NT, preferred_element_type=F32)
-    s = lax.dot_general(zw[:K], zw, NT, preferred_element_type=F32)
+    m = jnp.dot(zx_ref[...], zw, preferred_element_type=F32)
+    s = jnp.dot(whi_ref[...], zw, preferred_element_type=F32)
     cross = s[:, K:]
     sums_ref[0:K, 0:K] = m[:K, :K] + m[:K, K:] + m[K:, :K]
     row = lax.broadcasted_iota(jnp.int32, (K, K), 0)
@@ -296,13 +298,13 @@
     f1h, f1l = split(f_ref[:, 0:K])
     f2h, f2l = split(f_ref[:, K:])
     zero = jnp.zeros((K, K), BF16)
-    left = jnp.concatenate([jnp.concatenate([f1h, f1h, f2h, f2h], axis=1),
-                            jnp.concatenate([f1l, zero, f2l, zero], axis=1)], axis=0)
+    left = [jnp.concatenate([jnp.concatenate([hi, hi], axis=1), jnp.concatenate([lo, zero], axis=1)], axis=0)
+            for hi, lo in ((f1h, f1l), (f2h, f2l))]
     wide = NODES_DEV // CHUNKS
     for c in range(CHUNKS):
         lanes = slice(c * wide, (c + 1) * wide)
-        z = jnp.concatenate([zw_ref[:, lanes], zx_ref[:, lanes]], axis=0)
-        y = jnp.dot(left, z, preferred_element_type=F32)
+        y = (lax.dot_general(left[0], zw_ref[lanes, :], NT, preferred_element_type=F32)
+             + jnp.dot(left[1], zx_ref[:, lanes], preferred_element_type=F32))
         out_ref[:, lanes] = y[:K] + y[K:]
         copies.append(pltpu.make_async_copy(out_ref.at[:, lanes], out_hbm.at[:, lanes], sems.at[c]))
         copies[-1].start()
@@ -325,17 +327,18 @@
 
 def total(v):
     v = v + core_swap(v)
-    for axis, unit in (("row", 2), ("col", 1), ("col", 4)):
-        others = [exchange(v, axis, lambda i, d=d * unit: i ^ d) for d in (1, 2, 3)]
-        v = (v + others[0]) + (others[1] + others[2])
+    for axis, unit in (("row", 2), ("col", 4), ("col", 1)):
+        others = {d: exchange(v, axis, lambda i, d=d * unit: i ^ d) for d in (1, 2, 3)}
+        v = (v + others[2]) + (others[3] + others[1])
     return v
 
 
 def local(tile_blocks, tile_column, row_degree, node_weight, block_now, block_prev, coupling):
     node_total = NODES_DEV * lax.axis_size("row") * lax.axis_size("col")
     after = lax.optimization_barrier
-    slab_vmem = pltpu.VMEM(SLAB, F32)
+    w_vmem = pltpu.VMEM(NODE_ROWS, F32)
     pair_vmem = pltpu.VMEM((2 * K, NODES_DEV), BF16)
+    picked = lambda n: pltpu.VMEM((1 + n * ROWS, K, TILE), BF16)
     square = jax.ShapeDtypeStruct((K, K), F32)
 
     half, x = call(
@@ -343,43 +346,47 @@
         (vmem(), vmem()), 8, 1, [pltpu.SemaphoreType.DMA((4,))])(in_hbm(block_now.T))
     a1 = onward(half, 1)
     a2 = onward(half, -1)
-    sib = core_swap(half)
     tiles, w, zx, g, lists, counts = call(
         prepare_kernel, "prepare",
-        (pltpu.VMEM((SLOTS, TILE, TILE), BF16), slab_vmem, pair_vmem, pltpu.VMEM((K, K), F32),
+        (pltpu.VMEM((SLOTS, TILE, TILE), BF16), w_vmem, pair_vmem, pltpu.VMEM((K, K), F32),
          pltpu.SMEM((1, TABLE), jnp.int32), pltpu.SMEM((PARTS,), jnp.int32)),
-        [hbm()] * 6 + [vmem()] * 3, (vmem(), vmem(), vmem(), vmem(), smem(), smem()), 16, 9,
+        [hbm()] * 6 + [vmem()] * 2, (vmem(), vmem(), vmem(), vmem(), smem(), smem()), 16, 9,
         [pltpu.VMEM((1, SLOTS), jnp.int32), pltpu.VMEM((1, ROWS), jnp.int32), pltpu.VMEM((K, NODES_DEV), F32),
          pltpu.VMEM((1, NODES_DEV), F32), pltpu.VMEM((K, K), F32), pltpu.VMEM((1, TABLE), jnp.int32),
-         pltpu.VMEM((1 + 2 * ROWS, K, TILE), BF16), pltpu.SemaphoreType.DMA((6,)), pltpu.SemaphoreType.DMA((CHUNKS,))])(
+         picked(1), pltpu.SemaphoreType.DMA((6,)), pltpu.SemaphoreType.DMA((CHUNKS,))])(
             in_hbm(tile_blocks), in_hbm(tile_column.reshape(1, SLOTS)), in_hbm(row_degree.reshape(1, ROWS)),
-            in_hbm(block_prev.T), in_hbm(node_weight.reshape(1, NODES_DEV)), in_hbm(coupling), x, half, sib)
+            in_hbm(block_prev.T), in_hbm(node_weight.reshape(1, NODES_DEV)), in_hbm(coupling), x, half)
 
     def add_part(part, name, blocks, w, us):
         n = len(blocks)
-        count = sum(block.shape[0] for block in blocks)
-        return call(functools.partial(part_kernel, part), name, slab_vmem, [smem(), smem()] + [vmem()] * (n + 2),
-                    vmem(), 12, us, [pltpu.VMEM((1 + count, K, TILE), BF16)], {3 + n: 0})(
+        slabs = sum(block.shape[0] for block in blocks) // ROWS
+        return call(functools.partial(part_kernel, part), name, w_vmem, [smem(), smem()] + [vmem()] * (n + 2),
+                    vmem(), 12, us, [picked(slabs)], {3 + n: 0})(
                         lists, counts, tiles, *blocks, w)
 
-    a1, a2, w = after((a1, a2, w))
-    a3 = onward(a1, 1)
+    a1, w = after((a1, w))
+    h = ROWS // 2
+    f1 = onward(a1[:h], 1)
+    f2 = onward(a2[h:], -1)
+    half, w = after((half, w))
+    sib = core_swap(half)
     b1 = core_swap(a1)
     b2 = core_swap(a2)
-    w = add_part(1, "near_part", [a1, a2], w, 8)
+    w = add_part(1, "near_part", [a1, a2, sib], w, 8)
     w = add_part(2, "near_swapped", [b1, b2], w, 0)
-    a3, w = after((a3, w))
-    b3 = core_swap(a3)
-    w = add_part(3, "far_part", [a3], w, 2)
+    f1, f2, w = after((f1, f2, w))
+    s1 = core_swap(f1)
+    s2 = core_swap(f2)
+    w = add_part(3, "far_part", [f1, f2], w, 2)
     _, zw, sums = call(
-        last_kernel, "last_part", (slab_vmem, pair_vmem, jax.ShapeDtypeStruct((K + 8, 2 * K), F32)),
-        [smem(), smem()] + [vmem()] * 5, (vmem(), vmem(), vmem()), 16, 4,
-        [pltpu.VMEM((1 + ROWS, K, TILE), BF16)], {4: 0})(lists, counts, tiles, b3, w, zx, g)
+        last_kernel, "last_part", (w_vmem, pltpu.VMEM((NODES_DEV, 2 * K), BF16), jax.ShapeDtypeStruct((K + 8, 2 * K), F32)),
+        [smem(), smem()] + [vmem()] * 6, (vmem(), vmem(), vmem()), 16, 4,
+        [picked(1), pltpu.VMEM((K, NODES_DEV), BF16)], {5: 0})(lists, counts, tiles, s1, s2, w, zx, g)
 
     sums = total(sums)
     rayleigh, r_factor, f, flag = call(
         functools.partial(factor_kernel, node_total), "factor",
-        (square, square, jax.ShapeDtypeStruct((K, 2 * K), F32), jax.ShapeDtypeStruct((1,), jnp.int32)),
+        (square, square, jax.ShapeDtypeStruct((K, 2 * K), F32), pltpu.SMEM((1,), jnp.int32)),
         [vmem()], (vmem(), vmem(), vmem(), smem()), 8, 5)(sums)
 
     def plain(zw, zx, f, sums, r_factor):
@@ -390,6 +397,7 @@
 
     def two_passes(zw, zx, f, sums, r_factor):
         whole = lambda z: z[:K].astype(F32) + z[K:].astype(F32)
+        zw = zw.T
         rayleigh_t = sums[:K, :K].T / node_total
         w_next = whole(zw) - jnp.dot(rayleigh_t, whole(zx), precision=HIGHEST)
         gram = total(jnp.dot(w_next, w_next.T, precision=HIGHEST)) / node_total

time: 68.4 us -> 61.5 us (0.90)
  Pallas kernels: 26.9 us -> 21.3 us
  between operations: 1.57 us -> 0.88 us
    pallas_call x5, Pallas kernels: 20.6 us -> 14.8 us  [the longest x1 7.81 us: local(): call(prepare_kernel, 'prepare', (pltpu.VMEM((SLOTS, TILE, TILE), BF16), w...]
    ppermute x17 -> x19, waiting for transfers between devices: 16.9 us -> 16.7 us  [exchange(): return lax.ppermute(v, axis, [(i, to(i)) for i in range(n)])]
    ppermute x17 -> x19, starting transfers between devices: 22.6 us -> 22.6 us  [exchange(): return lax.ppermute(v, axis, [(i, to(i)) for i in range(n)])]
  transfers between devices with their start and end apart: 17 -> 19, of which waited for: 10 -> 12; matrix products, arithmetic and copies ran while one was open for 0% -> 0% of each run, Pallas kernels for 26% -> 21%
where the time goes in v5:
time: 61.5 us
  starting transfers between devices  22.6 us (37%)
  Pallas kernels  21.3 us (35%)
  waiting for transfers between devices  16.7 us (27%)
  between operations  0.88 us (1%)
    ppermute x19, starting transfers between devices, exchange(): return lax.ppermute(v, axis, [(i, to(i)) for i in range(n)])  22.6 us
    ppermute x19, waiting for transfers between devices, exchange(): return lax.ppermute(v, axis, [(i, to(i)) for i in range(n)])  16.7 us
    pallas_call x1, Pallas kernels, local(): call(prepare_kernel, 'prepare', (pltpu.VMEM((SLOTS, TILE, TILE), BF16), w...  7.81 us
    pallas_call x3, Pallas kernels, add_part(): call(functools.partial(part_kernel, part), name, w_vmem, [smem(), smem()]...  4.94 us
    pallas_call x1, Pallas kernels, local(): call(functools.partial(factor_kernel, node_total), 'factor', (square, squ...  3.82 us
    pallas_call x1, Pallas kernels, local(): call(last_kernel, 'last_part', (w_vmem, pltpu.VMEM((NODES_DEV, 2 * K), BF...  2 us
    pallas_call x1, Pallas kernels, plain(): call(final_kernel, 'scale_block', (pltpu.HBM((K, NODES_DEV), F32), pltpu....  1.47 us
    pallas_call x1, Pallas kernels, local(): call(round_kernel, 'round_block', (pltpu.VMEM(SLAB, BF16), pltpu.VMEM((K,...  1.24 us
  transfers between devices with their start and end apart: 19, of which 12 were waited for; matrix products, arithmetic and copies ran while one was open for 0% of the time, Pallas kernels for 21%

profile of v5, /device:TPU:0, one launch (start us, length us, event | category | flops | bytes accessed | tf_op | source)
XLA Modules:
  0.0 61.5 jit_solution(17707285169565203918)
XLA Ops:
  0.6 1.2 %round_block.1 = (bf16[32,64,128]{2,1,0:T(8,128)(2,1)S(1)}, f32[64,4096]{1,0:T(8,128)S(1)}) custom-call(f32[64,4096]{1,0:T(8,128)} %bitcast.23), custom_call_target="tpu_custom_call" | custom-call | flops 1000000000 | bytes 3000000 | tf_op jit(solution)/shard_map/round_block/pallas_call | solution.py:344
  1.9 2.1 %collective-permute-start.10 = (bf16[32,64,128]{2,1,0:T(8,128)(2,1)S(1)}, bf16[32,64,128]{2,1,0:T(8,128)(2,1)S(1)}, u32[]{:S(2)}, u32[]{:S(2)}) collective-permute-start(bf16[32,64,128]{2,1,0:T(8,128)(2,1)S(1)} %get-tuple-element.55.half_ref), channel_id=1, source_target_pairs={{0,32},{16,112},{32,64},{48,16},{64,96},{80,48},{96,0},{112,80},{1... | collective-permute-start | bytes 1572872 | tf_op jit(solution)/shard_map/ppermute | solution.py:317
  3.9 2.2 %collective-permute-start.12 = (bf16[32,64,128]{2,1,0:T(8,128)(2,1)S(1)}, bf16[32,64,128]{2,1,0:T(8,128)(2,1)S(1)}, u32[]{:S(2)}, u32[]{:S(2)}) collective-permute-start(bf16[32,64,128]{2,1,0:T(8,128)(2,1)S(1)} %get-tuple-element.55.half_ref), channel_id=1, source_target_pairs={{0,96},{16,48},{32,0},{48,80},{64,32},{80,112},{96,64},{112,16},{1... | collective-permute-start | bytes 1572872 | tf_op jit(solution)/shard_map/ppermute | solution.py:317
  6.1 7.8 %prepare.1 = (bf16[512,128,128]{2,1,0:T(8,128)(2,1)S(1)}, f32[32,128,64]{2,1,0:T(8,128)S(1)}, bf16[128,4096]{1,0:T(8,128)(2,1)S(1)}, f32[64,64]{1,0:T(8,128)S(1)}, s32[1,3072]{1,0:T(1,128)S(4)}, /*index=5*/s32[5]{0:T(128)S(4)}) custom-call(bf16[512,128,128]{2,1,0:T(8,128)(2,1)} %tiles_hbm.1, s32[1,512]{1,0:T(1,128)} %bitcast.26, s32[1,32]{1,0:T(1,128)} %bitcast.27, ...), custom_call_target="tpu_custom_call" | custom-call | flops 8999999488 | bytes 27000000 | tf_op jit(solution)/shard_map/prepare/pallas_call | solution.py:349
  14.0 3.0 %collective-permute-done.10.refs_0_ = bf16[32,64,128]{2,1,0:T(8,128)(2,1)S(1)} collective-permute-done((bf16[32,64,128]{2,1,0:T(8,128)(2,1)S(1)}, bf16[32,64,128]{2,1,0:T(8,128)(2,1)S(1)}, u32[]{:S(2)}, u32[]{:S(2)}) %collective-permute-start.10) | collective-permute-done | bytes 524320 | tf_op jit(solution)/shard_map/ppermute | solution.py:317
  18.4 2.6 %collective-permute-start.13 = (bf16[16,64,128]{2,1,0:T(8,128)(2,1)S(1)}, bf16[16,64,128]{2,1,0:T(8,128)(2,1)S(1)}, u32[]{:S(2)}, u32[]{:S(2)}) collective-permute-start(bf16[16,64,128]{2,1,0:T(8,128)(2,1)S(1)} %slice.38), channel_id=1, source_target_pairs={{0,96},{16,48},{32,0},{48,80},{64,32},{80,112},{96,64},{112,16},{1... | collective-permute-start | bytes 786440 | tf_op jit(solution)/shard_map/ppermute | solution.py:317
  21.0 2.3 %near_part.1.refs_2_ = f32[32,128,64]{2,1,0:T(8,128)S(1)} custom-call(s32[1,3072]{1,0:T(1,128)S(4)} %get-tuple-element.49.list_ref, s32[5]{0:T(128)S(4)} %get-tuple-element.50.count_ref, bf16[512,128,128]{2,1,0:T(8,128)(2,1)S(1)} %get-tuple-element.51.tiles_ref, ...), custom_call_target="tpu_custom_call", output_to_operand_aliasing={{}: (6, {})} | custom-call | flops 8000000000 | bytes 24000000 | tf_op jit(solution)/shard_map/near_part/pallas_call | solution.py:363
  23.3 1.8 %near_swapped.1.refs_2_ = f32[32,128,64]{2,1,0:T(8,128)S(1)} custom-call(s32[1,3072]{1,0:T(1,128)S(4)} %get-tuple-element.49.list_ref, s32[5]{0:T(128)S(4)} %get-tuple-element.50.count_ref, bf16[512,128,128]{2,1,0:T(8,128)(2,1)S(1)} %get-tuple-element.51.tiles_ref, ...), custom_call_target="tpu_custom_call", output_to_operand_aliasing={{}: (5, {})} | custom-call | tf_op jit(solution)/shard_map/near_swapped/pallas_call | solution.py:363
  25.1 1.0 %collective-permute-done.11.refs_0_ = bf16[16,64,128]{2,1,0:T(8,128)(2,1)S(1)} collective-permute-done((bf16[16,64,128]{2,1,0:T(8,128)(2,1)S(1)}, bf16[16,64,128]{2,1,0:T(8,128)(2,1)S(1)}, u32[]{:S(2)}, u32[]{:S(2)}) %collective-permute-start.11) | collective-permute-done | bytes 262176 | tf_op jit(solution)/shard_map/ppermute | solution.py:317
  26.2 1.6 %collective-permute-start.17 = (bf16[16,64,128]{2,1,0:T(8,128)(2,1)S(1)}, bf16[16,64,128]{2,1,0:T(8,128)(2,1)S(1)}, u32[]{:S(2)}, u32[]{:S(2)}) collective-permute-start(bf16[16,64,128]{2,1,0:T(8,128)(2,1)S(1)} %collective-permute-done.11.refs_0_), channel_id=1, source_target_pairs={{0,16},{16,0},{32,48},{48,32},{64,80},{80,64},{96,112},{112,96},{1... | collective-permute-start | bytes 786440 | tf_op jit(solution)/shard_map/ppermute | solution.py:317
  29.3 2.0 %last_part.1 = (f32[32,128,64]{2,1,0:T(8,128)S(1)}, bf16[4096,128]{1,0:T(8,128)(2,1)S(1)}, f32[72,128]{1,0:T(8,128)S(1)}) custom-call(s32[1,3072]{1,0:T(1,128)S(4)} %get-tuple-element.49.list_ref, s32[5]{0:T(128)S(4)} %get-tuple-element.50.count_ref, bf16[512,128,128]{2,1,0:T(8,128)(2,1)S(1)} %get-tuple-element.51.tiles_ref, ...), custom_call_target="tpu_custom_call", output_to_operand_aliasing={{0}: (5, {})} | custom-call | flops 4000000000 | bytes 12000000 | tf_op jit(solution)/shard_map/last_part/pallas_call | solution.py:381
  33.6 1.3 %collective-permute-start.21 = (f32[72,128]{1,0:T(8,128)S(1)}, f32[72,128]{1,0:T(8,128)S(1)}, u32[]{:S(2)}, u32[]{:S(2)}) collective-permute-start(f32[72,128]{1,0:T(8,128)S(1)} %add.78), channel_id=1, source_target_pairs={{0,96},{16,112},{32,64},{48,80},{64,32},{80,48},{96,0},{112,16},{1... | collective-permute-start | bytes 110600 | tf_op jit(solution)/shard_map/ppermute | solution.py:317
  34.9 1.2 %collective-permute-start.22 = (f32[72,128]{1,0:T(8,128)S(1)}, f32[72,128]{1,0:T(8,128)S(1)}, u32[]{:S(2)}, u32[]{:S(2)}) collective-permute-start(f32[72,128]{1,0:T(8,128)S(1)} %add.78), channel_id=1, source_target_pairs={{0,32},{16,48},{32,0},{48,16},{64,96},{80,112},{96,64},{112,80},{1... | collective-permute-start | bytes 110600 | tf_op jit(solution)/shard_map/ppermute | solution.py:317
  36.1 2.0 %collective-permute-done.20 = f32[72,128]{1,0:T(8,128)S(1)} collective-permute-done((f32[72,128]{1,0:T(8,128)S(1)}, f32[72,128]{1,0:T(8,128)S(1)}, u32[]{:S(2)}, u32[]{:S(2)}) %collective-permute-start.20) | collective-permute-done | bytes 36896 | tf_op jit(solution)/shard_map/ppermute | solution.py:317
  38.8 3.4 %collective-permute-start.23 = (f32[72,128]{1,0:T(8,128)S(1)}, f32[72,128]{1,0:T(8,128)S(1)}, u32[]{:S(2)}, u32[]{:S(2)}) collective-permute-start(f32[72,128]{1,0:T(8,128)S(1)} %add_add_fusion.4), channel_id=1, source_target_pairs={{0,8},{1,9},{2,10},{3,11},{4,12},{5,13},{6,14},{7,15},{8,0},{9,1},... | collective-permute-start | bytes 110600 | tf_op jit(solution)/shard_map/ppermute | solution.py:317
  42.2 1.1 %collective-permute-start.24 = (f32[72,128]{1,0:T(8,128)S(1)}, f32[72,128]{1,0:T(8,128)S(1)}, u32[]{:S(2)}, u32[]{:S(2)}) collective-permute-start(f32[72,128]{1,0:T(8,128)S(1)} %add_add_fusion.4), channel_id=1, source_target_pairs={{0,12},{1,13},{2,14},{3,15},{4,8},{5,9},{6,10},{7,11},{8,4},{9,5},... | collective-permute-start | bytes 110600 | tf_op jit(solution)/shard_map/ppermute | solution.py:317
  43.4 1.0 %collective-permute-done.23 = f32[72,128]{1,0:T(8,128)S(1)} collective-permute-done((f32[72,128]{1,0:T(8,128)S(1)}, f32[72,128]{1,0:T(8,128)S(1)}, u32[]{:S(2)}, u32[]{:S(2)}) %collective-permute-start.23) | collective-permute-done | bytes 36896 | tf_op jit(solution)/shard_map/ppermute | solution.py:317
  44.4 3.0 %collective-permute-done.24 = f32[72,128]{1,0:T(8,128)S(1)} collective-permute-done((f32[72,128]{1,0:T(8,128)S(1)}, f32[72,128]{1,0:T(8,128)S(1)}, u32[]{:S(2)}, u32[]{:S(2)}) %collective-permute-start.24) | collective-permute-done | bytes 36896 | tf_op jit(solution)/shard_map/ppermute | solution.py:317
  47.4 3.4 %collective-permute-start.26 = (f32[72,128]{1,0:T(8,128)S(1)}, f32[72,128]{1,0:T(8,128)S(1)}, u32[]{:S(2)}, u32[]{:S(2)}) collective-permute-start(f32[72,128]{1,0:T(8,128)S(1)} %add_add_fusion.3), channel_id=1, source_target_pairs={{0,2},{1,3},{2,0},{3,1},{4,6},{5,7},{6,4},{7,5},{8,10},{9,11},{10,... | collective-permute-start | bytes 110600 | tf_op jit(solution)/shard_map/ppermute | solution.py:317
  51.7 1.3 %collective-permute-done.26 = f32[72,128]{1,0:T(8,128)S(1)} collective-permute-done((f32[72,128]{1,0:T(8,128)S(1)}, f32[72,128]{1,0:T(8,128)S(1)}, u32[]{:S(2)}, u32[]{:S(2)}) %collective-permute-start.26) | collective-permute-done | bytes 36896 | tf_op jit(solution)/shard_map/ppermute | solution.py:317
  53.0 3.0 %collective-permute-done.27 = f32[72,128]{1,0:T(8,128)S(1)} collective-permute-done((f32[72,128]{1,0:T(8,128)S(1)}, f32[72,128]{1,0:T(8,128)S(1)}, u32[]{:S(2)}, u32[]{:S(2)}) %collective-permute-start.27) | collective-permute-done | bytes 36896 | tf_op jit(solution)/shard_map/ppermute | solution.py:317
  56.0 3.8 %factor.1 = (f32[64,64]{1,0:T(8,128)}, f32[64,64]{1,0:T(8,128)S(1)}, f32[64,128]{1,0:T(8,128)S(1)}, s32[1]{0:T(128)S(4)}) custom-call(f32[72,128]{1,0:T(8,128)S(1)} %add_add_fusion.2.sums_ref), custom_call_target="tpu_custom_call" | custom-call | flops 5000000000 | bytes 15000000 | tf_op jit(solution)/shard_map/factor/pallas_call | solution.py:387
  59.9 1.5 %conditional.1 = ((f32[64,4096]{1,0:T(8,128)}, f32[64,64]{1,0:T(8,128)})) conditional(s32[]{:T(128)} %bitcast.10, (bf16[4096,128]{1,0:T(8,128)(2,1)S(1)}, f32[72,128]{1,0:T(8,128)S(1)}, bf16[128,4096]{1,0:T(8,128)(2,1)S(1)}) %tuple.21, (f32[64,128]{1,0:T(8,128)S(1)}, bf16[4096,128]{1,0:T(8,128)(2,1)S(1)}, bf16[128,4096]{1,0:T(8,128)(2,1)S(1)}, ...), branch_computations={%region_0.0_spmd, %region_3.4_spmd} | conditional | flops 2000000000 | bytes 9659306 | solution.py:407
  59.9 1.5 %scale_block.1 = (f32[64,4096]{1,0:T(8,128)}, f32[64,64]{1,0:T(8,128)}) custom-call(f32[64,128]{1,0:T(8,128)S(1)} %get-tuple-element.17.f_ref, bf16[4096,128]{1,0:T(8,128)(2,1)S(1)} %get-tuple-element.18.zw_ref, bf16[128,4096]{1,0:T(8,128)(2,1)S(1)} %get-tuple-element.19.zx_ref, f32[64,64]{1,0:T(8,128)S(1)} %get-tuple-element.20.r_ref), custom_call_target="tpu_custom_call" | custom-call | flops 2000000000 | bytes 6000000 | tf_op jit(solution)/shard_map/cond/branch_1_fun/scale_block/pallas_call | solution.py:393
  (29 shorter events, 6.8 us)
Async XLA Ops:
  1.9 15.1 %collective-permute-start.10 = (bf16[32,64,128]{2,1,0:T(8,128)(2,1)S(1)}, bf16[32,64,128]{2,1,0:T(8,128)(2,1)S(1)}, u32[]{:S(2)}, u32[]{:S(2)}) collective-permute-start(bf16[32,64,128]{2,1,0:T(8,128)(2,1)S(1)} %get-tuple-element.55.half_ref), channel_id=1, source_target_pairs={{0,32},{16,112},{32,64},{48,16},{64,96},{80,48},{96,0},{112,80},{1... | collective-permute-start | bytes 1572872 | tf_op jit(solution)/shard_map/ppermute | solution.py:317
  3.9 14.4 %collective-permute-start.12 = (bf16[32,64,128]{2,1,0:T(8,128)(2,1)S(1)}, bf16[32,64,128]{2,1,0:T(8,128)(2,1)S(1)}, u32[]{:S(2)}, u32[]{:S(2)}) collective-permute-start(bf16[32,64,128]{2,1,0:T(8,128)(2,1)S(1)} %get-tuple-element.55.half_ref), channel_id=1, source_target_pairs={{0,96},{16,48},{32,0},{48,80},{64,32},{80,112},{96,64},{112,16},{1... | collective-permute-start | bytes 1572872 | tf_op jit(solution)/shard_map/ppermute | solution.py:317
  17.0 4.1 %collective-permute-start.16 = (bf16[32,64,128]{2,1,0:T(8,128)(2,1)S(1)}, bf16[32,64,128]{2,1,0:T(8,128)(2,1)S(1)}, u32[]{:S(2)}, u32[]{:S(2)}) collective-permute-start(bf16[32,64,128]{2,1,0:T(8,128)(2,1)S(1)} %get-tuple-element.55.half_ref), channel_id=1, source_target_pairs={{0,16},{16,0},{32,48},{48,32},{64,80},{80,64},{96,112},{112,96},{1... | collective-permute-start | bytes 1572872 | tf_op jit(solution)/shard_map/ppermute | solution.py:317
  17.0 6.3 %collective-permute-start.14 = (bf16[32,64,128]{2,1,0:T(8,128)(2,1)S(1)}, bf16[32,64,128]{2,1,0:T(8,128)(2,1)S(1)}, u32[]{:S(2)}, u32[]{:S(2)}) collective-permute-start(bf16[32,64,128]{2,1,0:T(8,128)(2,1)S(1)} %collective-permute-done.10.refs_0_), channel_id=1, source_target_pairs={{0,16},{16,0},{32,48},{48,32},{64,80},{80,64},{96,112},{112,96},{1... | collective-permute-start | bytes 1572872 | tf_op jit(solution)/shard_map/ppermute | solution.py:317
  17.5 8.7 %collective-permute-start.11 = (bf16[16,64,128]{2,1,0:T(8,128)(2,1)S(1)}, bf16[16,64,128]{2,1,0:T(8,128)(2,1)S(1)}, u32[]{:S(2)}, u32[]{:S(2)}) collective-permute-start(bf16[16,64,128]{2,1,0:T(8,128)(2,1)S(1)} %slice.33), channel_id=1, source_target_pairs={{0,32},{16,112},{32,64},{48,16},{64,96},{80,48},{96,0},{112,80},{1... | collective-permute-start | bytes 786440 | tf_op jit(solution)/shard_map/ppermute | solution.py:317
  18.4 7.8 %collective-permute-start.13 = (bf16[16,64,128]{2,1,0:T(8,128)(2,1)S(1)}, bf16[16,64,128]{2,1,0:T(8,128)(2,1)S(1)}, u32[]{:S(2)}, u32[]{:S(2)}) collective-permute-start(bf16[16,64,128]{2,1,0:T(8,128)(2,1)S(1)} %slice.38), channel_id=1, source_target_pairs={{0,96},{16,48},{32,0},{48,80},{64,32},{80,112},{96,64},{112,16},{1... | collective-permute-start | bytes 786440 | tf_op jit(solution)/shard_map/ppermute | solution.py:317
  21.0 2.3 %collective-permute-start.15 = (bf16[32,64,128]{2,1,0:T(8,128)(2,1)S(1)}, bf16[32,64,128]{2,1,0:T(8,128)(2,1)S(1)}, u32[]{:S(2)}, u32[]{:S(2)}) collective-permute-start(bf16[32,64,128]{2,1,0:T(8,128)(2,1)S(1)} %collective-permute-done.12.refs_1_), channel_id=1, source_target_pairs={{0,16},{16,0},{32,48},{48,32},{64,80},{80,64},{96,112},{112,96},{1... | collective-permute-start | bytes 1572872 | tf_op jit(solution)/shard_map/ppermute | solution.py:317
  26.2 2.8 %collective-permute-start.17 = (bf16[16,64,128]{2,1,0:T(8,128)(2,1)S(1)}, bf16[16,64,128]{2,1,0:T(8,128)(2,1)S(1)}, u32[]{:S(2)}, u32[]{:S(2)}) collective-permute-start(bf16[16,64,128]{2,1,0:T(8,128)(2,1)S(1)} %collective-permute-done.11.refs_0_), channel_id=1, source_target_pairs={{0,16},{16,0},{32,48},{48,32},{64,80},{80,64},{96,112},{112,96},{1... | collective-permute-start | bytes 786440 | tf_op jit(solution)/shard_map/ppermute | solution.py:317
  27.8 1.5 %collective-permute-start.18 = (bf16[16,64,128]{2,1,0:T(8,128)(2,1)S(1)}, bf16[16,64,128]{2,1,0:T(8,128)(2,1)S(1)}, u32[]{:S(2)}, u32[]{:S(2)}) collective-permute-start(bf16[16,64,128]{2,1,0:T(8,128)(2,1)S(1)} %collective-permute-done.13.refs_1_), channel_id=1, source_target_pairs={{0,16},{16,0},{32,48},{48,32},{64,80},{80,64},{96,112},{112,96},{1... | collective-permute-start | bytes 786440 | tf_op jit(solution)/shard_map/ppermute | solution.py:317
  31.3 1.3 %collective-permute-start.19 = (f32[72,128]{1,0:T(8,128)S(1)}, f32[72,128]{1,0:T(8,128)S(1)}, u32[]{:S(2)}, u32[]{:S(2)}) collective-permute-start(f32[72,128]{1,0:T(8,128)S(1)} %get-tuple-element.62), channel_id=1, source_target_pairs={{0,16},{16,0},{32,48},{48,32},{64,80},{80,64},{96,112},{112,96},{1... | collective-permute-start | bytes 110600 | tf_op jit(solution)/shard_map/ppermute | solution.py:317
  32.6 5.5 %collective-permute-start.20 = (f32[72,128]{1,0:T(8,128)S(1)}, f32[72,128]{1,0:T(8,128)S(1)}, u32[]{:S(2)}, u32[]{:S(2)}) collective-permute-start(f32[72,128]{1,0:T(8,128)S(1)} %add.78), channel_id=1, source_target_pairs={{0,64},{16,80},{32,96},{48,112},{64,0},{80,16},{96,32},{112,48},{1... | collective-permute-start | bytes 110600 | tf_op jit(solution)/shard_map/ppermute | solution.py:317
  33.6 5.2 %collective-permute-start.21 = (f32[72,128]{1,0:T(8,128)S(1)}, f32[72,128]{1,0:T(8,128)S(1)}, u32[]{:S(2)}, u32[]{:S(2)}) collective-permute-start(f32[72,128]{1,0:T(8,128)S(1)} %add.78), channel_id=1, source_target_pairs={{0,96},{16,112},{32,64},{48,80},{64,32},{80,48},{96,0},{112,16},{1... | collective-permute-start | bytes 110600 | tf_op jit(solution)/shard_map/ppermute | solution.py:317
  34.9 4.0 %collective-permute-start.22 = (f32[72,128]{1,0:T(8,128)S(1)}, f32[72,128]{1,0:T(8,128)S(1)}, u32[]{:S(2)}, u32[]{:S(2)}) collective-permute-start(f32[72,128]{1,0:T(8,128)S(1)} %add.78), channel_id=1, source_target_pairs={{0,32},{16,48},{32,0},{48,16},{64,96},{80,112},{96,64},{112,80},{1... | collective-permute-start | bytes 110600 | tf_op jit(solution)/shard_map/ppermute | solution.py:317
  38.8 5.5 %collective-permute-start.23 = (f32[72,128]{1,0:T(8,128)S(1)}, f32[72,128]{1,0:T(8,128)S(1)}, u32[]{:S(2)}, u32[]{:S(2)}) collective-permute-start(f32[72,128]{1,0:T(8,128)S(1)} %add_add_fusion.4), channel_id=1, source_target_pairs={{0,8},{1,9},{2,10},{3,11},{4,12},{5,13},{6,14},{7,15},{8,0},{9,1},... | collective-permute-start | bytes 110600 | tf_op jit(solution)/shard_map/ppermute | solution.py:317
  42.2 5.2 %collective-permute-start.24 = (f32[72,128]{1,0:T(8,128)S(1)}, f32[72,128]{1,0:T(8,128)S(1)}, u32[]{:S(2)}, u32[]{:S(2)}) collective-permute-start(f32[72,128]{1,0:T(8,128)S(1)} %add_add_fusion.4), channel_id=1, source_target_pairs={{0,12},{1,13},{2,14},{3,15},{4,8},{5,9},{6,10},{7,11},{8,4},{9,5},... | collective-permute-start | bytes 110600 | tf_op jit(solution)/shard_map/ppermute | solution.py:317
  43.4 4.0 %collective-permute-start.25 = (f32[72,128]{1,0:T(8,128)S(1)}, f32[72,128]{1,0:T(8,128)S(1)}, u32[]{:S(2)}, u32[]{:S(2)}) collective-permute-start(f32[72,128]{1,0:T(8,128)S(1)} %add_add_fusion.4), channel_id=1, source_target_pairs={{0,4},{1,5},{2,6},{3,7},{4,0},{5,1},{6,2},{7,3},{8,12},{9,13},{10,... | collective-permute-start | bytes 110600 | tf_op jit(solution)/shard_map/ppermute | solution.py:317
  47.4 5.5 %collective-permute-start.26 = (f32[72,128]{1,0:T(8,128)S(1)}, f32[72,128]{1,0:T(8,128)S(1)}, u32[]{:S(2)}, u32[]{:S(2)}) collective-permute-start(f32[72,128]{1,0:T(8,128)S(1)} %add_add_fusion.3), channel_id=1, source_target_pairs={{0,2},{1,3},{2,0},{3,1},{4,6},{5,7},{6,4},{7,5},{8,10},{9,11},{10,... | collective-permute-start | bytes 110600 | tf_op jit(solution)/shard_map/ppermute | solution.py:317
  50.8 5.2 %collective-permute-start.27 = (f32[72,128]{1,0:T(8,128)S(1)}, f32[72,128]{1,0:T(8,128)S(1)}, u32[]{:S(2)}, u32[]{:S(2)}) collective-permute-start(f32[72,128]{1,0:T(8,128)S(1)} %add_add_fusion.3), channel_id=1, source_target_pairs={{0,3},{1,2},{2,1},{3,0},{4,7},{5,6},{6,5},{7,4},{8,11},{9,10},{10,... | collective-permute-start | bytes 110600 | tf_op jit(solution)/shard_map/ppermute | solution.py:317
  51.7 4.3 %collective-permute-start.28 = (f32[72,128]{1,0:T(8,128)S(1)}, f32[72,128]{1,0:T(8,128)S(1)}, u32[]{:S(2)}, u32[]{:S(2)}) collective-permute-start(f32[72,128]{1,0:T(8,128)S(1)} %add_add_fusion.3), channel_id=1, source_target_pairs={{0,1},{1,0},{2,3},{3,2},{4,5},{5,4},{6,7},{7,6},{8,9},{9,8},{10,11... | collective-permute-start | bytes 110600 | tf_op jit(solution)/shard_map/ppermute | solution.py:317

commit v6 on v5

--- a/solution.py
+++ b/solution.py
@@ -52,6 +52,12 @@
 def split(x):
     hi = x.astype(BF16)
     return hi, (x - hi.astype(F32)).astype(BF16)
+
+
+def split3(x):
+    hi, rest = x.astype(BF16), x - x.astype(BF16).astype(F32)
+    mid = rest.astype(BF16)
+    return hi, mid, (rest - mid.astype(F32)).astype(BF16)
 
 
 def dot3(a, b):
@@ -182,15 +188,14 @@
     for c in range(NODES_DEV // wide):
         lanes = slice(c * wide, (c + 1) * wide)
         x = x_ref[:, lanes]
-        xhi, xlo = split(x)
-        zx_ref[0:K, lanes] = xhi
-        zx_ref[K:2 * K, lanes] = xlo
+        for i, part in enumerate(split3(x)):
+            zx_ref[i * K:(i + 1) * K, lanes] = part
         phi, plo = split(prev_ref[:, lanes])
         coupled = jnp.dot(left, jnp.concatenate([phi, plo, phi], axis=0), preferred_element_type=F32)
         w = x * weight_ref[:, lanes] - coupled
         for t in range(wide // TILE):
             w_ref[c * (wide // TILE) + t] = w[:, t * TILE:(t + 1) * TILE].T
-    zx = zx_ref[...]
+    zx = zx_ref[0:2 * K, :]
     gg = lax.dot_general(zx[:K], zx, NT, preferred_element_type=F32)
     cross = gg[:, K:]
     g_ref[...] = gg[:, :K] + cross + cross.T
@@ -207,17 +212,15 @@
     multiply_part(part, list_ref, count_ref, tiles_ref, picked_ref, w_ref)
 
 
-def last_kernel(list_ref, count_ref, tiles_ref, first_ref, second_ref, w_in_ref, zx_ref, g_ref, w_ref, zw_ref, sums_ref, picked_ref,
-                whi_ref):
+def last_kernel(list_ref, count_ref, tiles_ref, first_ref, second_ref, w_in_ref, zx_ref, g_ref, w_ref, zw_ref, sums_ref, picked_ref):
     place_tiles(picked_ref, first_ref, second_ref)
     multiply_part(4, list_ref, count_ref, tiles_ref, picked_ref, w_ref)
     for t in range(ROWS):
-        whi, wlo = split(w_ref[t])
-        zw_ref[t * TILE:(t + 1) * TILE, :] = jnp.concatenate([whi, wlo], axis=1)
-        whi_ref[:, t * TILE:(t + 1) * TILE] = whi.T
-    zw = zw_ref[...]
-    m = jnp.dot(zx_ref[...], zw, preferred_element_type=F32)
-    s = jnp.dot(whi_ref[...], zw, preferred_element_type=F32)
+        for i, part in enumerate(split3(w_ref[t].T)):
+            zw_ref[i * K:(i + 1) * K, t * TILE:(t + 1) * TILE] = part
+    zw = zw_ref[0:2 * K, :]
+    m = lax.dot_general(zx_ref[0:2 * K, :], zw, NT, preferred_element_type=F32)
+    s = lax.dot_general(zw[:K], zw, NT, preferred_element_type=F32)
     cross = s[:, K:]
     sums_ref[0:K, 0:K] = m[:K, :K] + m[:K, K:] + m[K:, :K]
     row = lax.broadcasted_iota(jnp.int32, (K, K), 0)
@@ -274,8 +277,8 @@
     row = lax.broadcasted_iota(jnp.int32, (K, K), 0)
     col = lax.broadcasted_iota(jnp.int32, (K, K), 1)
     eye = jnp.where(row == col, 1.0, 0.0)
-    rt = r.T
-    flip = both.T
+    turned = sums_ref[0:K, :].T * inv
+    rt, flip = turned[:K], turned[K:]
     s = jnp.where(col >= row, both, flip)
     g = jnp.where(col < row, both, jnp.where(col > row, flip, diagonal))
     gram = s - dot3(rt, dot3(2.0 * eye - g, r))
@@ -298,13 +301,13 @@
     f1h, f1l = split(f_ref[:, 0:K])
     f2h, f2l = split(f_ref[:, K:])
     zero = jnp.zeros((K, K), BF16)
-    left = [jnp.concatenate([jnp.concatenate([hi, hi], axis=1), jnp.concatenate([lo, zero], axis=1)], axis=0)
-            for hi, lo in ((f1h, f1l), (f2h, f2l))]
+    left = jnp.concatenate([jnp.concatenate([f1h, f1h, f2h, f2h], axis=1),
+                            jnp.concatenate([f1l, zero, f2l, zero], axis=1)], axis=0)
     wide = NODES_DEV // CHUNKS
     for c in range(CHUNKS):
         lanes = slice(c * wide, (c + 1) * wide)
-        y = (lax.dot_general(left[0], zw_ref[lanes, :], NT, preferred_element_type=F32)
-             + jnp.dot(left[1], zx_ref[:, lanes], preferred_element_type=F32))
+        z = jnp.concatenate([zw_ref[0:2 * K, lanes], zx_ref[0:2 * K, lanes]], axis=0)
+        y = jnp.dot(left, z, preferred_element_type=F32)
         out_ref[:, lanes] = y[:K] + y[K:]
         copies.append(pltpu.make_async_copy(out_ref.at[:, lanes], out_hbm.at[:, lanes], sems.at[c]))
         copies[-1].start()
@@ -337,7 +340,7 @@
     node_total = NODES_DEV * lax.axis_size("row") * lax.axis_size("col")
     after = lax.optimization_barrier
     w_vmem = pltpu.VMEM(NODE_ROWS, F32)
-    pair_vmem = pltpu.VMEM((2 * K, NODES_DEV), BF16)
+    parts_vmem = pltpu.VMEM((3 * K, NODES_DEV), BF16)
     picked = lambda n: pltpu.VMEM((1 + n * ROWS, K, TILE), BF16)
     square = jax.ShapeDtypeStruct((K, K), F32)
 
@@ -348,7 +351,7 @@
     a2 = onward(half, -1)
     tiles, w, zx, g, lists, counts = call(
         prepare_kernel, "prepare",
-        (pltpu.VMEM((SLOTS, TILE, TILE), BF16), w_vmem, pair_vmem, pltpu.VMEM((K, K), F32),
+        (pltpu.VMEM((SLOTS, TILE, TILE), BF16), w_vmem, parts_vmem, pltpu.VMEM((K, K), F32),
          pltpu.SMEM((1, TABLE), jnp.int32), pltpu.SMEM((PARTS,), jnp.int32)),
         [hbm()] * 6 + [vmem()] * 2, (vmem(), vmem(), vmem(), vmem(), smem(), smem()), 16, 9,
         [pltpu.VMEM((1, SLOTS), jnp.int32), pltpu.VMEM((1, ROWS), jnp.int32), pltpu.VMEM((K, NODES_DEV), F32),
@@ -379,9 +382,9 @@
     s2 = core_swap(f2)
     w = add_part(3, "far_part", [f1, f2], w, 2)
     _, zw, sums = call(
-        last_kernel, "last_part", (w_vmem, pltpu.VMEM((NODES_DEV, 2 * K), BF16), jax.ShapeDtypeStruct((K + 8, 2 * K), F32)),
+        last_kernel, "last_part", (w_vmem, parts_vmem, jax.ShapeDtypeStruct((K + 8, 2 * K), F32)),
         [smem(), smem()] + [vmem()] * 6, (vmem(), vmem(), vmem()), 16, 4,
-        [picked(1), pltpu.VMEM((K, NODES_DEV), BF16)], {5: 0})(lists, counts, tiles, s1, s2, w, zx, g)
+        [picked(1)], {5: 0})(lists, counts, tiles, s1, s2, w, zx, g)
 
     sums = total(sums)
     rayleigh, r_factor, f, flag = call(
@@ -396,9 +399,8 @@
                 f, zw, zx, r_factor)
 
     def two_passes(zw, zx, f, sums, r_factor):
-        whole = lambda z: z[:K].astype(F32) + z[K:].astype(F32)
-        zw = zw.T
         rayleigh_t = sums[:K, :K].T / node_total
+        whole = lambda z: (z[:K].astype(F32) + z[K:2 * K].astype(F32)) + z[2 * K:].astype(F32)
         w_next = whole(zw) - jnp.dot(rayleigh_t, whole(zx), precision=HIGHEST)
         gram = total(jnp.dot(w_next, w_next.T, precision=HIGHEST)) / node_total
         lower = jnp.linalg.cholesky(gram)

time: 61.5 us -> 61.3 us (level)
  no operation moved by 1% of the time
where the time goes in v6:
time: 61.3 us; the launch traced here: 61.1 us
  starting transfers between devices  22.5 us (37%)
  Pallas kernels  21.1 us (34%)
  waiting for transfers between devices  16.4 us (27%)
  between operations  0.88 us (1%)
    ppermute x19, starting transfers between devices, exchange(): return lax.ppermute(v, axis, [(i, to(i)) for i in range(n)])  22.5 us
    ppermute x19, waiting for transfers between devices, exchange(): return lax.ppermute(v, axis, [(i, to(i)) for i in range(n)])  16.4 us
    pallas_call x1, Pallas kernels, local(): call(prepare_kernel, 'prepare', (pltpu.VMEM((SLOTS, TILE, TILE), BF16), w...  7.86 us
    pallas_call x3, Pallas kernels, add_part(): call(functools.partial(part_kernel, part), name, w_vmem, [smem(), smem()]...  4.94 us
    pallas_call x1, Pallas kernels, local(): call(functools.partial(factor_kernel, node_total), 'factor', (square, squ...  3.8 us
    pallas_call x1, Pallas kernels, local(): call(last_kernel, 'last_part', (w_vmem, parts_vmem, jax.ShapeDtypeStruct(...  2.03 us
    pallas_call x1, Pallas kernels, plain(): call(final_kernel, 'scale_block', (pltpu.HBM((K, NODES_DEV), F32), pltpu....  1.27 us
    pallas_call x1, Pallas kernels, local(): call(round_kernel, 'round_block', (pltpu.VMEM(SLAB, BF16), pltpu.VMEM((K,...  1.24 us
  transfers between devices with their start and end apart: 19, of which 12 were waited for; matrix products, arithmetic and copies ran while one was open for 0% of the time, Pallas kernels for 21%

profile of v6, /device:TPU:0, one launch (start us, length us, event | category | flops | bytes accessed | tf_op | source)
XLA Modules:
  0.0 61.1 jit_solution(7135166520140245983)
XLA Ops:
  0.6 1.2 %round_block.1 = (bf16[32,64,128]{2,1,0:T(8,128)(2,1)S(1)}, f32[64,4096]{1,0:T(8,128)S(1)}) custom-call(f32[64,4096]{1,0:T(8,128)} %bitcast.21), custom_call_target="tpu_custom_call" | custom-call | flops 1000000000 | bytes 3000000 | tf_op jit(solution)/shard_map/round_block/pallas_call | solution.py:347
  1.9 2.1 %collective-permute-start.10 = (bf16[32,64,128]{2,1,0:T(8,128)(2,1)S(1)}, bf16[32,64,128]{2,1,0:T(8,128)(2,1)S(1)}, u32[]{:S(2)}, u32[]{:S(2)}) collective-permute-start(bf16[32,64,128]{2,1,0:T(8,128)(2,1)S(1)} %get-tuple-element.55.half_ref), channel_id=1, source_target_pairs={{0,32},{16,112},{32,64},{48,16},{64,96},{80,48},{96,0},{112,80},{1... | collective-permute-start | bytes 1572872 | tf_op jit(solution)/shard_map/ppermute | solution.py:320
  3.9 2.2 %collective-permute-start.12 = (bf16[32,64,128]{2,1,0:T(8,128)(2,1)S(1)}, bf16[32,64,128]{2,1,0:T(8,128)(2,1)S(1)}, u32[]{:S(2)}, u32[]{:S(2)}) collective-permute-start(bf16[32,64,128]{2,1,0:T(8,128)(2,1)S(1)} %get-tuple-element.55.half_ref), channel_id=1, source_target_pairs={{0,96},{16,48},{32,0},{48,80},{64,32},{80,112},{96,64},{112,16},{1... | collective-permute-start | bytes 1572872 | tf_op jit(solution)/shard_map/ppermute | solution.py:320
  6.1 7.9 %prepare.1 = (bf16[512,128,128]{2,1,0:T(8,128)(2,1)S(1)}, f32[32,128,64]{2,1,0:T(8,128)S(1)}, bf16[192,4096]{1,0:T(8,128)(2,1)S(1)}, f32[64,64]{1,0:T(8,128)S(1)}, s32[1,3072]{1,0:T(1,128)S(4)}, /*index=5*/s32[5]{0:T(128)S(4)}) custom-call(bf16[512,128,128]{2,1,0:T(8,128)(2,1)} %tiles_hbm.1, s32[1,512]{1,0:T(1,128)} %bitcast.24, s32[1,32]{1,0:T(1,128)} %bitcast.25, ...), custom_call_target="tpu_custom_call" | custom-call | flops 8999999488 | bytes 27000000 | tf_op jit(solution)/shard_map/prepare/pallas_call | solution.py:352
  14.0 2.9 %collective-permute-done.10.refs_0_ = bf16[32,64,128]{2,1,0:T(8,128)(2,1)S(1)} collective-permute-done((bf16[32,64,128]{2,1,0:T(8,128)(2,1)S(1)}, bf16[32,64,128]{2,1,0:T(8,128)(2,1)S(1)}, u32[]{:S(2)}, u32[]{:S(2)}) %collective-permute-start.10) | collective-permute-done | bytes 524320 | tf_op jit(solution)/shard_map/ppermute | solution.py:320
  18.4 2.6 %collective-permute-start.13 = (bf16[16,64,128]{2,1,0:T(8,128)(2,1)S(1)}, bf16[16,64,128]{2,1,0:T(8,128)(2,1)S(1)}, u32[]{:S(2)}, u32[]{:S(2)}) collective-permute-start(bf16[16,64,128]{2,1,0:T(8,128)(2,1)S(1)} %slice.42), channel_id=1, source_target_pairs={{0,96},{16,48},{32,0},{48,80},{64,32},{80,112},{96,64},{112,16},{1... | collective-permute-start | bytes 786440 | tf_op jit(solution)/shard_map/ppermute | solution.py:320
  21.0 2.3 %near_part.1.refs_2_ = f32[32,128,64]{2,1,0:T(8,128)S(1)} custom-call(s32[1,3072]{1,0:T(1,128)S(4)} %get-tuple-element.49.list_ref, s32[5]{0:T(128)S(4)} %get-tuple-element.50.count_ref, bf16[512,128,128]{2,1,0:T(8,128)(2,1)S(1)} %get-tuple-element.51.tiles_ref, ...), custom_call_target="tpu_custom_call", output_to_operand_aliasing={{}: (6, {})} | custom-call | flops 8000000000 | bytes 24000000 | tf_op jit(solution)/shard_map/near_part/pallas_call | solution.py:366
  23.3 1.8 %near_swapped.1.refs_2_ = f32[32,128,64]{2,1,0:T(8,128)S(1)} custom-call(s32[1,3072]{1,0:T(1,128)S(4)} %get-tuple-element.49.list_ref, s32[5]{0:T(128)S(4)} %get-tuple-element.50.count_ref, bf16[512,128,128]{2,1,0:T(8,128)(2,1)S(1)} %get-tuple-element.51.tiles_ref, ...), custom_call_target="tpu_custom_call", output_to_operand_aliasing={{}: (5, {})} | custom-call | tf_op jit(solution)/shard_map/near_swapped/pallas_call | solution.py:366
  26.2 1.6 %collective-permute-start.17 = (bf16[16,64,128]{2,1,0:T(8,128)(2,1)S(1)}, bf16[16,64,128]{2,1,0:T(8,128)(2,1)S(1)}, u32[]{:S(2)}, u32[]{:S(2)}) collective-permute-start(bf16[16,64,128]{2,1,0:T(8,128)(2,1)S(1)} %collective-permute-done.11.refs_0_), channel_id=1, source_target_pairs={{0,16},{16,0},{32,48},{48,32},{64,80},{80,64},{96,112},{112,96},{1... | collective-permute-start | bytes 786440 | tf_op jit(solution)/shard_map/ppermute | solution.py:320
  29.3 2.0 %last_part.1 = (f32[32,128,64]{2,1,0:T(8,128)S(1)}, bf16[192,4096]{1,0:T(8,128)(2,1)S(1)}, f32[72,128]{1,0:T(8,128)S(1)}) custom-call(s32[1,3072]{1,0:T(1,128)S(4)} %get-tuple-element.49.list_ref, s32[5]{0:T(128)S(4)} %get-tuple-element.50.count_ref, bf16[512,128,128]{2,1,0:T(8,128)(2,1)S(1)} %get-tuple-element.51.tiles_ref, ...), custom_call_target="tpu_custom_call", output_to_operand_aliasing={{0}: (5, {})} | custom-call | flops 4000000000 | bytes 12000000 | tf_op jit(solution)/shard_map/last_part/pallas_call | solution.py:384
  32.6 1.2 %collective-permute-start.20 = (f32[72,128]{1,0:T(8,128)S(1)}, f32[72,128]{1,0:T(8,128)S(1)}, u32[]{:S(2)}, u32[]{:S(2)}) collective-permute-start(f32[72,128]{1,0:T(8,128)S(1)} %add.84), channel_id=1, source_target_pairs={{0,64},{16,80},{32,96},{48,112},{64,0},{80,16},{96,32},{112,48},{1... | collective-permute-start | bytes 110600 | tf_op jit(solution)/shard_map/ppermute | solution.py:320
  33.8 1.2 %collective-permute-start.21 = (f32[72,128]{1,0:T(8,128)S(1)}, f32[72,128]{1,0:T(8,128)S(1)}, u32[]{:S(2)}, u32[]{:S(2)}) collective-permute-start(f32[72,128]{1,0:T(8,128)S(1)} %add.84), channel_id=1, source_target_pairs={{0,96},{16,112},{32,64},{48,80},{64,32},{80,48},{96,0},{112,16},{1... | collective-permute-start | bytes 110600 | tf_op jit(solution)/shard_map/ppermute | solution.py:320
  35.0 1.2 %collective-permute-start.22 = (f32[72,128]{1,0:T(8,128)S(1)}, f32[72,128]{1,0:T(8,128)S(1)}, u32[]{:S(2)}, u32[]{:S(2)}) collective-permute-start(f32[72,128]{1,0:T(8,128)S(1)} %add.84), channel_id=1, source_target_pairs={{0,32},{16,48},{32,0},{48,16},{64,96},{80,112},{96,64},{112,80},{1... | collective-permute-start | bytes 110600 | tf_op jit(solution)/shard_map/ppermute | solution.py:320
  36.1 2.1 %collective-permute-done.20 = f32[72,128]{1,0:T(8,128)S(1)} collective-permute-done((f32[72,128]{1,0:T(8,128)S(1)}, f32[72,128]{1,0:T(8,128)S(1)}, u32[]{:S(2)}, u32[]{:S(2)}) %collective-permute-start.20) | collective-permute-done | bytes 36896 | tf_op jit(solution)/shard_map/ppermute | solution.py:320
  39.0 3.5 %collective-permute-start.23 = (f32[72,128]{1,0:T(8,128)S(1)}, f32[72,128]{1,0:T(8,128)S(1)}, u32[]{:S(2)}, u32[]{:S(2)}) collective-permute-start(f32[72,128]{1,0:T(8,128)S(1)} %add_add_fusion.4), channel_id=1, source_target_pairs={{0,8},{1,9},{2,10},{3,11},{4,12},{5,13},{6,14},{7,15},{8,0},{9,1},... | collective-permute-start | bytes 110600 | tf_op jit(solution)/shard_map/ppermute | solution.py:320
  42.5 1.4 %collective-permute-start.24 = (f32[72,128]{1,0:T(8,128)S(1)}, f32[72,128]{1,0:T(8,128)S(1)}, u32[]{:S(2)}, u32[]{:S(2)}) collective-permute-start(f32[72,128]{1,0:T(8,128)S(1)} %add_add_fusion.4), channel_id=1, source_target_pairs={{0,12},{1,13},{2,14},{3,15},{4,8},{5,9},{6,10},{7,11},{8,4},{9,5},... | collective-permute-start | bytes 110600 | tf_op jit(solution)/shard_map/ppermute | solution.py:320
  44.5 3.1 %collective-permute-done.24 = f32[72,128]{1,0:T(8,128)S(1)} collective-permute-done((f32[72,128]{1,0:T(8,128)S(1)}, f32[72,128]{1,0:T(8,128)S(1)}, u32[]{:S(2)}, u32[]{:S(2)}) %collective-permute-start.24) | collective-permute-done | bytes 36896 | tf_op jit(solution)/shard_map/ppermute | solution.py:320
  47.8 2.8 %collective-permute-start.26 = (f32[72,128]{1,0:T(8,128)S(1)}, f32[72,128]{1,0:T(8,128)S(1)}, u32[]{:S(2)}, u32[]{:S(2)}) collective-permute-start(f32[72,128]{1,0:T(8,128)S(1)} %add_add_fusion.3), channel_id=1, source_target_pairs={{0,2},{1,3},{2,0},{3,1},{4,6},{5,7},{6,4},{7,5},{8,10},{9,11},{10,... | collective-permute-start | bytes 110600 | tf_op jit(solution)/shard_map/ppermute | solution.py:320
  50.6 1.1 %collective-permute-start.27 = (f32[72,128]{1,0:T(8,128)S(1)}, f32[72,128]{1,0:T(8,128)S(1)}, u32[]{:S(2)}, u32[]{:S(2)}) collective-permute-start(f32[72,128]{1,0:T(8,128)S(1)} %add_add_fusion.3), channel_id=1, source_target_pairs={{0,3},{1,2},{2,1},{3,0},{4,7},{5,6},{6,5},{7,4},{8,11},{9,10},{10,... | collective-permute-start | bytes 110600 | tf_op jit(solution)/shard_map/ppermute | solution.py:320
  51.7 1.8 %collective-permute-done.26 = f32[72,128]{1,0:T(8,128)S(1)} collective-permute-done((f32[72,128]{1,0:T(8,128)S(1)}, f32[72,128]{1,0:T(8,128)S(1)}, u32[]{:S(2)}, u32[]{:S(2)}) %collective-permute-start.26) | collective-permute-done | bytes 36896 | tf_op jit(solution)/shard_map/ppermute | solution.py:320
  53.5 2.3 %collective-permute-done.27 = f32[72,128]{1,0:T(8,128)S(1)} collective-permute-done((f32[72,128]{1,0:T(8,128)S(1)}, f32[72,128]{1,0:T(8,128)S(1)}, u32[]{:S(2)}, u32[]{:S(2)}) %collective-permute-start.27) | collective-permute-done | bytes 36896 | tf_op jit(solution)/shard_map/ppermute | solution.py:320
  55.8 3.8 %factor.1 = (f32[64,64]{1,0:T(8,128)}, f32[64,64]{1,0:T(8,128)S(1)}, f32[64,128]{1,0:T(8,128)S(1)}, s32[1]{0:T(128)S(4)}) custom-call(f32[72,128]{1,0:T(8,128)S(1)} %add_add_fusion.2.sums_ref), custom_call_target="tpu_custom_call" | custom-call | flops 5000000000 | bytes 15000000 | tf_op jit(solution)/shard_map/factor/pallas_call | solution.py:390
  59.6 1.3 %conditional.1 = ((f32[64,4096]{1,0:T(8,128)}, f32[64,64]{1,0:T(8,128)})) conditional(s32[]{:T(128)} %bitcast.9, (bf16[192,4096]{1,0:T(8,128)(2,1)S(1)}, f32[72,128]{1,0:T(8,128)S(1)}, bf16[192,4096]{1,0:T(8,128)(2,1)S(1)}) %tuple.21, (f32[64,128]{1,0:T(8,128)S(1)}, bf16[192,4096]{1,0:T(8,128)(2,1)S(1)}, bf16[192,4096]{1,0:T(8,128)(2,1)S(1)}, ...), branch_computations={%region_0.0_spmd, %region_3.4_spmd} | conditional | flops 2000000000 | bytes 12805062 | solution.py:409
  59.6 1.3 %scale_block.1 = (f32[64,4096]{1,0:T(8,128)}, f32[64,64]{1,0:T(8,128)}) custom-call(f32[64,128]{1,0:T(8,128)S(1)} %get-tuple-element.17.f_ref, bf16[192,4096]{1,0:T(8,128)(2,1)S(1)} %get-tuple-element.18.zw_ref, bf16[192,4096]{1,0:T(8,128)(2,1)S(1)} %get-tuple-element.19.zx_ref, f32[64,64]{1,0:T(8,128)S(1)} %get-tuple-element.20.r_ref), custom_call_target="tpu_custom_call" | custom-call | flops 2000000000 | bytes 6000000 | tf_op jit(solution)/shard_map/cond/branch_1_fun/scale_block/pallas_call | solution.py:396
  (29 shorter events, 7.0 us)
Async XLA Ops:
  1.9 15.1 %collective-permute-start.10 = (bf16[32,64,128]{2,1,0:T(8,128)(2,1)S(1)}, bf16[32,64,128]{2,1,0:T(8,128)(2,1)S(1)}, u32[]{:S(2)}, u32[]{:S(2)}) collective-permute-start(bf16[32,64,128]{2,1,0:T(8,128)(2,1)S(1)} %get-tuple-element.55.half_ref), channel_id=1, source_target_pairs={{0,32},{16,112},{32,64},{48,16},{64,96},{80,48},{96,0},{112,80},{1... | collective-permute-start | bytes 1572872 | tf_op jit(solution)/shard_map/ppermute | solution.py:320
  3.9 14.4 %collective-permute-start.12 = (bf16[32,64,128]{2,1,0:T(8,128)(2,1)S(1)}, bf16[32,64,128]{2,1,0:T(8,128)(2,1)S(1)}, u32[]{:S(2)}, u32[]{:S(2)}) collective-permute-start(bf16[32,64,128]{2,1,0:T(8,128)(2,1)S(1)} %get-tuple-element.55.half_ref), channel_id=1, source_target_pairs={{0,96},{16,48},{32,0},{48,80},{64,32},{80,112},{96,64},{112,16},{1... | collective-permute-start | bytes 1572872 | tf_op jit(solution)/shard_map/ppermute | solution.py:320
  17.0 4.1 %collective-permute-start.16 = (bf16[32,64,128]{2,1,0:T(8,128)(2,1)S(1)}, bf16[32,64,128]{2,1,0:T(8,128)(2,1)S(1)}, u32[]{:S(2)}, u32[]{:S(2)}) collective-permute-start(bf16[32,64,128]{2,1,0:T(8,128)(2,1)S(1)} %get-tuple-element.55.half_ref), channel_id=1, source_target_pairs={{0,16},{16,0},{32,48},{48,32},{64,80},{80,64},{96,112},{112,96},{1... | collective-permute-start | bytes 1572872 | tf_op jit(solution)/shard_map/ppermute | solution.py:320
  17.0 6.3 %collective-permute-start.14 = (bf16[32,64,128]{2,1,0:T(8,128)(2,1)S(1)}, bf16[32,64,128]{2,1,0:T(8,128)(2,1)S(1)}, u32[]{:S(2)}, u32[]{:S(2)}) collective-permute-start(bf16[32,64,128]{2,1,0:T(8,128)(2,1)S(1)} %collective-permute-done.10.refs_0_), channel_id=1, source_target_pairs={{0,16},{16,0},{32,48},{48,32},{64,80},{80,64},{96,112},{112,96},{1... | collective-permute-start | bytes 1572872 | tf_op jit(solution)/shard_map/ppermute | solution.py:320
  17.5 8.7 %collective-permute-start.11 = (bf16[16,64,128]{2,1,0:T(8,128)(2,1)S(1)}, bf16[16,64,128]{2,1,0:T(8,128)(2,1)S(1)}, u32[]{:S(2)}, u32[]{:S(2)}) collective-permute-start(bf16[16,64,128]{2,1,0:T(8,128)(2,1)S(1)} %slice.39), channel_id=1, source_target_pairs={{0,32},{16,112},{32,64},{48,16},{64,96},{80,48},{96,0},{112,80},{1... | collective-permute-start | bytes 786440 | tf_op jit(solution)/shard_map/ppermute | solution.py:320
  18.4 7.8 %collective-permute-start.13 = (bf16[16,64,128]{2,1,0:T(8,128)(2,1)S(1)}, bf16[16,64,128]{2,1,0:T(8,128)(2,1)S(1)}, u32[]{:S(2)}, u32[]{:S(2)}) collective-permute-start(bf16[16,64,128]{2,1,0:T(8,128)(2,1)S(1)} %slice.42), channel_id=1, source_target_pairs={{0,96},{16,48},{32,0},{48,80},{64,32},{80,112},{96,64},{112,16},{1... | collective-permute-start | bytes 786440 | tf_op jit(solution)/shard_map/ppermute | solution.py:320
  21.0 2.3 %collective-permute-start.15 = (bf16[32,64,128]{2,1,0:T(8,128)(2,1)S(1)}, bf16[32,64,128]{2,1,0:T(8,128)(2,1)S(1)}, u32[]{:S(2)}, u32[]{:S(2)}) collective-permute-start(bf16[32,64,128]{2,1,0:T(8,128)(2,1)S(1)} %collective-permute-done.12.refs_1_), channel_id=1, source_target_pairs={{0,16},{16,0},{32,48},{48,32},{64,80},{80,64},{96,112},{112,96},{1... | collective-permute-start | bytes 1572872 | tf_op jit(solution)/shard_map/ppermute | solution.py:320
  26.2 2.8 %collective-permute-start.17 = (bf16[16,64,128]{2,1,0:T(8,128)(2,1)S(1)}, bf16[16,64,128]{2,1,0:T(8,128)(2,1)S(1)}, u32[]{:S(2)}, u32[]{:S(2)}) collective-permute-start(bf16[16,64,128]{2,1,0:T(8,128)(2,1)S(1)} %collective-permute-done.11.refs_0_), channel_id=1, source_target_pairs={{0,16},{16,0},{32,48},{48,32},{64,80},{80,64},{96,112},{112,96},{1... | collective-permute-start | bytes 786440 | tf_op jit(solution)/shard_map/ppermute | solution.py:320
  27.8 1.5 %collective-permute-start.18 = (bf16[16,64,128]{2,1,0:T(8,128)(2,1)S(1)}, bf16[16,64,128]{2,1,0:T(8,128)(2,1)S(1)}, u32[]{:S(2)}, u32[]{:S(2)}) collective-permute-start(bf16[16,64,128]{2,1,0:T(8,128)(2,1)S(1)} %collective-permute-done.13.refs_1_), channel_id=1, source_target_pairs={{0,16},{16,0},{32,48},{48,32},{64,80},{80,64},{96,112},{112,96},{1... | collective-permute-start | bytes 786440 | tf_op jit(solution)/shard_map/ppermute | solution.py:320
  31.3 1.3 %collective-permute-start.19 = (f32[72,128]{1,0:T(8,128)S(1)}, f32[72,128]{1,0:T(8,128)S(1)}, u32[]{:S(2)}, u32[]{:S(2)}) collective-permute-start(f32[72,128]{1,0:T(8,128)S(1)} %get-tuple-element.62), channel_id=1, source_target_pairs={{0,16},{16,0},{32,48},{48,32},{64,80},{80,64},{96,112},{112,96},{1... | collective-permute-start | bytes 110600 | tf_op jit(solution)/shard_map/ppermute | solution.py:320
  32.6 5.6 %collective-permute-start.20 = (f32[72,128]{1,0:T(8,128)S(1)}, f32[72,128]{1,0:T(8,128)S(1)}, u32[]{:S(2)}, u32[]{:S(2)}) collective-permute-start(f32[72,128]{1,0:T(8,128)S(1)} %add.84), channel_id=1, source_target_pairs={{0,64},{16,80},{32,96},{48,112},{64,0},{80,16},{96,32},{112,48},{1... | collective-permute-start | bytes 110600 | tf_op jit(solution)/shard_map/ppermute | solution.py:320
  33.8 5.2 %collective-permute-start.21 = (f32[72,128]{1,0:T(8,128)S(1)}, f32[72,128]{1,0:T(8,128)S(1)}, u32[]{:S(2)}, u32[]{:S(2)}) collective-permute-start(f32[72,128]{1,0:T(8,128)S(1)} %add.84), channel_id=1, source_target_pairs={{0,96},{16,112},{32,64},{48,80},{64,32},{80,48},{96,0},{112,16},{1... | collective-permute-start | bytes 110600 | tf_op jit(solution)/shard_map/ppermute | solution.py:320
  35.0 4.0 %collective-permute-start.22 = (f32[72,128]{1,0:T(8,128)S(1)}, f32[72,128]{1,0:T(8,128)S(1)}, u32[]{:S(2)}, u32[]{:S(2)}) collective-permute-start(f32[72,128]{1,0:T(8,128)S(1)} %add.84), channel_id=1, source_target_pairs={{0,32},{16,48},{32,0},{48,16},{64,96},{80,112},{96,64},{112,80},{1... | collective-permute-start | bytes 110600 | tf_op jit(solution)/shard_map/ppermute | solution.py:320
  39.0 5.5 %collective-permute-start.23 = (f32[72,128]{1,0:T(8,128)S(1)}, f32[72,128]{1,0:T(8,128)S(1)}, u32[]{:S(2)}, u32[]{:S(2)}) collective-permute-start(f32[72,128]{1,0:T(8,128)S(1)} %add_add_fusion.4), channel_id=1, source_target_pairs={{0,8},{1,9},{2,10},{3,11},{4,12},{5,13},{6,14},{7,15},{8,0},{9,1},... | collective-permute-start | bytes 110600 | tf_op jit(solution)/shard_map/ppermute | solution.py:320
  42.5 5.2 %collective-permute-start.24 = (f32[72,128]{1,0:T(8,128)S(1)}, f32[72,128]{1,0:T(8,128)S(1)}, u32[]{:S(2)}, u32[]{:S(2)}) collective-permute-start(f32[72,128]{1,0:T(8,128)S(1)} %add_add_fusion.4), channel_id=1, source_target_pairs={{0,12},{1,13},{2,14},{3,15},{4,8},{5,9},{6,10},{7,11},{8,4},{9,5},... | collective-permute-start | bytes 110600 | tf_op jit(solution)/shard_map/ppermute | solution.py:320
  43.8 4.0 %collective-permute-start.25 = (f32[72,128]{1,0:T(8,128)S(1)}, f32[72,128]{1,0:T(8,128)S(1)}, u32[]{:S(2)}, u32[]{:S(2)}) collective-permute-start(f32[72,128]{1,0:T(8,128)S(1)} %add_add_fusion.4), channel_id=1, source_target_pairs={{0,4},{1,5},{2,6},{3,7},{4,0},{5,1},{6,2},{7,3},{8,12},{9,13},{10,... | collective-permute-start | bytes 110600 | tf_op jit(solution)/shard_map/ppermute | solution.py:320
  47.8 5.7 %collective-permute-start.26 = (f32[72,128]{1,0:T(8,128)S(1)}, f32[72,128]{1,0:T(8,128)S(1)}, u32[]{:S(2)}, u32[]{:S(2)}) collective-permute-start(f32[72,128]{1,0:T(8,128)S(1)} %add_add_fusion.3), channel_id=1, source_target_pairs={{0,2},{1,3},{2,0},{3,1},{4,6},{5,7},{6,4},{7,5},{8,10},{9,11},{10,... | collective-permute-start | bytes 110600 | tf_op jit(solution)/shard_map/ppermute | solution.py:320
  50.6 5.2 %collective-permute-start.27 = (f32[72,128]{1,0:T(8,128)S(1)}, f32[72,128]{1,0:T(8,128)S(1)}, u32[]{:S(2)}, u32[]{:S(2)}) collective-permute-start(f32[72,128]{1,0:T(8,128)S(1)} %add_add_fusion.3), channel_id=1, source_target_pairs={{0,3},{1,2},{2,1},{3,0},{4,7},{5,6},{6,5},{7,4},{8,11},{9,10},{10,... | collective-permute-start | bytes 110600 | tf_op jit(solution)/shard_map/ppermute | solution.py:320
  51.7 4.1 %collective-permute-start.28 = (f32[72,128]{1,0:T(8,128)S(1)}, f32[72,128]{1,0:T(8,128)S(1)}, u32[]{:S(2)}, u32[]{:S(2)}) collective-permute-start(f32[72,128]{1,0:T(8,128)S(1)} %add_add_fusion.3), channel_id=1, source_target_pairs={{0,1},{1,0},{2,3},{3,2},{4,5},{5,4},{6,7},{7,6},{8,9},{9,8},{10,11... | collective-permute-start | bytes 110600 | tf_op jit(solution)/shard_map/ppermute | solution.py:320

commit v7 on v6

--- a/solution.py
+++ b/solution.py
@@ -332,7 +332,10 @@
     v = v + core_swap(v)
     for axis, unit in (("row", 2), ("col", 4), ("col", 1)):
         others = {d: exchange(v, axis, lambda i, d=d * unit: i ^ d) for d in (1, 2, 3)}
-        v = (v + others[2]) + (others[3] + others[1])
+        if axis == "row":
+            v = (v + others[2]) + (others[1] + others[3])
+        else:
+            v = (v + others[2]) + (others[3] + others[1])
     return v
 
 

time: 61.3 us -> 63.2 us (1.031)
  waiting for transfers between devices: 16.4 us -> 20.6 us
  Pallas kernels: 21.1 us -> 18.1 us
  starting transfers between devices: 22.5 us -> 23.6 us
    ppermute x19, waiting for transfers between devices: 16.4 us -> 20.6 us  [exchange(): return lax.ppermute(v, axis, [(i, to(i)) for i in range(n)])]
    pallas_call x3, Pallas kernels: 4.94 us -> 2.36 us  [add_part(): call(functools.partial(part_kernel, part), name, w_vmem, [smem(), smem()]...]
    ppermute x19, starting transfers between devices: 22.5 us -> 23.6 us  [exchange(): return lax.ppermute(v, axis, [(i, to(i)) for i in range(n)])]
  transfers between devices with their start and end apart: 19 -> 19, of which waited for: 12 -> 14; matrix products, arithmetic and copies ran while one was open for 0% -> 0% of each run, Pallas kernels for 21% -> 15%
where the time goes in v7:
time: 63.2 us; the launch traced here: 63.3 us
  starting transfers between devices  23.6 us (37%)
  waiting for transfers between devices  20.6 us (33%)
  Pallas kernels  18.1 us (29%)
  between operations  0.87 us (1%)
    ppermute x19, starting transfers between devices, exchange(): return lax.ppermute(v, axis, [(i, to(i)) for i in range(n)])  23.6 us
    ppermute x19, waiting for transfers between devices, exchange(): return lax.ppermute(v, axis, [(i, to(i)) for i in range(n)])  20.6 us
    pallas_call x1, Pallas kernels, local(): call(prepare_kernel, 'prepare', (pltpu.VMEM((SLOTS, TILE, TILE), BF16), w...  7.42 us
    pallas_call x1, Pallas kernels, local(): call(functools.partial(factor_kernel, node_total), 'factor', (square, squ...  3.8 us
    pallas_call x3, Pallas kernels, add_part(): call(functools.partial(part_kernel, part), name, w_vmem, [smem(), smem()]...  2.36 us
    pallas_call x1, Pallas kernels, local(): call(last_kernel, 'last_part', (w_vmem, parts_vmem, jax.ShapeDtypeStruct(...  2.03 us
    pallas_call x1, Pallas kernels, plain(): call(final_kernel, 'scale_block', (pltpu.HBM((K, NODES_DEV), F32), pltpu....  1.27 us
  transfers between devices with their start and end apart: 19, of which 14 were waited for; matrix products, arithmetic and copies ran while one was open for 0% of the time, Pallas kernels for 15%

profile of v7, /device:TPU:0, one launch (start us, length us, event | category | flops | bytes accessed | tf_op | source)
XLA Modules:
  0.0 63.3 jit_solution(8356667989603942087)
XLA Ops:
  0.6 1.2 %round_block.1 = (bf16[32,64,128]{2,1,0:T(8,128)(2,1)S(1)}, f32[64,4096]{1,0:T(8,128)S(1)}) custom-call(f32[64,4096]{1,0:T(8,128)} %bitcast.21), custom_call_target="tpu_custom_call" | custom-call | flops 1000000000 | bytes 3000000 | tf_op jit(solution)/shard_map/round_block/pallas_call | solution.py:350
  1.9 2.1 %collective-permute-start.10 = (bf16[32,64,128]{2,1,0:T(8,128)(2,1)S(1)}, bf16[32,64,128]{2,1,0:T(8,128)(2,1)S(1)}, u32[]{:S(2)}, u32[]{:S(2)}) collective-permute-start(bf16[32,64,128]{2,1,0:T(8,128)(2,1)S(1)} %get-tuple-element.55.half_ref), channel_id=1, source_target_pairs={{0,32},{16,112},{32,64},{48,16},{64,96},{80,48},{96,0},{112,80},{1... | collective-permute-start | bytes 1572872 | tf_op jit(solution)/shard_map/ppermute | solution.py:320
  3.9 2.2 %collective-permute-start.12 = (bf16[32,64,128]{2,1,0:T(8,128)(2,1)S(1)}, bf16[32,64,128]{2,1,0:T(8,128)(2,1)S(1)}, u32[]{:S(2)}, u32[]{:S(2)}) collective-permute-start(bf16[32,64,128]{2,1,0:T(8,128)(2,1)S(1)} %get-tuple-element.55.half_ref), channel_id=1, source_target_pairs={{0,96},{16,48},{32,0},{48,80},{64,32},{80,112},{96,64},{112,16},{1... | collective-permute-start | bytes 1572872 | tf_op jit(solution)/shard_map/ppermute | solution.py:320
  6.1 7.4 %prepare.1 = (bf16[512,128,128]{2,1,0:T(8,128)(2,1)S(1)}, f32[32,128,64]{2,1,0:T(8,128)S(1)}, bf16[192,4096]{1,0:T(8,128)(2,1)S(1)}, f32[64,64]{1,0:T(8,128)S(1)}, s32[1,3072]{1,0:T(1,128)S(4)}, /*index=5*/s32[5]{0:T(128)S(4)}) custom-call(bf16[512,128,128]{2,1,0:T(8,128)(2,1)} %tiles_hbm.1, s32[1,512]{1,0:T(1,128)} %bitcast.24, s32[1,32]{1,0:T(1,128)} %bitcast.25, ...), custom_call_target="tpu_custom_call" | custom-call | flops 8999999488 | bytes 27000000 | tf_op jit(solution)/shard_map/prepare/pallas_call | solution.py:355
  13.6 3.4 %collective-permute-done.10.refs_0_ = bf16[32,64,128]{2,1,0:T(8,128)(2,1)S(1)} collective-permute-done((bf16[32,64,128]{2,1,0:T(8,128)(2,1)S(1)}, bf16[32,64,128]{2,1,0:T(8,128)(2,1)S(1)}, u32[]{:S(2)}, u32[]{:S(2)}) %collective-permute-start.10) | collective-permute-done | bytes 524320 | tf_op jit(solution)/shard_map/ppermute | solution.py:320
  18.4 2.6 %collective-permute-start.13 = (bf16[16,64,128]{2,1,0:T(8,128)(2,1)S(1)}, bf16[16,64,128]{2,1,0:T(8,128)(2,1)S(1)}, u32[]{:S(2)}, u32[]{:S(2)}) collective-permute-start(bf16[16,64,128]{2,1,0:T(8,128)(2,1)S(1)} %slice.42), channel_id=1, source_target_pairs={{0,96},{16,48},{32,0},{48,80},{64,32},{80,112},{96,64},{112,16},{1... | collective-permute-start | bytes 786440 | tf_op jit(solution)/shard_map/ppermute | solution.py:320
  23.9 2.3 %collective-permute-done.11.refs_0_ = bf16[16,64,128]{2,1,0:T(8,128)(2,1)S(1)} collective-permute-done((bf16[16,64,128]{2,1,0:T(8,128)(2,1)S(1)}, bf16[16,64,128]{2,1,0:T(8,128)(2,1)S(1)}, u32[]{:S(2)}, u32[]{:S(2)}) %collective-permute-start.11) | collective-permute-done | bytes 262176 | tf_op jit(solution)/shard_map/ppermute | solution.py:320
  26.2 1.6 %collective-permute-start.17 = (bf16[16,64,128]{2,1,0:T(8,128)(2,1)S(1)}, bf16[16,64,128]{2,1,0:T(8,128)(2,1)S(1)}, u32[]{:S(2)}, u32[]{:S(2)}) collective-permute-start(bf16[16,64,128]{2,1,0:T(8,128)(2,1)S(1)} %collective-permute-done.11.refs_0_), channel_id=1, source_target_pairs={{0,16},{16,0},{32,48},{48,32},{64,80},{80,64},{96,112},{112,96},{1... | collective-permute-start | bytes 786440 | tf_op jit(solution)/shard_map/ppermute | solution.py:320
  29.3 2.0 %last_part.1 = (f32[32,128,64]{2,1,0:T(8,128)S(1)}, bf16[192,4096]{1,0:T(8,128)(2,1)S(1)}, f32[72,128]{1,0:T(8,128)S(1)}) custom-call(s32[1,3072]{1,0:T(1,128)S(4)} %get-tuple-element.49.list_ref, s32[5]{0:T(128)S(4)} %get-tuple-element.50.count_ref, bf16[512,128,128]{2,1,0:T(8,128)(2,1)S(1)} %get-tuple-element.51.tiles_ref, ...), custom_call_target="tpu_custom_call", output_to_operand_aliasing={{0}: (5, {})} | custom-call | flops 4000000000 | bytes 12000000 | tf_op jit(solution)/shard_map/last_part/pallas_call | solution.py:387
  32.6 1.2 %collective-permute-start.20 = (f32[72,128]{1,0:T(8,128)S(1)}, f32[72,128]{1,0:T(8,128)S(1)}, u32[]{:S(2)}, u32[]{:S(2)}) collective-permute-start(f32[72,128]{1,0:T(8,128)S(1)} %add.84), channel_id=1, source_target_pairs={{0,64},{16,80},{32,96},{48,112},{64,0},{80,16},{96,32},{112,48},{1... | collective-permute-start | bytes 110600 | tf_op jit(solution)/shard_map/ppermute | solution.py:320
  33.8 1.9 %collective-permute-start.21 = (f32[72,128]{1,0:T(8,128)S(1)}, f32[72,128]{1,0:T(8,128)S(1)}, u32[]{:S(2)}, u32[]{:S(2)}) collective-permute-start(f32[72,128]{1,0:T(8,128)S(1)} %add.84), channel_id=1, source_target_pairs={{0,32},{16,48},{32,0},{48,16},{64,96},{80,112},{96,64},{112,80},{1... | collective-permute-start | bytes 110600 | tf_op jit(solution)/shard_map/ppermute | solution.py:320
  35.7 1.0 %collective-permute-start.22 = (f32[72,128]{1,0:T(8,128)S(1)}, f32[72,128]{1,0:T(8,128)S(1)}, u32[]{:S(2)}, u32[]{:S(2)}) collective-permute-start(f32[72,128]{1,0:T(8,128)S(1)} %add.84), channel_id=1, source_target_pairs={{0,96},{16,112},{32,64},{48,80},{64,32},{80,48},{96,0},{112,16},{1... | collective-permute-start | bytes 110600 | tf_op jit(solution)/shard_map/ppermute | solution.py:320
  36.7 1.5 %collective-permute-done.20 = f32[72,128]{1,0:T(8,128)S(1)} collective-permute-done((f32[72,128]{1,0:T(8,128)S(1)}, f32[72,128]{1,0:T(8,128)S(1)}, u32[]{:S(2)}, u32[]{:S(2)}) %collective-permute-start.20) | collective-permute-done | bytes 36896 | tf_op jit(solution)/shard_map/ppermute | solution.py:320
  38.3 2.6 %collective-permute-done.22 = f32[72,128]{1,0:T(8,128)S(1)} collective-permute-done((f32[72,128]{1,0:T(8,128)S(1)}, f32[72,128]{1,0:T(8,128)S(1)}, u32[]{:S(2)}, u32[]{:S(2)}) %collective-permute-start.22) | collective-permute-done | bytes 36896 | tf_op jit(solution)/shard_map/ppermute | solution.py:320
  40.9 2.9 %collective-permute-start.23 = (f32[72,128]{1,0:T(8,128)S(1)}, f32[72,128]{1,0:T(8,128)S(1)}, u32[]{:S(2)}, u32[]{:S(2)}) collective-permute-start(f32[72,128]{1,0:T(8,128)S(1)} %add_add_fusion.4), channel_id=1, source_target_pairs={{0,8},{1,9},{2,10},{3,11},{4,12},{5,13},{6,14},{7,15},{8,0},{9,1},... | collective-permute-start | bytes 110600 | tf_op jit(solution)/shard_map/ppermute | solution.py:320
  43.8 1.4 %collective-permute-start.24 = (f32[72,128]{1,0:T(8,128)S(1)}, f32[72,128]{1,0:T(8,128)S(1)}, u32[]{:S(2)}, u32[]{:S(2)}) collective-permute-start(f32[72,128]{1,0:T(8,128)S(1)} %add_add_fusion.4), channel_id=1, source_target_pairs={{0,12},{1,13},{2,14},{3,15},{4,8},{5,9},{6,10},{7,11},{8,4},{9,5},... | collective-permute-start | bytes 110600 | tf_op jit(solution)/shard_map/ppermute | solution.py:320
  45.2 1.4 %collective-permute-done.23 = f32[72,128]{1,0:T(8,128)S(1)} collective-permute-done((f32[72,128]{1,0:T(8,128)S(1)}, f32[72,128]{1,0:T(8,128)S(1)}, u32[]{:S(2)}, u32[]{:S(2)}) %collective-permute-start.23) | collective-permute-done | bytes 36896 | tf_op jit(solution)/shard_map/ppermute | solution.py:320
  46.6 2.4 %collective-permute-done.24 = f32[72,128]{1,0:T(8,128)S(1)} collective-permute-done((f32[72,128]{1,0:T(8,128)S(1)}, f32[72,128]{1,0:T(8,128)S(1)}, u32[]{:S(2)}, u32[]{:S(2)}) %collective-permute-start.24) | collective-permute-done | bytes 36896 | tf_op jit(solution)/shard_map/ppermute | solution.py:320
  49.1 3.6 %collective-permute-start.26 = (f32[72,128]{1,0:T(8,128)S(1)}, f32[72,128]{1,0:T(8,128)S(1)}, u32[]{:S(2)}, u32[]{:S(2)}) collective-permute-start(f32[72,128]{1,0:T(8,128)S(1)} %add_add_fusion.3), channel_id=1, source_target_pairs={{0,2},{1,3},{2,0},{3,1},{4,6},{5,7},{6,4},{7,5},{8,10},{9,11},{10,... | collective-permute-start | bytes 110600 | tf_op jit(solution)/shard_map/ppermute | solution.py:320
  52.7 1.4 %collective-permute-start.27 = (f32[72,128]{1,0:T(8,128)S(1)}, f32[72,128]{1,0:T(8,128)S(1)}, u32[]{:S(2)}, u32[]{:S(2)}) collective-permute-start(f32[72,128]{1,0:T(8,128)S(1)} %add_add_fusion.3), channel_id=1, source_target_pairs={{0,3},{1,2},{2,1},{3,0},{4,7},{5,6},{6,5},{7,4},{8,11},{9,10},{10,... | collective-permute-start | bytes 110600 | tf_op jit(solution)/shard_map/ppermute | solution.py:320
  54.7 3.2 %collective-permute-done.27 = f32[72,128]{1,0:T(8,128)S(1)} collective-permute-done((f32[72,128]{1,0:T(8,128)S(1)}, f32[72,128]{1,0:T(8,128)S(1)}, u32[]{:S(2)}, u32[]{:S(2)}) %collective-permute-start.27) | collective-permute-done | bytes 36896 | tf_op jit(solution)/shard_map/ppermute | solution.py:320
  58.1 3.8 %factor.1 = (f32[64,64]{1,0:T(8,128)}, f32[64,64]{1,0:T(8,128)S(1)}, f32[64,128]{1,0:T(8,128)S(1)}, s32[1]{0:T(128)S(4)}) custom-call(f32[72,128]{1,0:T(8,128)S(1)} %add_add_fusion.2.sums_ref), custom_call_target="tpu_custom_call" | custom-call | flops 5000000000 | bytes 15000000 | tf_op jit(solution)/shard_map/factor/pallas_call | solution.py:393
  61.9 1.3 %conditional.1 = ((f32[64,4096]{1,0:T(8,128)}, f32[64,64]{1,0:T(8,128)})) conditional(s32[]{:T(128)} %bitcast.9, (bf16[192,4096]{1,0:T(8,128)(2,1)S(1)}, f32[72,128]{1,0:T(8,128)S(1)}, bf16[192,4096]{1,0:T(8,128)(2,1)S(1)}) %tuple.21, (f32[64,128]{1,0:T(8,128)S(1)}, bf16[192,4096]{1,0:T(8,128)(2,1)S(1)}, bf16[192,4096]{1,0:T(8,128)(2,1)S(1)}, ...), branch_computations={%region_0.0_spmd, %region_3.4_spmd} | conditional | flops 2000000000 | bytes 12805062 | solution.py:412
  61.9 1.3 %scale_block.1 = (f32[64,4096]{1,0:T(8,128)}, f32[64,64]{1,0:T(8,128)}) custom-call(f32[64,128]{1,0:T(8,128)S(1)} %get-tuple-element.17.f_ref, bf16[192,4096]{1,0:T(8,128)(2,1)S(1)} %get-tuple-element.18.zw_ref, bf16[192,4096]{1,0:T(8,128)(2,1)S(1)} %get-tuple-element.19.zx_ref, f32[64,64]{1,0:T(8,128)S(1)} %get-tuple-element.20.r_ref), custom_call_target="tpu_custom_call" | custom-call | flops 2000000000 | bytes 6000000 | tf_op jit(solution)/shard_map/cond/branch_1_fun/scale_block/pallas_call | solution.py:399
  (29 shorter events, 8.1 us)
Async XLA Ops:
  1.9 15.1 %collective-permute-start.10 = (bf16[32,64,128]{2,1,0:T(8,128)(2,1)S(1)}, bf16[32,64,128]{2,1,0:T(8,128)(2,1)S(1)}, u32[]{:S(2)}, u32[]{:S(2)}) collective-permute-start(bf16[32,64,128]{2,1,0:T(8,128)(2,1)S(1)} %get-tuple-element.55.half_ref), channel_id=1, source_target_pairs={{0,32},{16,112},{32,64},{48,16},{64,96},{80,48},{96,0},{112,80},{1... | collective-permute-start | bytes 1572872 | tf_op jit(solution)/shard_map/ppermute | solution.py:320
  3.9 14.4 %collective-permute-start.12 = (bf16[32,64,128]{2,1,0:T(8,128)(2,1)S(1)}, bf16[32,64,128]{2,1,0:T(8,128)(2,1)S(1)}, u32[]{:S(2)}, u32[]{:S(2)}) collective-permute-start(bf16[32,64,128]{2,1,0:T(8,128)(2,1)S(1)} %get-tuple-element.55.half_ref), channel_id=1, source_target_pairs={{0,96},{16,48},{32,0},{48,80},{64,32},{80,112},{96,64},{112,16},{1... | collective-permute-start | bytes 1572872 | tf_op jit(solution)/shard_map/ppermute | solution.py:320
  17.0 4.1 %collective-permute-start.16 = (bf16[32,64,128]{2,1,0:T(8,128)(2,1)S(1)}, bf16[32,64,128]{2,1,0:T(8,128)(2,1)S(1)}, u32[]{:S(2)}, u32[]{:S(2)}) collective-permute-start(bf16[32,64,128]{2,1,0:T(8,128)(2,1)S(1)} %get-tuple-element.55.half_ref), channel_id=1, source_target_pairs={{0,16},{16,0},{32,48},{48,32},{64,80},{80,64},{96,112},{112,96},{1... | collective-permute-start | bytes 1572872 | tf_op jit(solution)/shard_map/ppermute | solution.py:320
  17.0 5.0 %collective-permute-start.14 = (bf16[32,64,128]{2,1,0:T(8,128)(2,1)S(1)}, bf16[32,64,128]{2,1,0:T(8,128)(2,1)S(1)}, u32[]{:S(2)}, u32[]{:S(2)}) collective-permute-start(bf16[32,64,128]{2,1,0:T(8,128)(2,1)S(1)} %collective-permute-done.10.refs_0_), channel_id=1, source_target_pairs={{0,16},{16,0},{32,48},{48,32},{64,80},{80,64},{96,112},{112,96},{1... | collective-permute-start | bytes 1572872 | tf_op jit(solution)/shard_map/ppermute | solution.py:320
  17.5 8.7 %collective-permute-start.11 = (bf16[16,64,128]{2,1,0:T(8,128)(2,1)S(1)}, bf16[16,64,128]{2,1,0:T(8,128)(2,1)S(1)}, u32[]{:S(2)}, u32[]{:S(2)}) collective-permute-start(bf16[16,64,128]{2,1,0:T(8,128)(2,1)S(1)} %slice.39), channel_id=1, source_target_pairs={{0,32},{16,112},{32,64},{48,16},{64,96},{80,48},{96,0},{112,80},{1... | collective-permute-start | bytes 786440 | tf_op jit(solution)/shard_map/ppermute | solution.py:320
  18.4 7.8 %collective-permute-start.13 = (bf16[16,64,128]{2,1,0:T(8,128)(2,1)S(1)}, bf16[16,64,128]{2,1,0:T(8,128)(2,1)S(1)}, u32[]{:S(2)}, u32[]{:S(2)}) collective-permute-start(bf16[16,64,128]{2,1,0:T(8,128)(2,1)S(1)} %slice.42), channel_id=1, source_target_pairs={{0,96},{16,48},{32,0},{48,80},{64,32},{80,112},{96,64},{112,16},{1... | collective-permute-start | bytes 786440 | tf_op jit(solution)/shard_map/ppermute | solution.py:320
  21.0 1.9 %collective-permute-start.15 = (bf16[32,64,128]{2,1,0:T(8,128)(2,1)S(1)}, bf16[32,64,128]{2,1,0:T(8,128)(2,1)S(1)}, u32[]{:S(2)}, u32[]{:S(2)}) collective-permute-start(bf16[32,64,128]{2,1,0:T(8,128)(2,1)S(1)} %collective-permute-done.12.refs_1_), channel_id=1, source_target_pairs={{0,16},{16,0},{32,48},{48,32},{64,80},{80,64},{96,112},{112,96},{1... | collective-permute-start | bytes 1572872 | tf_op jit(solution)/shard_map/ppermute | solution.py:320
  26.2 2.8 %collective-permute-start.17 = (bf16[16,64,128]{2,1,0:T(8,128)(2,1)S(1)}, bf16[16,64,128]{2,1,0:T(8,128)(2,1)S(1)}, u32[]{:S(2)}, u32[]{:S(2)}) collective-permute-start(bf16[16,64,128]{2,1,0:T(8,128)(2,1)S(1)} %collective-permute-done.11.refs_0_), channel_id=1, source_target_pairs={{0,16},{16,0},{32,48},{48,32},{64,80},{80,64},{96,112},{112,96},{1... | collective-permute-start | bytes 786440 | tf_op jit(solution)/shard_map/ppermute | solution.py:320
  27.8 1.5 %collective-permute-start.18 = (bf16[16,64,128]{2,1,0:T(8,128)(2,1)S(1)}, bf16[16,64,128]{2,1,0:T(8,128)(2,1)S(1)}, u32[]{:S(2)}, u32[]{:S(2)}) collective-permute-start(bf16[16,64,128]{2,1,0:T(8,128)(2,1)S(1)} %collective-permute-done.13.refs_1_), channel_id=1, source_target_pairs={{0,16},{16,0},{32,48},{48,32},{64,80},{80,64},{96,112},{112,96},{1... | collective-permute-start | bytes 786440 | tf_op jit(solution)/shard_map/ppermute | solution.py:320
  31.3 1.3 %collective-permute-start.19 = (f32[72,128]{1,0:T(8,128)S(1)}, f32[72,128]{1,0:T(8,128)S(1)}, u32[]{:S(2)}, u32[]{:S(2)}) collective-permute-start(f32[72,128]{1,0:T(8,128)S(1)} %get-tuple-element.62), channel_id=1, source_target_pairs={{0,16},{16,0},{32,48},{48,32},{64,80},{80,64},{96,112},{112,96},{1... | collective-permute-start | bytes 110600 | tf_op jit(solution)/shard_map/ppermute | solution.py:320
  32.6 5.6 %collective-permute-start.20 = (f32[72,128]{1,0:T(8,128)S(1)}, f32[72,128]{1,0:T(8,128)S(1)}, u32[]{:S(2)}, u32[]{:S(2)}) collective-permute-start(f32[72,128]{1,0:T(8,128)S(1)} %add.84), channel_id=1, source_target_pairs={{0,64},{16,80},{32,96},{48,112},{64,0},{80,16},{96,32},{112,48},{1... | collective-permute-start | bytes 110600 | tf_op jit(solution)/shard_map/ppermute | solution.py:320
  33.8 4.5 %collective-permute-start.21 = (f32[72,128]{1,0:T(8,128)S(1)}, f32[72,128]{1,0:T(8,128)S(1)}, u32[]{:S(2)}, u32[]{:S(2)}) collective-permute-start(f32[72,128]{1,0:T(8,128)S(1)} %add.84), channel_id=1, source_target_pairs={{0,32},{16,48},{32,0},{48,16},{64,96},{80,112},{96,64},{112,80},{1... | collective-permute-start | bytes 110600 | tf_op jit(solution)/shard_map/ppermute | solution.py:320
  35.7 5.2 %collective-permute-start.22 = (f32[72,128]{1,0:T(8,128)S(1)}, f32[72,128]{1,0:T(8,128)S(1)}, u32[]{:S(2)}, u32[]{:S(2)}) collective-permute-start(f32[72,128]{1,0:T(8,128)S(1)} %add.84), channel_id=1, source_target_pairs={{0,96},{16,112},{32,64},{48,80},{64,32},{80,48},{96,0},{112,16},{1... | collective-permute-start | bytes 110600 | tf_op jit(solution)/shard_map/ppermute | solution.py:320
  40.9 5.6 %collective-permute-start.23 = (f32[72,128]{1,0:T(8,128)S(1)}, f32[72,128]{1,0:T(8,128)S(1)}, u32[]{:S(2)}, u32[]{:S(2)}) collective-permute-start(f32[72,128]{1,0:T(8,128)S(1)} %add_add_fusion.4), channel_id=1, source_target_pairs={{0,8},{1,9},{2,10},{3,11},{4,12},{5,13},{6,14},{7,15},{8,0},{9,1},... | collective-permute-start | bytes 110600 | tf_op jit(solution)/shard_map/ppermute | solution.py:320
  43.8 5.2 %collective-permute-start.24 = (f32[72,128]{1,0:T(8,128)S(1)}, f32[72,128]{1,0:T(8,128)S(1)}, u32[]{:S(2)}, u32[]{:S(2)}) collective-permute-start(f32[72,128]{1,0:T(8,128)S(1)} %add_add_fusion.4), channel_id=1, source_target_pairs={{0,12},{1,13},{2,14},{3,15},{4,8},{5,9},{6,10},{7,11},{8,4},{9,5},... | collective-permute-start | bytes 110600 | tf_op jit(solution)/shard_map/ppermute | solution.py:320
  45.2 4.0 %collective-permute-start.25 = (f32[72,128]{1,0:T(8,128)S(1)}, f32[72,128]{1,0:T(8,128)S(1)}, u32[]{:S(2)}, u32[]{:S(2)}) collective-permute-start(f32[72,128]{1,0:T(8,128)S(1)} %add_add_fusion.4), channel_id=1, source_target_pairs={{0,4},{1,5},{2,6},{3,7},{4,0},{5,1},{6,2},{7,3},{8,12},{9,13},{10,... | collective-permute-start | bytes 110600 | tf_op jit(solution)/shard_map/ppermute | solution.py:320
  49.1 5.5 %collective-permute-start.26 = (f32[72,128]{1,0:T(8,128)S(1)}, f32[72,128]{1,0:T(8,128)S(1)}, u32[]{:S(2)}, u32[]{:S(2)}) collective-permute-start(f32[72,128]{1,0:T(8,128)S(1)} %add_add_fusion.3), channel_id=1, source_target_pairs={{0,2},{1,3},{2,0},{3,1},{4,6},{5,7},{6,4},{7,5},{8,10},{9,11},{10,... | collective-permute-start | bytes 110600 | tf_op jit(solution)/shard_map/ppermute | solution.py:320
  52.7 5.2 %collective-permute-start.27 = (f32[72,128]{1,0:T(8,128)S(1)}, f32[72,128]{1,0:T(8,128)S(1)}, u32[]{:S(2)}, u32[]{:S(2)}) collective-permute-start(f32[72,128]{1,0:T(8,128)S(1)} %add_add_fusion.3), channel_id=1, source_target_pairs={{0,3},{1,2},{2,1},{3,0},{4,7},{5,6},{6,5},{7,4},{8,11},{9,10},{10,... | collective-permute-start | bytes 110600 | tf_op jit(solution)/shard_map/ppermute | solution.py:320
  54.1 4.0 %collective-permute-start.28 = (f32[72,128]{1,0:T(8,128)S(1)}, f32[72,128]{1,0:T(8,128)S(1)}, u32[]{:S(2)}, u32[]{:S(2)}) collective-permute-start(f32[72,128]{1,0:T(8,128)S(1)} %add_add_fusion.3), channel_id=1, source_target_pairs={{0,1},{1,0},{2,3},{3,2},{4,5},{5,4},{6,7},{7,6},{8,9},{9,8},{10,11... | collective-permute-start | bytes 110600 | tf_op jit(solution)/shard_map/ppermute | solution.py:320
